TPU v7x, 32 devices: a whole 2x2x4 slice. The times are simulated.
32 devices in a mesh: floor: 4 (over x, core), facade: 8 (over z, y).
Axes of the slice: x: 2, y: 2, z: 4, core: 2. Of those that a mesh axis runs over, the one named last changes fastest.
Arguments:
- interface_rhs: float32 [4, 8, 2, 256, 128], P('floor', 'facade'), may hold values from -40 to 40
- inverse_factor: float32 [4, 8, 1024, 1024], P('floor', 'facade')
- near_coupling: bfloat16 [4, 8, 1024, 1024], P('floor', 'facade'), may hold values from -0.09375 to 0.09375
- near_pattern: int32 [4, 8, 8, 8], P('floor', 'facade'), may hold values from 0 to 1, as said below
Outputs:
- multipliers: float32 [4, 8, 2, 256, 128], P('floor', 'facade')
- residual: float32 [4, 8, 2, 256, 128], P('floor', 'facade')
Inputs may be any that keep to these rules, and one draw needn't show every extreme that they name: `near_pattern`: every diagonal block is set; each subdomain has from 8 to 32 blocks set, and in every draw some subdomain has exactly 32.
All inputs are finite; a program needn't handle non-finite values.
Results may differ from a plain program's by a relative error of at most 0.0022.
Values sent between devices are 32-bit elements; how exact they have to be, the bound alone decides.
No kernel may reach another device: no remote copies, remote signals or barrier semaphores. Data moves between devices by JAX's collectives and lax.ppermute only.
A program may use at most 64 MiB of HBM per device.

v0:
```python
import functools

import jax
import jax.numpy as jnp
from jax import lax
from jax.experimental import pallas as pl
from jax.experimental.pallas import tpu as pltpu
from jax.sharding import PartitionSpec as P

ITERS = 4
SLOT, KEEP, ODD = 0, 4, 7
PADS = (8, 0, 24, 16)
PAIRS = [(i, j) for i in range(4) for j in range(i, 4)]
CENTER, NODE = 20, 24
AXES = ("floor", "facade")
F32 = jnp.float32
BF16 = jnp.bfloat16


def halves(x):
    high = x.astype(BF16)
    return high, (x - high.astype(F32)).astype(BF16)


def params(mib):
    return pltpu.CompilerParams(vmem_limit_bytes=mib << 20)


def operator_kernel(info, pattern_hbm, w_hbm, n_hbm, g_ref, center_ref, pattern, w_buf, n_buf, sems, left, right, total):
    size = w_buf.shape[1]
    face = size // 4
    nb = pattern.shape[0]
    blk = size // nb
    pattern_copy = pltpu.make_async_copy(pattern_hbm, pattern, sems.at[2, 0])
    pattern_copy.start()

    def fetch(k):
        rows = pl.ds(k * face, face)
        return (
            pltpu.make_async_copy(w_hbm.at[rows, :], w_buf.at[rows, :], sems.at[0, k]),
            pltpu.make_async_copy(n_hbm.at[rows, :], n_buf.at[rows, :], sems.at[1, k]),
        )

    def prepare(k):
        for copy in fetch(k):
            copy.wait()
        high, low = halves(w_buf[k * face : (k + 1) * face, :])
        here, there = left.at[k % 2], right.at[k % 2]
        there[0:face, :] = high
        there[face : 2 * face, :] = low
        there[2 * face : 3 * face, :] = high
        for a in range(face // blk):
            for b in range(nb):
                keep = pattern[k * (face // blk) + a, b] != 0
                cols = slice(b * blk, (b + 1) * blk)
                block = n_buf[k * face + a * blk : k * face + (a + 1) * blk, cols]
                there[3 * face + a * blk : 3 * face + (a + 1) * blk, cols] = jnp.where(
                    keep, block, jnp.zeros_like(block)
                )
        high_t = high.T
        here[:, 0:face] = high_t
        here[:, face : 2 * face] = high_t
        here[:, 2 * face : 3 * face] = low.T
        here[:, 3 * face :] = there[3 * face :, :].T

    def multiply(k):
        for i in range(4):
            rows, cols = slice(i * face, (i + 1) * face), slice(i * face, size)
            part = jnp.dot(left[k % 2, rows, :], right[k % 2, :, cols], preferred_element_type=F32)
            if k == 0:
                total[rows, cols] = part
            else:
                total[rows, cols] += part

    for k in range(4):
        for copy in fetch(k):
            copy.start()
    pattern_copy.wait()
    prepare(0)
    for k in range(4):
        if k < 3:
            prepare(k + 1)
        multiply(k)

    def put(i, j, block):
        def at(k):
            return pl.multiple_of(info[k] * face, face)

        rows = pl.ds(at(i), face)
        high, low = halves(block)
        g_ref[rows, pl.ds(at(j), face)] = high
        g_ref[rows, pl.ds(pl.multiple_of(size + at(j), face), face)] = low

    diagonal = lax.broadcasted_iota(jnp.int32, (face, face), 0) == lax.broadcasted_iota(jnp.int32, (face, face), 1)
    trace = jnp.zeros((1, face), F32)
    for i in range(4):
        for j in range(i, 4):
            block = total[i * face : (i + 1) * face, j * face : (j + 1) * face]
            put(i, j, block)
            if j == i:
                trace = trace + rows_sum(jnp.where(diagonal, block, 0.0))
            if j > i:
                put(j, i, block.T)


    center_ref[...] = jnp.broadcast_to(jnp.sum(trace, axis=1, keepdims=True) * (2.0 / size), center_ref.shape)


def build_operator(info, factor, coupling, pattern, cases):
    size = factor.shape[0]
    return pl.pallas_call(
        operator_kernel,
        in_specs=[pl.BlockSpec(memory_space=pltpu.SMEM)] + [pl.BlockSpec(memory_space=pl.ANY)] * 3,
        out_specs=[pl.BlockSpec(memory_space=pltpu.VMEM)] * 2,
        out_shape=[jax.ShapeDtypeStruct((size, 2 * size), BF16), jax.ShapeDtypeStruct((8, cases), F32)],
        scratch_shapes=[
            pltpu.SMEM(pattern.shape, jnp.int32),
            pltpu.VMEM((size, size), F32),
            pltpu.VMEM((size, size), BF16),
            pltpu.SemaphoreType.DMA((3, 4)),
            pltpu.VMEM((2, size, size), BF16),
            pltpu.VMEM((2, size, size), BF16),
            pltpu.VMEM((size, size), F32),
        ],
        compiler_params=params(32),
        name="operator",
    )(
        info,
        pltpu.with_memory_space_constraint(pattern, pltpu.HBM),
        pltpu.with_memory_space_constraint(factor, pltpu.HBM),
        pltpu.with_memory_space_constraint(coupling, pltpu.HBM),
    )


def operand(u):
    high, low = halves(u)
    straight = jnp.concatenate([high, low], axis=1)
    crossed = jnp.concatenate([low, high], axis=1)
    return jnp.concatenate([straight, crossed], axis=0)


def product(g_ref, u):
    cases = u.shape[1]
    wide = jnp.dot(g_ref[...], operand(u), preferred_element_type=F32)
    return wide[:, :cases] + wide[:, cases:]


def fine_product(g_ref, u):
    size, cases = u.shape
    high, low = halves(u)
    rest = (u - high.astype(F32) - low.astype(F32)).astype(BF16)
    wide = jnp.dot(g_ref[:, :size], jnp.concatenate([high, low], axis=1), preferred_element_type=F32)
    crossed = jnp.concatenate([jnp.concatenate([rest, jnp.zeros_like(rest)], axis=1), jnp.concatenate([high, low], axis=1)], axis=0)
    fine = jnp.dot(g_ref[...], crossed, preferred_element_type=F32)
    return wide[:, :cases] + (wide[:, cases:] + (fine[:, :cases] + fine[:, cases:]))


def rows_sum(x):
    return jnp.sum(x, axis=0, keepdims=True)


def take_in(info, u_ref, own, got):
    face = u_ref.shape[0] // 4
    for k in range(4):
        value = own[k][0:face, :] - got[k][0:face, :]
        if k < 2:
            value = jnp.where(info[KEEP + k] != 0, value, 0.0)
        u_ref[k * face : (k + 1) * face, :] = value


def hand_out(y, outs):
    face = y.shape[0] // 4
    for k, out in enumerate(outs):
        out[0:face, :] = y[k * face : (k + 1) * face]
        if out.shape[0] > face:
            out[face:, :] = jnp.zeros((out.shape[0] - face, out.shape[1]), F32)


def first_kernel(info, below, beside, up, right, g_ref, u_ref, a, b, c, d):
    face = up.shape[0]
    own_up = jnp.where(info[KEEP + 2] != 0, up[...], 0.0)
    own_right = right[...]
    odd_floor, odd_facade = info[ODD] != 0, info[ODD + 1] != 0
    u_ref[0:face, :] = jnp.where(odd_floor, -below[...], own_up)
    u_ref[face : 2 * face, :] = jnp.where(odd_floor, own_up, -below[...])
    u_ref[2 * face : 3 * face, :] = jnp.where(odd_facade, -beside[...], own_right)
    u_ref[3 * face :, :] = jnp.where(odd_facade, own_right, -beside[...])
    hand_out(product(g_ref, u_ref[...]), (a, b, c, d))


def next_kernel(fine, info, ya, yb, yc, yd, ra, rb, rc, rd, g_ref, u_ref, a, b, c, d):
    take_in(info, u_ref, (ya, yb, yc, yd), (ra, rb, rc, rd))
    hand_out((fine_product if fine else product)(g_ref, u_ref[...]), (a, b, c, d))


def differences(w, scale):
    values = []
    power = None
    for k, value in enumerate(w):
        values.append(value if k == 0 else value * power)
        power = scale if k == 0 else power * scale
    out = [values[0]]
    while len(values) > 1:
        values = [values[k + 1] - values[k] for k in range(len(values) - 1)]
        out.append(values[0])
    return out


def last_kernel(info, ya, yb, yc, yd, ra, rb, rc, rd, u0, u1, u2, *rest):
    ys, (center, g_ref, u_ref, down, left, yo_ref, node, y_ref) = rest[:8], rest[8:]
    ys = [ys[:4], ys[4:], (ya, yb, yc, yd)]
    take_in(info, u_ref, (ya, yb, yc, yd), (ra, rb, rc, rd))
    face = down.shape[0]
    y_ref[...] = fine_product(g_ref, u_ref[...])

    def rows(j):
        return pl.ds(pl.multiple_of(info[SLOT + j] * face, face), face)

    down[...] = y_ref[rows(0), :]
    left[...] = y_ref[rows(2), :]
    yo_ref[0:face, :] = y_ref[rows(1), :]
    yo_ref[face:, :] = y_ref[rows(3), :]

    middle = center[0:1, :]
    scale = 1.0 / middle
    sums = [jnp.zeros((8, down.shape[1]), F32)] * (2 * len(PAIRS))
    step = 16
    for k in range(4):
        for at in range(0, face, step):
            here, there = slice(at, at + step), slice(k * face + at, k * face + at + step)
            v = differences([u[there, :] for u in (u0, u1, u2, u_ref)], scale)
            f = differences([y[k][here, :] for y in ys] + [y_ref[there, :]], scale)
            for q, (i, j) in enumerate(PAIRS):
                for part, term in ((0, v[i] * v[j]), (1, v[j] * f[i])):
                    for m in range(0, step, 8):
                        sums[2 * q + part] = sums[2 * q + part] + term[m : m + 8]
    for q in range(len(PAIRS)):
        node[2 * q : 2 * q + 1, :] = 0.5 * rows_sum(sums[2 * q])
        node[2 * q + 1 : 2 * q + 2, :] = scale * rows_sum(sums[2 * q + 1])
    node[CENTER:NODE, :] = jnp.broadcast_to(middle, (NODE - CENTER, middle.shape[1]))


def tree(values):
    while len(values) > 1:
        values = [values[k] + values[k + 1] for k in range(0, len(values), 2)]
    return values[0]


BINOMIAL = ((1,), (1, 1), (1, 2, 1), (1, 3, 3, 1), (1, 4, 6, 4, 1))


def merged(parts):
    centers = [part[CENTER : CENTER + 1, :] for part in parts]
    middle = tree(centers) * (1.0 / len(parts))
    moved = []
    for part, center in zip(parts, centers):
        ratio = center / middle
        shift = (center - middle) / middle
        ratios, shifts = [None, ratio, ratio * ratio, ratio * ratio * ratio], [None, shift, shift * shift, shift * shift * shift]

        def entry(k, j):
            value = None
            for power in (ratios[j], shifts[k - j]):
                if power is not None:
                    value = power if value is None else value * power
            return value if BINOMIAL[k][j] == 1 or value is None else BINOMIAL[k][j] * value

        change = [[entry(k, j) for j in range(k + 1)] for k in range(4)]

        def times(factor, value):
            return value if factor is None else factor * value

        row = {}
        for q, (i, j) in enumerate(PAIRS):
            row[i, j] = row[j, i] = part[2 * q : 2 * q + 2, :]
        half = [[tree_any([times(change[k][j], row[j, m]) for j in range(k + 1)]) for m in range(4)] for k in range(4)]
        unit = jnp.concatenate([jnp.ones_like(ratio), ratio], axis=0)
        moved.append(
            [unit * tree_any([times(change[j][m], half[i][m]) for m in range(j + 1)]) for i, j in PAIRS]
        )
    return [tree([values[q] for values in moved]) for q in range(len(PAIRS))], middle


def tree_any(values):
    return functools.reduce(lambda a, b: a + b, values)


def write_node(node, rows, middle):
    for q in range(len(PAIRS)):
        node[2 * q : 2 * q + 2, :] = rows[q]
    node[CENTER:NODE, :] = jnp.broadcast_to(middle, (NODE - CENTER, middle.shape[1]))


def merge_kernel(*refs):
    parts, node = refs[:-1], refs[-1]
    write_node(node, *merged(parts))


def conjugate_coefficients(rows):
    inner, energy = {}, {}
    for q, pair in enumerate(PAIRS):
        inner[pair], energy[pair] = rows[q][0:1, :], rows[q][1:2, :]

    def square(a, matrix):
        terms = []
        for i in range(len(a)):
            mixed = [2.0 * (a[j] * matrix[i, j]) for j in range(i + 1, len(a))]
            terms.append(a[i] * tree_any([a[i] * matrix[i, i]] + mixed))
        return tree_any(terms)

    def plus(a, s, b):
        return [a[k] + s * b[k] if k < len(a) else s * b[k] for k in range(len(b))]

    one = jnp.ones_like(rows[0][0:1, :])
    x, r, p = [], [one], [one]
    norm = inner[0, 0]
    for sweep in range(ITERS):
        step = norm / square(p, energy)
        x = plus(x, step, p)
        image = [p[0]] + [p[k] + p[k - 1] for k in range(1, len(p))] + [p[-1]]
        r = plus(r, -step, image)
        if sweep + 1 < ITERS:
            fresh = square(r, inner)
            p = plus(r, fresh / norm, p + [jnp.zeros_like(one)])
            norm = fresh
    return x, r


def powers(coefficients, scale):
    out = []
    power = None
    for j in range(len(coefficients)):
        value = tree_any(
            [coefficients[k] * float(BINOMIAL[k][j] * (-1) ** (k - j)) for k in range(j, len(coefficients))]
        )
        out.append(value if power is None else value * power)
        power = scale if power is None else power * scale
    return out


def image_kernel(info, yo_ref, got_up, got_right, *rest):
    parts, (w4_ref, node) = rest[:-2], rest[-2:]
    face = got_up.shape[0]
    for f, got in enumerate((got_up, got_right)):
        rows = slice(f * face, (f + 1) * face)
        image = yo_ref[rows, :] - got[...]
        if f == 0:
            image = jnp.where(info[KEEP + 2] != 0, image, 0.0)
        w4_ref[rows, :] = image
    write_node(node, *merged(parts))


def final_kernel(info, u0, u1, u2, u3, w4_ref, *rest):
    parts, (mult, resid) = rest[:-2], rest[-2:]
    rows, middle = merged(parts)
    scale = 1.0 / middle
    x, r = conjugate_coefficients(rows)
    x = [value * scale for value in powers(x, scale)]
    r = powers(r, scale)
    face = w4_ref.shape[0] // 2
    for f in range(2):
        place = pl.ds(pl.multiple_of(info[SLOT + 2 * f + 1] * face, face), face)
        here = slice(f * face, (f + 1) * face)
        w = [u[place, :] for u in (u0, u1, u2, u3)]
        mult[here, :] = x[0] * w[0] + x[1] * w[1] + x[2] * w[2] + x[3] * w[3]
        resid[here, :] = r[0] * w[0] + r[1] * w[1] + r[2] * w[2] + r[3] * w[3] + r[4] * w4_ref[here, :]


def upward(value, axis, steps, wrap):
    count = lax.axis_size(axis)
    pairs = [(i, (i + steps) % count) for i in range(count) if wrap or 0 <= i + steps < count]
    return lax.ppermute(value, axis, pairs)


def swapped(value, axis, odd, wrap):
    count = lax.axis_size(axis)
    pairs = []
    for i in range(odd, count, 2):
        if i + 1 < count or wrap:
            j = (i + 1) % count
            pairs += [(i, j), (j, i)]
    return lax.ppermute(value, axis, pairs)


def exchanged(a, b, c, d):
    d = swapped(d, "facade", 1, True)
    c = swapped(c, "facade", 0, True)
    b = swapped(b, "floor", 1, True)
    a = swapped(a, "floor", 0, False)
    return a, b, c, d


def flipped(value, flip_floor, flip_facade):
    floors, columns = lax.axis_size("floor"), lax.axis_size("facade")
    pairs = [
        (f * columns + c, (f ^ flip_floor) * columns + (c ^ flip_facade)) for f in range(floors) for c in range(columns)
    ]
    return lax.ppermute(value, AXES, pairs)


def sum_stages():
    floors, columns = lax.axis_size("floor"), lax.axis_size("facade")
    flips = []
    bit = 1
    while bit < floors:
        flips.append((bit, 0))
        bit *= 2
    bit = 1
    while bit < columns:
        flips.append((0, bit))
        bit *= 2
    return [flips[:1]] + [flips[k : k + 2] for k in range(1, len(flips), 2)]


def stage_parts(value, stage):
    if len(stage) == 1:
        return [value, flipped(value, *stage[0])]
    (f1, c1), (f2, c2) = stage
    return [value, flipped(value, f1, c1), flipped(value, f2, c2), flipped(value, f1 ^ f2, c1 ^ c2)]


def call(kernel, outs, scratch, smem, *args):
    return pl.pallas_call(
        kernel,
        in_specs=[pl.BlockSpec(memory_space=pltpu.SMEM)] * smem
        + [pl.BlockSpec(memory_space=pltpu.VMEM)] * (len(args) - smem),
        out_specs=[pl.BlockSpec(memory_space=pltpu.VMEM)] * len(outs),
        out_shape=outs,
        scratch_shapes=scratch,
        compiler_params=params(16),
    )(*args)


def local(interface_rhs, inverse_factor, near_coupling, near_pattern):
    face, cases = interface_rhs.shape[3:]
    size = 4 * face
    floors = lax.axis_size("floor")
    floor_pos, facade_pos = lax.axis_index("floor"), lax.axis_index("facade")
    odd_floor, odd_facade = floor_pos % 2, facade_pos % 2
    has_below = (floor_pos > 0).astype(jnp.int32)
    has_above = (floor_pos < floors - 1).astype(jnp.int32)
    keep_a = jnp.where(odd_floor == 0, has_above, has_below)
    keep_b = jnp.where(odd_floor == 0, has_below, has_above)
    flags = [1 - odd_floor, odd_floor, 3 - odd_facade, 2 + odd_facade, keep_a, keep_b, has_above, odd_floor, odd_facade]
    info = jnp.stack(flags).astype(jnp.int32)
    up, right = interface_rhs[0, 0, 0], interface_rhs[0, 0, 1]
    beside = upward(right, "facade", 1, True)
    below = upward(up, "floor", 1, False)
    operator, center = build_operator(info, inverse_factor[0, 0], near_coupling[0, 0], near_pattern[0, 0], cases)

    def shaped(*dims):
        return jax.ShapeDtypeStruct(dims, F32)

    whole, part, node, owned = shaped(size, cases), shaped(face, cases), shaped(NODE, cases), shaped(2 * face, cases)
    sent = [shaped(face + rows, cases) for rows in PADS]

    u0, *y0 = call(first_kernel, [whole, *sent], [], 1, info, below, beside, up, right, operator)
    u1, *y1 = call(functools.partial(next_kernel, False), [whole, *sent], [], 1, info, *y0, *exchanged(*y0), operator)
    u2, *y2 = call(functools.partial(next_kernel, True), [whole, *sent], [], 1, info, *y1, *exchanged(*y1), operator)
    u3, y_down, y_left, y_own, total = call(
        last_kernel,
        [whole, part, part, owned, node],
        [pltpu.VMEM((size, cases), F32)],
        1,
        info, *y2, *exchanged(*y2), u0, u1, u2, *y0, *y1, center, operator,
    )
    got_right = upward(y_left, "facade", -1, True)
    got_up = upward(y_down, "floor", -1, False)
    *stages, before, last = sum_stages()
    for stage in stages:
        (total,) = call(merge_kernel, [node], [], 0, *stage_parts(total, stage))
    w4, total = call(image_kernel, [owned, node], [], 1, info, y_own, got_up, got_right, *stage_parts(total, before))
    mult, resid = call(final_kernel, [owned, owned], [], 1, info, u0, u1, u2, u3, w4, *stage_parts(total, last))
    shape = (1, 1, 2, face, cases)
    return mult.reshape(shape), resid.reshape(shape)


def solution(mesh):
    spec = P("floor", "facade", None, None, None)
    flat = P("floor", "facade", None, None)
    return jax.shard_map(
        local,
        mesh=mesh,
        in_specs=(spec, flat, flat, flat),
        out_specs=(spec, spec),
        check_vma=False,
    )
```

profile of v0, /device:TPU:0, one launch (start us, length us, event | category | flops | bytes accessed | tf_op | source)
XLA Modules:
  0.0 75.2 jit_solution(2886217293103546099)
XLA Ops:
  0.6 1.0 %slice_bitcast_fusion = (f32[256,128]{1,0:T(8,128)S(1)}, f32[256,128]{1,0:T(8,128)S(1)}) fusion(f32[1,1,2,256,128]{4,3,2,1,0:T(8,128)} %param.4), kind=kLoop, calls=%fused_computation | loop fusion | bytes 524288 | tf_op jit(solution)/shard_map/squeeze | solution.py:446
  1.6 3.0 %collective-permute-start.1 = (f32[256,128]{1,0:T(8,128)S(1)}, f32[256,128]{1,0:T(8,128)S(1)}, u32[]{:S(2)}, u32[]{:S(2)}) collective-permute-start(f32[256,128]{1,0:T(8,128)S(1)} %get-tuple-element.54.right), channel_id=1, source_target_pairs={{0,1},{1,2},{2,3},{3,4},{4,5},{5,6},{6,7},{7,0},{8,9},{9,10},{10,1... | collective-permute-start | bytes 393224 | tf_op jit(solution)/shard_map/ppermute | solution.py:372
  4.6 1.5 %collective-permute-start = (f32[256,128]{1,0:T(8,128)S(1)}, f32[256,128]{1,0:T(8,128)S(1)}, u32[]{:S(2)}, u32[]{:S(2)}) collective-permute-start(f32[256,128]{1,0:T(8,128)S(1)} %get-tuple-element.55.up), channel_id=1, source_target_pairs={{0,8},{8,16},{16,24},{1,9},{9,17},{17,25},{2,10},{10,18},{18,26},{... | collective-permute-start | bytes 393224 | tf_op jit(solution)/shard_map/ppermute | solution.py:372
  6.1 0.1 stack.36.info
  6.2 9.3 %operator.1 = (bf16[1024,2048]{1,0:T(8,128)(2,1)S(1)}, f32[8,128]{1,0:T(8,128)S(1)}) custom-call(s32[9]{0:T(128)S(1)} %stack.36.info, s32[8,8]{1,0:T(8,128)} %bitcast.19, f32[1024,1024]{1,0:T(8,128)} %bitcast.17, bf16[1024,1024]{1,0:T(8,128)(2,1)} %bitcast.18), custom_call_target="tpu_custom_call" | custom-call | tf_op jit(solution)/shard_map/operator/pallas_call | solution.py:111
  15.6 0.0 collective-permute-done.1.beside
  15.6 1.8 %shard_map.59 = (f32[1024,128]{1,0:T(8,128)S(1)}, f32[264,128]{1,0:T(8,128)S(1)}, f32[256,128]{1,0:T(8,128)S(1)}, f32[280,128]{1,0:T(8,128)S(1)}, f32[272,128]{1,0:T(8,128)S(1)}) custom-call(s32[9]{0:T(128)S(1)} %stack.36.info, f32[256,128]{1,0:T(8,128)S(1)} %collective-permute-done.below, f32[256,128]{1,0:T(8,128)S(1)} %collective-permute-done.1.beside, ...), custom_call_target="tpu_custom_call" | custom-call | tf_op jit(solution)/shard_map/pallas_call | solution.py:423
  17.4 1.6 %collective-permute-start.4 = (f32[280,128]{1,0:T(8,128)S(1)}, f32[280,128]{1,0:T(8,128)S(1)}, u32[]{:S(2)}, u32[]{:S(2)}) collective-permute-start(f32[280,128]{1,0:T(8,128)S(1)} %get-tuple-element.32.yc.rest_2_), channel_id=1, source_target_pairs={{0,1},{1,0},{2,3},{3,2},{4,5},{5,4},{6,7},{7,6},{8,9},{9,8},{10,11... | collective-permute-start | bytes 430088 | tf_op jit(solution)/shard_map/ppermute | solution.py:382
  19.0 3.5 %collective-permute-start.5 = (f32[272,128]{1,0:T(8,128)S(1)}, f32[272,128]{1,0:T(8,128)S(1)}, u32[]{:S(2)}, u32[]{:S(2)}) collective-permute-start(f32[272,128]{1,0:T(8,128)S(1)} %get-tuple-element.33.yd.rest_3_), channel_id=1, source_target_pairs={{1,2},{2,1},{3,4},{4,3},{5,6},{6,5},{7,0},{0,7},{9,10},{10,9},{11,... | collective-permute-start | bytes 417800 | tf_op jit(solution)/shard_map/ppermute | solution.py:382
  22.5 1.5 %collective-permute-start.2 = (f32[264,128]{1,0:T(8,128)S(1)}, f32[264,128]{1,0:T(8,128)S(1)}, u32[]{:S(2)}, u32[]{:S(2)}) collective-permute-start(f32[264,128]{1,0:T(8,128)S(1)} %get-tuple-element.30.ya.rest_0_), channel_id=1, source_target_pairs={{0,8},{8,0},{16,24},{24,16},{1,9},{9,1},{17,25},{25,17},{2,10},{10... | collective-permute-start | bytes 405512 | tf_op jit(solution)/shard_map/ppermute | solution.py:382
  24.0 0.6 collective-permute-start.3
  24.6 5.0 %collective-permute-done.3.rb = f32[256,128]{1,0:T(8,128)S(1)} collective-permute-done((f32[256,128]{1,0:T(8,128)S(1)}, f32[256,128]{1,0:T(8,128)S(1)}, u32[]{:S(2)}, u32[]{:S(2)}) %collective-permute-start.3) | collective-permute-done | bytes 131104 | tf_op jit(solution)/shard_map/ppermute | solution.py:382
  29.6 0.0 collective-permute-done.5.rd
  29.6 0.0 collective-permute-done.4.rc
  29.7 1.8 %shard_map.60 = (f32[1024,128]{1,0:T(8,128)S(1)}, f32[264,128]{1,0:T(8,128)S(1)}, f32[256,128]{1,0:T(8,128)S(1)}, f32[280,128]{1,0:T(8,128)S(1)}, f32[272,128]{1,0:T(8,128)S(1)}) custom-call(s32[9]{0:T(128)S(1)} %stack.36.info, f32[264,128]{1,0:T(8,128)S(1)} %get-tuple-element.30.ya.rest_0_, f32[256,128]{1,0:T(8,128)S(1)} %get-tuple-element.31.yb.rest_1_, ...), custom_call_target="tpu_custom_call" | custom-call | tf_op jit(solution)/shard_map/pallas_call | solution.py:423
  31.5 0.1 collective-permute-start.8
  31.5 1.9 %collective-permute-start.9 = (f32[272,128]{1,0:T(8,128)S(1)}, f32[272,128]{1,0:T(8,128)S(1)}, u32[]{:S(2)}, u32[]{:S(2)}) collective-permute-start(f32[272,128]{1,0:T(8,128)S(1)} %get-tuple-element.38.yd.rest_7_), channel_id=1, source_target_pairs={{1,2},{2,1},{3,4},{4,3},{5,6},{6,5},{7,0},{0,7},{9,10},{10,9},{11,... | collective-permute-start | bytes 417800 | tf_op jit(solution)/shard_map/ppermute | solution.py:382
  33.4 0.9 %collective-permute-start.7 = (f32[256,128]{1,0:T(8,128)S(1)}, f32[256,128]{1,0:T(8,128)S(1)}, u32[]{:S(2)}, u32[]{:S(2)}) collective-permute-start(f32[256,128]{1,0:T(8,128)S(1)} %get-tuple-element.36.yb.rest_5_), channel_id=1, source_target_pairs={{8,16},{16,8},{24,0},{0,24},{9,17},{17,9},{25,1},{1,25},{10,18},{1... | collective-permute-start | bytes 393224 | tf_op jit(solution)/shard_map/ppermute | solution.py:382
  34.3 4.3 %collective-permute-done.7.rb = f32[256,128]{1,0:T(8,128)S(1)} collective-permute-done((f32[256,128]{1,0:T(8,128)S(1)}, f32[256,128]{1,0:T(8,128)S(1)}, u32[]{:S(2)}, u32[]{:S(2)}) %collective-permute-start.7) | collective-permute-done | bytes 131104 | tf_op jit(solution)/shard_map/ppermute | solution.py:382
  38.6 1.5 %collective-permute-done.9.rd = f32[272,128]{1,0:T(8,128)S(1)} collective-permute-done((f32[272,128]{1,0:T(8,128)S(1)}, f32[272,128]{1,0:T(8,128)S(1)}, u32[]{:S(2)}, u32[]{:S(2)}) %collective-permute-start.9) | collective-permute-done | bytes 139296 | tf_op jit(solution)/shard_map/ppermute | solution.py:382
  40.1 0.2 collective-permute-done.8.rc
  40.3 2.4 %shard_map.61 = (f32[1024,128]{1,0:T(8,128)S(1)}, f32[264,128]{1,0:T(8,128)S(1)}, f32[256,128]{1,0:T(8,128)S(1)}, f32[280,128]{1,0:T(8,128)S(1)}, f32[272,128]{1,0:T(8,128)S(1)}) custom-call(s32[9]{0:T(128)S(1)} %stack.36.info, f32[264,128]{1,0:T(8,128)S(1)} %get-tuple-element.35.ya.rest_4_, f32[256,128]{1,0:T(8,128)S(1)} %get-tuple-element.36.yb.rest_5_, ...), custom_call_target="tpu_custom_call" | custom-call | tf_op jit(solution)/shard_map/pallas_call | solution.py:423
  42.7 0.3 collective-permute-start.12
  43.0 1.9 %collective-permute-start.13 = (f32[272,128]{1,0:T(8,128)S(1)}, f32[272,128]{1,0:T(8,128)S(1)}, u32[]{:S(2)}, u32[]{:S(2)}) collective-permute-start(f32[272,128]{1,0:T(8,128)S(1)} %get-tuple-element.43.yd), channel_id=1, source_target_pairs={{1,2},{2,1},{3,4},{4,3},{5,6},{6,5},{7,0},{0,7},{9,10},{10,9},{11,... | collective-permute-start | bytes 417800 | tf_op jit(solution)/shard_map/ppermute | solution.py:382
  45.0 0.3 collective-permute-start.11
  45.3 4.8 %collective-permute-done.11.rb = f32[256,128]{1,0:T(8,128)S(1)} collective-permute-done((f32[256,128]{1,0:T(8,128)S(1)}, f32[256,128]{1,0:T(8,128)S(1)}, u32[]{:S(2)}, u32[]{:S(2)}) %collective-permute-start.11) | collective-permute-done | bytes 131104 | tf_op jit(solution)/shard_map/ppermute | solution.py:382
  50.1 0.7 collective-permute-done.13.rd
  50.9 3.2 %shard_map.62 = (f32[1024,128]{1,0:T(8,128)S(1)}, f32[256,128]{1,0:T(8,128)S(1)}, f32[256,128]{1,0:T(8,128)S(1)}, f32[512,128]{1,0:T(8,128)S(1)}, f32[24,128]{1,0:T(8,128)S(1)}) custom-call(s32[9]{0:T(128)S(1)} %stack.36.info, f32[264,128]{1,0:T(8,128)S(1)} %get-tuple-element.40.ya, f32[256,128]{1,0:T(8,128)S(1)} %get-tuple-element.41.yb, ...), custom_call_target="tpu_custom_call" | custom-call | tf_op jit(solution)/shard_map/pallas_call | solution.py:423
  54.1 1.3 %collective-permute-start.14 = (f32[256,128]{1,0:T(8,128)S(1)}, f32[256,128]{1,0:T(8,128)S(1)}, u32[]{:S(2)}, u32[]{:S(2)}) collective-permute-start(f32[256,128]{1,0:T(8,128)S(1)} %get-tuple-element.47), channel_id=1, source_target_pairs={{8,0},{16,8},{24,16},{9,1},{17,9},{25,17},{10,2},{18,10},{26,18},{... | collective-permute-start | bytes 393224 | tf_op jit(solution)/shard_map/ppermute | solution.py:372
  55.4 2.6 %collective-permute-start.15 = (f32[256,128]{1,0:T(8,128)S(1)}, f32[256,128]{1,0:T(8,128)S(1)}, u32[]{:S(2)}, u32[]{:S(2)}) collective-permute-start(f32[256,128]{1,0:T(8,128)S(1)} %get-tuple-element.48), channel_id=1, source_target_pairs={{0,7},{1,0},{2,1},{3,2},{4,3},{5,4},{6,5},{7,6},{8,15},{9,8},{10,9... | collective-permute-start | bytes 393224 | tf_op jit(solution)/shard_map/ppermute | solution.py:372
  57.9 0.8 %collective-permute-start.16 = (f32[24,128]{1,0:T(8,128)S(1)}, f32[24,128]{1,0:T(8,128)S(1)}, u32[]{:S(2)}, u32[]{:S(2)}) collective-permute-start(f32[24,128]{1,0:T(8,128)S(1)} %get-tuple-element.49.refs_0_), channel_id=1, source_target_pairs={{0,8},{1,9},{2,10},{3,11},{4,12},{5,13},{6,14},{7,15},{8,0},{9,1},... | collective-permute-start | bytes 36872 | tf_op jit(solution)/shard_map/ppermute | solution.py:398
  58.8 0.8 %collective-permute-done.16.refs_1_ = f32[24,128]{1,0:T(8,128)S(1)} collective-permute-done((f32[24,128]{1,0:T(8,128)S(1)}, f32[24,128]{1,0:T(8,128)S(1)}, u32[]{:S(2)}, u32[]{:S(2)}) %collective-permute-start.16) | collective-permute-done | bytes 12320 | tf_op jit(solution)/shard_map/ppermute | solution.py:398
  59.7 0.8 %collective-permute-start.19 = (f32[24,128]{1,0:T(8,128)S(1)}, f32[24,128]{1,0:T(8,128)S(1)}, u32[]{:S(2)}, u32[]{:S(2)}) collective-permute-start(f32[24,128]{1,0:T(8,128)S(1)} %shard_map.63.rest_0_), channel_id=1, source_target_pairs={{0,17},{1,16},{2,19},{3,18},{4,21},{5,20},{6,23},{7,22},{8,25},{9,... | collective-permute-start | bytes 36872 | tf_op jit(solution)/shard_map/ppermute | solution.py:398
  60.5 2.6 %collective-permute-start.18 = (f32[24,128]{1,0:T(8,128)S(1)}, f32[24,128]{1,0:T(8,128)S(1)}, u32[]{:S(2)}, u32[]{:S(2)}) collective-permute-start(f32[24,128]{1,0:T(8,128)S(1)} %shard_map.63.rest_0_), channel_id=1, source_target_pairs={{0,1},{1,0},{2,3},{3,2},{4,5},{5,4},{6,7},{7,6},{8,9},{9,8},{10,11... | collective-permute-start | bytes 36872 | tf_op jit(solution)/shard_map/ppermute | solution.py:398
  63.1 0.1 collective-permute-start.17
  63.2 1.1 %collective-permute-done.19.rest_3_ = f32[24,128]{1,0:T(8,128)S(1)} collective-permute-done((f32[24,128]{1,0:T(8,128)S(1)}, f32[24,128]{1,0:T(8,128)S(1)}, u32[]{:S(2)}, u32[]{:S(2)}) %collective-permute-start.19) | collective-permute-done | bytes 12320 | tf_op jit(solution)/shard_map/ppermute | solution.py:398
  64.3 0.4 collective-permute-done.18.rest_2_
  64.8 2.0 %collective-permute-done.17.rest_1_ = f32[24,128]{1,0:T(8,128)S(1)} collective-permute-done((f32[24,128]{1,0:T(8,128)S(1)}, f32[24,128]{1,0:T(8,128)S(1)}, u32[]{:S(2)}, u32[]{:S(2)}) %collective-permute-start.17) | collective-permute-done | bytes 12320 | tf_op jit(solution)/shard_map/ppermute | solution.py:398
  66.8 0.0 collective-permute-done.14.got_up
  66.8 0.0 collective-permute-done.15.got_right
  66.8 0.7 shard_map.64
  67.5 0.3 collective-permute-start.22
  67.7 0.4 collective-permute-start.21
  68.2 3.7 %collective-permute-start.20 = (f32[24,128]{1,0:T(8,128)S(1)}, f32[24,128]{1,0:T(8,128)S(1)}, u32[]{:S(2)}, u32[]{:S(2)}) collective-permute-start(f32[24,128]{1,0:T(8,128)S(1)} %get-tuple-element.51.rest_0_), channel_id=1, source_target_pairs={{0,2},{1,3},{2,0},{3,1},{4,6},{5,7},{6,4},{7,5},{8,10},{9,11},{10,... | collective-permute-start | bytes 36872 | tf_op jit(solution)/shard_map/ppermute | solution.py:398
  71.9 1.1 %collective-permute-done.22.rest_3_ = f32[24,128]{1,0:T(8,128)S(1)} collective-permute-done((f32[24,128]{1,0:T(8,128)S(1)}, f32[24,128]{1,0:T(8,128)S(1)}, u32[]{:S(2)}, u32[]{:S(2)}) %collective-permute-start.22) | collective-permute-done | bytes 12320 | tf_op jit(solution)/shard_map/ppermute | solution.py:398
  73.0 0.0 collective-permute-done.21.rest_2_
  73.0 0.6 collective-permute-done.20.rest_1_
  73.6 1.6 %shard_map.65 = (f32[512,128]{1,0:T(8,128)}, f32[512,128]{1,0:T(8,128)}) custom-call(s32[9]{0:T(128)S(1)} %stack.36.info, f32[1024,128]{1,0:T(8,128)S(1)} %get-tuple-element.29.u0, f32[1024,128]{1,0:T(8,128)S(1)} %get-tuple-element.34.u1, f32[1024,128]{1,0:T(8,128)S(1)} %get-tuple-element.39.u2, f32[1024,128]{1,0:T(8,128)S(1)} %get-tuple-element.45.u3, ...), custom_call_target="tpu_custom_call" | custom-call | tf_op jit(solution)/shard_map/pallas_call | solution.py:423
  (8 shorter events, 0.1 us)
Async XLA Ops:
  1.6 14.0 %collective-permute-start.1 = (f32[256,128]{1,0:T(8,128)S(1)}, f32[256,128]{1,0:T(8,128)S(1)}, u32[]{:S(2)}, u32[]{:S(2)}) collective-permute-start(f32[256,128]{1,0:T(8,128)S(1)} %get-tuple-element.54.right), channel_id=1, source_target_pairs={{0,1},{1,2},{2,3},{3,4},{4,5},{5,6},{6,7},{7,0},{8,9},{9,10},{10,1... | collective-permute-start | bytes 393224 | tf_op jit(solution)/shard_map/ppermute | solution.py:372
  4.6 10.9 %collective-permute-start = (f32[256,128]{1,0:T(8,128)S(1)}, f32[256,128]{1,0:T(8,128)S(1)}, u32[]{:S(2)}, u32[]{:S(2)}) collective-permute-start(f32[256,128]{1,0:T(8,128)S(1)} %get-tuple-element.55.up), channel_id=1, source_target_pairs={{0,8},{8,16},{16,24},{1,9},{9,17},{17,25},{2,10},{10,18},{18,26},{... | collective-permute-start | bytes 393224 | tf_op jit(solution)/shard_map/ppermute | solution.py:372
  17.4 12.2 %collective-permute-start.4 = (f32[280,128]{1,0:T(8,128)S(1)}, f32[280,128]{1,0:T(8,128)S(1)}, u32[]{:S(2)}, u32[]{:S(2)}) collective-permute-start(f32[280,128]{1,0:T(8,128)S(1)} %get-tuple-element.32.yc.rest_2_), channel_id=1, source_target_pairs={{0,1},{1,0},{2,3},{3,2},{4,5},{5,4},{6,7},{7,6},{8,9},{9,8},{10,11... | collective-permute-start | bytes 430088 | tf_op jit(solution)/shard_map/ppermute | solution.py:382
  19.0 10.6 %collective-permute-start.5 = (f32[272,128]{1,0:T(8,128)S(1)}, f32[272,128]{1,0:T(8,128)S(1)}, u32[]{:S(2)}, u32[]{:S(2)}) collective-permute-start(f32[272,128]{1,0:T(8,128)S(1)} %get-tuple-element.33.yd.rest_3_), channel_id=1, source_target_pairs={{1,2},{2,1},{3,4},{4,3},{5,6},{6,5},{7,0},{0,7},{9,10},{10,9},{11,... | collective-permute-start | bytes 417800 | tf_op jit(solution)/shard_map/ppermute | solution.py:382
  22.5 7.1 %collective-permute-start.2 = (f32[264,128]{1,0:T(8,128)S(1)}, f32[264,128]{1,0:T(8,128)S(1)}, u32[]{:S(2)}, u32[]{:S(2)}) collective-permute-start(f32[264,128]{1,0:T(8,128)S(1)} %get-tuple-element.30.ya.rest_0_), channel_id=1, source_target_pairs={{0,8},{8,0},{16,24},{24,16},{1,9},{9,1},{17,25},{25,17},{2,10},{10... | collective-permute-start | bytes 405512 | tf_op jit(solution)/shard_map/ppermute | solution.py:382
  24.0 5.6 %collective-permute-start.3 = (f32[256,128]{1,0:T(8,128)S(1)}, f32[256,128]{1,0:T(8,128)S(1)}, u32[]{:S(2)}, u32[]{:S(2)}) collective-permute-start(f32[256,128]{1,0:T(8,128)S(1)} %get-tuple-element.31.yb.rest_1_), channel_id=1, source_target_pairs={{8,16},{16,8},{24,0},{0,24},{9,17},{17,9},{25,1},{1,25},{10,18},{1... | collective-permute-start | bytes 393224 | tf_op jit(solution)/shard_map/ppermute | solution.py:382
  31.5 8.8 %collective-permute-start.8 = (f32[280,128]{1,0:T(8,128)S(1)}, f32[280,128]{1,0:T(8,128)S(1)}, u32[]{:S(2)}, u32[]{:S(2)}) collective-permute-start(f32[280,128]{1,0:T(8,128)S(1)} %get-tuple-element.37.yc.rest_6_), channel_id=1, source_target_pairs={{0,1},{1,0},{2,3},{3,2},{4,5},{5,4},{6,7},{7,6},{8,9},{9,8},{10,11... | collective-permute-start | bytes 430088 | tf_op jit(solution)/shard_map/ppermute | solution.py:382
  31.5 8.6 %collective-permute-start.9 = (f32[272,128]{1,0:T(8,128)S(1)}, f32[272,128]{1,0:T(8,128)S(1)}, u32[]{:S(2)}, u32[]{:S(2)}) collective-permute-start(f32[272,128]{1,0:T(8,128)S(1)} %get-tuple-element.38.yd.rest_7_), channel_id=1, source_target_pairs={{1,2},{2,1},{3,4},{4,3},{5,6},{6,5},{7,0},{0,7},{9,10},{10,9},{11,... | collective-permute-start | bytes 417800 | tf_op jit(solution)/shard_map/ppermute | solution.py:382
  33.4 5.2 %collective-permute-start.6 = (f32[264,128]{1,0:T(8,128)S(1)}, f32[264,128]{1,0:T(8,128)S(1)}, u32[]{:S(2)}, u32[]{:S(2)}) collective-permute-start(f32[264,128]{1,0:T(8,128)S(1)} %get-tuple-element.35.ya.rest_4_), channel_id=1, source_target_pairs={{0,8},{8,0},{16,24},{24,16},{1,9},{9,1},{17,25},{25,17},{2,10},{10... | collective-permute-start | bytes 405512 | tf_op jit(solution)/shard_map/ppermute | solution.py:382
  33.4 5.2 %collective-permute-start.7 = (f32[256,128]{1,0:T(8,128)S(1)}, f32[256,128]{1,0:T(8,128)S(1)}, u32[]{:S(2)}, u32[]{:S(2)}) collective-permute-start(f32[256,128]{1,0:T(8,128)S(1)} %get-tuple-element.36.yb.rest_5_), channel_id=1, source_target_pairs={{8,16},{16,8},{24,0},{0,24},{9,17},{17,9},{25,1},{1,25},{10,18},{1... | collective-permute-start | bytes 393224 | tf_op jit(solution)/shard_map/ppermute | solution.py:382
  42.7 8.2 %collective-permute-start.12 = (f32[280,128]{1,0:T(8,128)S(1)}, f32[280,128]{1,0:T(8,128)S(1)}, u32[]{:S(2)}, u32[]{:S(2)}) collective-permute-start(f32[280,128]{1,0:T(8,128)S(1)} %get-tuple-element.42.yc), channel_id=1, source_target_pairs={{0,1},{1,0},{2,3},{3,2},{4,5},{5,4},{6,7},{7,6},{8,9},{9,8},{10,11... | collective-permute-start | bytes 430088 | tf_op jit(solution)/shard_map/ppermute | solution.py:382
  43.0 7.8 %collective-permute-start.13 = (f32[272,128]{1,0:T(8,128)S(1)}, f32[272,128]{1,0:T(8,128)S(1)}, u32[]{:S(2)}, u32[]{:S(2)}) collective-permute-start(f32[272,128]{1,0:T(8,128)S(1)} %get-tuple-element.43.yd), channel_id=1, source_target_pairs={{1,2},{2,1},{3,4},{4,3},{5,6},{6,5},{7,0},{0,7},{9,10},{10,9},{11,... | collective-permute-start | bytes 417800 | tf_op jit(solution)/shard_map/ppermute | solution.py:382
  45.0 5.2 %collective-permute-start.10 = (f32[264,128]{1,0:T(8,128)S(1)}, f32[264,128]{1,0:T(8,128)S(1)}, u32[]{:S(2)}, u32[]{:S(2)}) collective-permute-start(f32[264,128]{1,0:T(8,128)S(1)} %get-tuple-element.40.ya), channel_id=1, source_target_pairs={{0,8},{8,0},{16,24},{24,16},{1,9},{9,1},{17,25},{25,17},{2,10},{10... | collective-permute-start | bytes 405512 | tf_op jit(solution)/shard_map/ppermute | solution.py:382
  45.0 5.2 %collective-permute-start.11 = (f32[256,128]{1,0:T(8,128)S(1)}, f32[256,128]{1,0:T(8,128)S(1)}, u32[]{:S(2)}, u32[]{:S(2)}) collective-permute-start(f32[256,128]{1,0:T(8,128)S(1)} %get-tuple-element.41.yb), channel_id=1, source_target_pairs={{8,16},{16,8},{24,0},{0,24},{9,17},{17,9},{25,1},{1,25},{10,18},{1... | collective-permute-start | bytes 393224 | tf_op jit(solution)/shard_map/ppermute | solution.py:382
  54.1 12.7 %collective-permute-start.14 = (f32[256,128]{1,0:T(8,128)S(1)}, f32[256,128]{1,0:T(8,128)S(1)}, u32[]{:S(2)}, u32[]{:S(2)}) collective-permute-start(f32[256,128]{1,0:T(8,128)S(1)} %get-tuple-element.47), channel_id=1, source_target_pairs={{8,0},{16,8},{24,16},{9,1},{17,9},{25,17},{10,2},{18,10},{26,18},{... | collective-permute-start | bytes 393224 | tf_op jit(solution)/shard_map/ppermute | solution.py:372
  55.4 11.4 %collective-permute-start.15 = (f32[256,128]{1,0:T(8,128)S(1)}, f32[256,128]{1,0:T(8,128)S(1)}, u32[]{:S(2)}, u32[]{:S(2)}) collective-permute-start(f32[256,128]{1,0:T(8,128)S(1)} %get-tuple-element.48), channel_id=1, source_target_pairs={{0,7},{1,0},{2,1},{3,2},{4,3},{5,4},{6,5},{7,6},{8,15},{9,8},{10,9... | collective-permute-start | bytes 393224 | tf_op jit(solution)/shard_map/ppermute | solution.py:372
  57.9 1.7 %collective-permute-start.16 = (f32[24,128]{1,0:T(8,128)S(1)}, f32[24,128]{1,0:T(8,128)S(1)}, u32[]{:S(2)}, u32[]{:S(2)}) collective-permute-start(f32[24,128]{1,0:T(8,128)S(1)} %get-tuple-element.49.refs_0_), channel_id=1, source_target_pairs={{0,8},{1,9},{2,10},{3,11},{4,12},{5,13},{6,14},{7,15},{8,0},{9,1},... | collective-permute-start | bytes 36872 | tf_op jit(solution)/shard_map/ppermute | solution.py:398
  59.7 4.7 %collective-permute-start.19 = (f32[24,128]{1,0:T(8,128)S(1)}, f32[24,128]{1,0:T(8,128)S(1)}, u32[]{:S(2)}, u32[]{:S(2)}) collective-permute-start(f32[24,128]{1,0:T(8,128)S(1)} %shard_map.63.rest_0_), channel_id=1, source_target_pairs={{0,17},{1,16},{2,19},{3,18},{4,21},{5,20},{6,23},{7,22},{8,25},{9,... | collective-permute-start | bytes 36872 | tf_op jit(solution)/shard_map/ppermute | solution.py:398
  60.5 4.3 %collective-permute-start.18 = (f32[24,128]{1,0:T(8,128)S(1)}, f32[24,128]{1,0:T(8,128)S(1)}, u32[]{:S(2)}, u32[]{:S(2)}) collective-permute-start(f32[24,128]{1,0:T(8,128)S(1)} %shard_map.63.rest_0_), channel_id=1, source_target_pairs={{0,1},{1,0},{2,3},{3,2},{4,5},{5,4},{6,7},{7,6},{8,9},{9,8},{10,11... | collective-permute-start | bytes 36872 | tf_op jit(solution)/shard_map/ppermute | solution.py:398
  63.1 3.7 %collective-permute-start.17 = (f32[24,128]{1,0:T(8,128)S(1)}, f32[24,128]{1,0:T(8,128)S(1)}, u32[]{:S(2)}, u32[]{:S(2)}) collective-permute-start(f32[24,128]{1,0:T(8,128)S(1)} %shard_map.63.rest_0_), channel_id=1, source_target_pairs={{0,16},{1,17},{2,18},{3,19},{4,20},{5,21},{6,22},{7,23},{8,24},{9,... | collective-permute-start | bytes 36872 | tf_op jit(solution)/shard_map/ppermute | solution.py:398
  67.5 5.6 %collective-permute-start.22 = (f32[24,128]{1,0:T(8,128)S(1)}, f32[24,128]{1,0:T(8,128)S(1)}, u32[]{:S(2)}, u32[]{:S(2)}) collective-permute-start(f32[24,128]{1,0:T(8,128)S(1)} %get-tuple-element.51.rest_0_), channel_id=1, source_target_pairs={{0,6},{1,7},{2,4},{3,5},{4,2},{5,3},{6,0},{7,1},{8,14},{9,15},{10,... | collective-permute-start | bytes 36872 | tf_op jit(solution)/shard_map/ppermute | solution.py:398
  67.7 5.3 %collective-permute-start.21 = (f32[24,128]{1,0:T(8,128)S(1)}, f32[24,128]{1,0:T(8,128)S(1)}, u32[]{:S(2)}, u32[]{:S(2)}) collective-permute-start(f32[24,128]{1,0:T(8,128)S(1)} %get-tuple-element.51.rest_0_), channel_id=1, source_target_pairs={{0,4},{1,5},{2,6},{3,7},{4,0},{5,1},{6,2},{7,3},{8,12},{9,13},{10,... | collective-permute-start | bytes 36872 | tf_op jit(solution)/shard_map/ppermute | solution.py:398
  68.2 5.4 %collective-permute-start.20 = (f32[24,128]{1,0:T(8,128)S(1)}, f32[24,128]{1,0:T(8,128)S(1)}, u32[]{:S(2)}, u32[]{:S(2)}) collective-permute-start(f32[24,128]{1,0:T(8,128)S(1)} %get-tuple-element.51.rest_0_), channel_id=1, source_target_pairs={{0,2},{1,3},{2,0},{3,1},{4,6},{5,7},{6,4},{7,5},{8,10},{9,11},{10,... | collective-permute-start | bytes 36872 | tf_op jit(solution)/shard_map/ppermute | solution.py:398
where the time goes:
time: 75.4 us; the launch traced here: 75.2 us
  starting transfers between devices  29.8 us (40%)
  waiting for transfers between devices  22.7 us (30%)
  Pallas kernels  20.9 us (28%)
  local copies, waits for them, and re-layouts  1.07 us (1%)
  between operations  0.77 us (1%)
    ppermute x12, waiting for transfers between devices, swapped(): return lax.ppermute(value, axis, pairs)  16.6 us
    ppermute x12, starting transfers between devices, swapped(): return lax.ppermute(value, axis, pairs)  12.6 us
    pallas_call x7, Pallas kernels, call(): pl.pallas_call(kernel, in_specs=[pl.BlockSpec(memory_space=pltpu.SMEM)] *...  11.6 us
    pallas_call x1, Pallas kernels, build_operator(): pl.pallas_call(operator_kernel, in_specs=[pl.BlockSpec(memory_space=pltpu...  9.34 us
    ppermute x7, starting transfers between devices, flipped(): return lax.ppermute(value, AXES, pairs)  8.85 us
    ppermute x4, starting transfers between devices, upward(): return lax.ppermute(value, axis, pairs)  8.34 us
    ppermute x7, waiting for transfers between devices, flipped(): return lax.ppermute(value, AXES, pairs)  6.06 us
  transfers between devices with their start and end apart: 23, of which 12 were waited for; matrix products, arithmetic and copies ran while one was open for 0% of the time, Pallas kernels for 12%

commit v1 on v0

--- a/solution.py
+++ b/solution.py
@@ -350,20 +350,23 @@
     write_node(node, *merged(parts))
 
 
-def final_kernel(info, u0, u1, u2, u3, w4_ref, *rest):
+def final_kernel(info, u0, u1, u2, u3, yo_ref, got_up, got_right, *rest):
     parts, (mult, resid) = rest[:-2], rest[-2:]
     rows, middle = merged(parts)
     scale = 1.0 / middle
     x, r = conjugate_coefficients(rows)
     x = [value * scale for value in powers(x, scale)]
     r = powers(r, scale)
-    face = w4_ref.shape[0] // 2
-    for f in range(2):
+    face = got_up.shape[0]
+    for f, got in enumerate((got_up, got_right)):
         place = pl.ds(pl.multiple_of(info[SLOT + 2 * f + 1] * face, face), face)
         here = slice(f * face, (f + 1) * face)
         w = [u[place, :] for u in (u0, u1, u2, u3)]
+        image = yo_ref[here, :] - got[...]
+        if f == 0:
+            image = jnp.where(info[KEEP + 2] != 0, image, 0.0)
         mult[here, :] = x[0] * w[0] + x[1] * w[1] + x[2] * w[2] + x[3] * w[3]
-        resid[here, :] = r[0] * w[0] + r[1] * w[1] + r[2] * w[2] + r[3] * w[3] + r[4] * w4_ref[here, :]
+        resid[here, :] = r[0] * w[0] + r[1] * w[1] + r[2] * w[2] + r[3] * w[3] + r[4] * image
 
 
 def upward(value, axis, steps, wrap):
@@ -419,7 +422,10 @@
     return [value, flipped(value, f1, c1), flipped(value, f2, c2), flipped(value, f1 ^ f2, c1 ^ c2)]
 
 
-def call(kernel, outs, scratch, smem, *args):
+MERGE_FLOPS = 3000000000
+
+
+def call(kernel, outs, scratch, smem, *args, flops=0):
     return pl.pallas_call(
         kernel,
         in_specs=[pl.BlockSpec(memory_space=pltpu.SMEM)] * smem
@@ -428,6 +434,7 @@
         out_shape=outs,
         scratch_shapes=scratch,
         compiler_params=params(16),
+        cost_estimate=pl.CostEstimate(flops=flops, bytes_accessed=0, transcendentals=0) if flops else None,
     )(*args)
 
 
@@ -467,10 +474,9 @@
     got_right = upward(y_left, "facade", -1, True)
     got_up = upward(y_down, "floor", -1, False)
     *stages, before, last = sum_stages()
-    for stage in stages:
-        (total,) = call(merge_kernel, [node], [], 0, *stage_parts(total, stage))
-    w4, total = call(image_kernel, [owned, node], [], 1, info, y_own, got_up, got_right, *stage_parts(total, before))
-    mult, resid = call(final_kernel, [owned, owned], [], 1, info, u0, u1, u2, u3, w4, *stage_parts(total, last))
+    for stage in stages + [before]:
+        (total,) = call(merge_kernel, [node], [], 0, *stage_parts(total, stage), flops=MERGE_FLOPS if stage is before else 0)
+    mult, resid = call(final_kernel, [owned, owned], [], 1, info, u0, u1, u2, u3, y_own, got_up, got_right, *stage_parts(total, last))
     shape = (1, 1, 2, face, cases)
     return mult.reshape(shape), resid.reshape(shape)
 

time: 75.4 us -> 70.9 us (0.940)
  waiting for transfers between devices: 22.7 us -> 19.4 us
    ppermute x7, waiting for transfers between devices: 6.06 us -> 2.78 us  [flipped(): return lax.ppermute(value, AXES, pairs)]
  transfers between devices with their start and end apart: 23 -> 23, of which waited for: 12 -> 9; matrix products, arithmetic and copies ran while one was open for 0% -> 0% of each run, Pallas kernels for 12% -> 13%
where the time goes in v1:
time: 70.9 us; the launch traced here: 70.7 us
  starting transfers between devices  29.1 us (41%)
  Pallas kernels  20.3 us (29%)
  waiting for transfers between devices  19.4 us (27%)
  local copies, waits for them, and re-layouts  1.07 us (2%)
  between operations  0.77 us (1%)
    ppermute x12, waiting for transfers between devices, swapped(): return lax.ppermute(value, axis, pairs)  16.6 us
    ppermute x12, starting transfers between devices, swapped(): return lax.ppermute(value, axis, pairs)  12.6 us
    pallas_call x7, Pallas kernels, call(): pl.pallas_call(kernel, in_specs=[pl.BlockSpec(memory_space=pltpu.SMEM)] *...  11 us
    pallas_call x1, Pallas kernels, build_operator(): pl.pallas_call(operator_kernel, in_specs=[pl.BlockSpec(memory_space=pltpu...  9.34 us
    ppermute x4, starting transfers between devices, upward(): return lax.ppermute(value, axis, pairs)  8.33 us
    ppermute x7, starting transfers between devices, flipped(): return lax.ppermute(value, AXES, pairs)  8.14 us
    ppermute x7, waiting for transfers between devices, flipped(): return lax.ppermute(value, AXES, pairs)  2.78 us
  transfers between devices with their start and end apart: 23, of which 9 were waited for; matrix products, arithmetic and copies ran while one was open for 0% of the time, Pallas kernels for 13%

profile of v1, /device:TPU:0, one launch (start us, length us, event | category | flops | bytes accessed | tf_op | source)
XLA Modules:
  0.0 70.7 jit_solution(18248656546541112402)
XLA Ops:
  0.6 1.0 %slice_bitcast_fusion = (f32[256,128]{1,0:T(8,128)S(1)}, f32[256,128]{1,0:T(8,128)S(1)}) fusion(f32[1,1,2,256,128]{4,3,2,1,0:T(8,128)} %param.4), kind=kLoop, calls=%fused_computation | loop fusion | bytes 524288 | tf_op jit(solution)/shard_map/squeeze | solution.py:453
  1.6 3.0 %collective-permute-start.1 = (f32[256,128]{1,0:T(8,128)S(1)}, f32[256,128]{1,0:T(8,128)S(1)}, u32[]{:S(2)}, u32[]{:S(2)}) collective-permute-start(f32[256,128]{1,0:T(8,128)S(1)} %get-tuple-element.50.right), channel_id=1, source_target_pairs={{0,1},{1,2},{2,3},{3,4},{4,5},{5,6},{6,7},{7,0},{8,9},{9,10},{10,1... | collective-permute-start | bytes 393224 | tf_op jit(solution)/shard_map/ppermute | solution.py:375
  4.6 1.5 %collective-permute-start = (f32[256,128]{1,0:T(8,128)S(1)}, f32[256,128]{1,0:T(8,128)S(1)}, u32[]{:S(2)}, u32[]{:S(2)}) collective-permute-start(f32[256,128]{1,0:T(8,128)S(1)} %get-tuple-element.51.up), channel_id=1, source_target_pairs={{0,8},{8,16},{16,24},{1,9},{9,17},{17,25},{2,10},{10,18},{18,26},{... | collective-permute-start | bytes 393224 | tf_op jit(solution)/shard_map/ppermute | solution.py:375
  6.1 0.1 stack.36.info
  6.2 9.3 %operator.1 = (bf16[1024,2048]{1,0:T(8,128)(2,1)S(1)}, f32[8,128]{1,0:T(8,128)S(1)}) custom-call(s32[9]{0:T(128)S(1)} %stack.36.info, s32[8,8]{1,0:T(8,128)} %bitcast.19, f32[1024,1024]{1,0:T(8,128)} %bitcast.17, bf16[1024,1024]{1,0:T(8,128)(2,1)} %bitcast.18), custom_call_target="tpu_custom_call" | custom-call | tf_op jit(solution)/shard_map/operator/pallas_call | solution.py:111
  15.6 0.0 collective-permute-done.1.beside
  15.6 0.0 collective-permute-done.below
  15.6 1.8 %shard_map.59 = (f32[1024,128]{1,0:T(8,128)S(1)}, f32[264,128]{1,0:T(8,128)S(1)}, f32[256,128]{1,0:T(8,128)S(1)}, f32[280,128]{1,0:T(8,128)S(1)}, f32[272,128]{1,0:T(8,128)S(1)}) custom-call(s32[9]{0:T(128)S(1)} %stack.36.info, f32[256,128]{1,0:T(8,128)S(1)} %collective-permute-done.below, f32[256,128]{1,0:T(8,128)S(1)} %collective-permute-done.1.beside, ...), custom_call_target="tpu_custom_call" | custom-call | tf_op jit(solution)/shard_map/pallas_call | solution.py:429
  17.4 1.6 %collective-permute-start.4 = (f32[280,128]{1,0:T(8,128)S(1)}, f32[280,128]{1,0:T(8,128)S(1)}, u32[]{:S(2)}, u32[]{:S(2)}) collective-permute-start(f32[280,128]{1,0:T(8,128)S(1)} %get-tuple-element.30.yc.rest_2_), channel_id=1, source_target_pairs={{0,1},{1,0},{2,3},{3,2},{4,5},{5,4},{6,7},{7,6},{8,9},{9,8},{10,11... | collective-permute-start | bytes 430088 | tf_op jit(solution)/shard_map/ppermute | solution.py:385
  19.0 3.5 %collective-permute-start.5 = (f32[272,128]{1,0:T(8,128)S(1)}, f32[272,128]{1,0:T(8,128)S(1)}, u32[]{:S(2)}, u32[]{:S(2)}) collective-permute-start(f32[272,128]{1,0:T(8,128)S(1)} %get-tuple-element.31.yd.rest_3_), channel_id=1, source_target_pairs={{1,2},{2,1},{3,4},{4,3},{5,6},{6,5},{7,0},{0,7},{9,10},{10,9},{11,... | collective-permute-start | bytes 417800 | tf_op jit(solution)/shard_map/ppermute | solution.py:385
  22.5 1.5 %collective-permute-start.2 = (f32[264,128]{1,0:T(8,128)S(1)}, f32[264,128]{1,0:T(8,128)S(1)}, u32[]{:S(2)}, u32[]{:S(2)}) collective-permute-start(f32[264,128]{1,0:T(8,128)S(1)} %get-tuple-element.28.ya.rest_0_), channel_id=1, source_target_pairs={{0,8},{8,0},{16,24},{24,16},{1,9},{9,1},{17,25},{25,17},{2,10},{10... | collective-permute-start | bytes 405512 | tf_op jit(solution)/shard_map/ppermute | solution.py:385
  24.0 0.6 collective-permute-start.3
  24.6 5.0 %collective-permute-done.3.rb = f32[256,128]{1,0:T(8,128)S(1)} collective-permute-done((f32[256,128]{1,0:T(8,128)S(1)}, f32[256,128]{1,0:T(8,128)S(1)}, u32[]{:S(2)}, u32[]{:S(2)}) %collective-permute-start.3) | collective-permute-done | bytes 131104 | tf_op jit(solution)/shard_map/ppermute | solution.py:385
  29.7 1.8 %shard_map.60 = (f32[1024,128]{1,0:T(8,128)S(1)}, f32[264,128]{1,0:T(8,128)S(1)}, f32[256,128]{1,0:T(8,128)S(1)}, f32[280,128]{1,0:T(8,128)S(1)}, f32[272,128]{1,0:T(8,128)S(1)}) custom-call(s32[9]{0:T(128)S(1)} %stack.36.info, f32[264,128]{1,0:T(8,128)S(1)} %get-tuple-element.28.ya.rest_0_, f32[256,128]{1,0:T(8,128)S(1)} %get-tuple-element.29.yb.rest_1_, ...), custom_call_target="tpu_custom_call" | custom-call | tf_op jit(solution)/shard_map/pallas_call | solution.py:429
  31.5 0.1 collective-permute-start.8
  31.5 1.9 %collective-permute-start.9 = (f32[272,128]{1,0:T(8,128)S(1)}, f32[272,128]{1,0:T(8,128)S(1)}, u32[]{:S(2)}, u32[]{:S(2)}) collective-permute-start(f32[272,128]{1,0:T(8,128)S(1)} %get-tuple-element.36.yd.rest_7_), channel_id=1, source_target_pairs={{1,2},{2,1},{3,4},{4,3},{5,6},{6,5},{7,0},{0,7},{9,10},{10,9},{11,... | collective-permute-start | bytes 417800 | tf_op jit(solution)/shard_map/ppermute | solution.py:385
  33.4 0.0 collective-permute-start.6
  33.4 0.9 %collective-permute-start.7 = (f32[256,128]{1,0:T(8,128)S(1)}, f32[256,128]{1,0:T(8,128)S(1)}, u32[]{:S(2)}, u32[]{:S(2)}) collective-permute-start(f32[256,128]{1,0:T(8,128)S(1)} %get-tuple-element.34.yb.rest_5_), channel_id=1, source_target_pairs={{8,16},{16,8},{24,0},{0,24},{9,17},{17,9},{25,1},{1,25},{10,18},{1... | collective-permute-start | bytes 393224 | tf_op jit(solution)/shard_map/ppermute | solution.py:385
  34.3 4.3 %collective-permute-done.7.rb = f32[256,128]{1,0:T(8,128)S(1)} collective-permute-done((f32[256,128]{1,0:T(8,128)S(1)}, f32[256,128]{1,0:T(8,128)S(1)}, u32[]{:S(2)}, u32[]{:S(2)}) %collective-permute-start.7) | collective-permute-done | bytes 131104 | tf_op jit(solution)/shard_map/ppermute | solution.py:385
  38.6 1.5 %collective-permute-done.9.rd = f32[272,128]{1,0:T(8,128)S(1)} collective-permute-done((f32[272,128]{1,0:T(8,128)S(1)}, f32[272,128]{1,0:T(8,128)S(1)}, u32[]{:S(2)}, u32[]{:S(2)}) %collective-permute-start.9) | collective-permute-done | bytes 139296 | tf_op jit(solution)/shard_map/ppermute | solution.py:385
  40.1 0.2 collective-permute-done.8.rc
  40.3 2.4 %shard_map.61 = (f32[1024,128]{1,0:T(8,128)S(1)}, f32[264,128]{1,0:T(8,128)S(1)}, f32[256,128]{1,0:T(8,128)S(1)}, f32[280,128]{1,0:T(8,128)S(1)}, f32[272,128]{1,0:T(8,128)S(1)}) custom-call(s32[9]{0:T(128)S(1)} %stack.36.info, f32[264,128]{1,0:T(8,128)S(1)} %get-tuple-element.33.ya.rest_4_, f32[256,128]{1,0:T(8,128)S(1)} %get-tuple-element.34.yb.rest_5_, ...), custom_call_target="tpu_custom_call" | custom-call | tf_op jit(solution)/shard_map/pallas_call | solution.py:429
  42.7 0.3 collective-permute-start.12
  43.0 1.9 %collective-permute-start.13 = (f32[272,128]{1,0:T(8,128)S(1)}, f32[272,128]{1,0:T(8,128)S(1)}, u32[]{:S(2)}, u32[]{:S(2)}) collective-permute-start(f32[272,128]{1,0:T(8,128)S(1)} %get-tuple-element.41.yd), channel_id=1, source_target_pairs={{1,2},{2,1},{3,4},{4,3},{5,6},{6,5},{7,0},{0,7},{9,10},{10,9},{11,... | collective-permute-start | bytes 417800 | tf_op jit(solution)/shard_map/ppermute | solution.py:385
  45.0 0.3 collective-permute-start.11
  45.3 4.8 %collective-permute-done.11.rb = f32[256,128]{1,0:T(8,128)S(1)} collective-permute-done((f32[256,128]{1,0:T(8,128)S(1)}, f32[256,128]{1,0:T(8,128)S(1)}, u32[]{:S(2)}, u32[]{:S(2)}) %collective-permute-start.11) | collective-permute-done | bytes 131104 | tf_op jit(solution)/shard_map/ppermute | solution.py:385
  50.1 0.7 %collective-permute-done.13.rd = f32[272,128]{1,0:T(8,128)S(1)} collective-permute-done((f32[272,128]{1,0:T(8,128)S(1)}, f32[272,128]{1,0:T(8,128)S(1)}, u32[]{:S(2)}, u32[]{:S(2)}) %collective-permute-start.13) | collective-permute-done | bytes 139296 | tf_op jit(solution)/shard_map/ppermute | solution.py:385
  50.8 3.2 %shard_map.62 = (f32[1024,128]{1,0:T(8,128)S(1)}, f32[256,128]{1,0:T(8,128)S(1)}, f32[256,128]{1,0:T(8,128)S(1)}, f32[512,128]{1,0:T(8,128)S(1)}, f32[24,128]{1,0:T(8,128)S(1)}) custom-call(s32[9]{0:T(128)S(1)} %stack.36.info, f32[264,128]{1,0:T(8,128)S(1)} %get-tuple-element.38.ya, f32[256,128]{1,0:T(8,128)S(1)} %get-tuple-element.39.yb, ...), custom_call_target="tpu_custom_call" | custom-call | tf_op jit(solution)/shard_map/pallas_call | solution.py:429
  54.0 0.1 collective-permute-start.16
  54.2 1.1 %collective-permute-done.16.refs_1_ = f32[24,128]{1,0:T(8,128)S(1)} collective-permute-done((f32[24,128]{1,0:T(8,128)S(1)}, f32[24,128]{1,0:T(8,128)S(1)}, u32[]{:S(2)}, u32[]{:S(2)}) %collective-permute-start.16) | collective-permute-done | bytes 12320 | tf_op jit(solution)/shard_map/ppermute | solution.py:401
  55.3 0.6 collective-permute-start.19
  55.9 1.4 %collective-permute-start.18 = (f32[24,128]{1,0:T(8,128)S(1)}, f32[24,128]{1,0:T(8,128)S(1)}, u32[]{:S(2)}, u32[]{:S(2)}) collective-permute-start(f32[24,128]{1,0:T(8,128)S(1)} %shard_map.63.refs_0_), channel_id=1, source_target_pairs={{0,1},{1,0},{2,3},{3,2},{4,5},{5,4},{6,7},{7,6},{8,9},{9,8},{10,11... | collective-permute-start | bytes 36872 | tf_op jit(solution)/shard_map/ppermute | solution.py:401
  57.3 1.6 %collective-permute-start.17 = (f32[24,128]{1,0:T(8,128)S(1)}, f32[24,128]{1,0:T(8,128)S(1)}, u32[]{:S(2)}, u32[]{:S(2)}) collective-permute-start(f32[24,128]{1,0:T(8,128)S(1)} %shard_map.63.refs_0_), channel_id=1, source_target_pairs={{0,16},{1,17},{2,18},{3,19},{4,20},{5,21},{6,22},{7,23},{8,24},{9,... | collective-permute-start | bytes 36872 | tf_op jit(solution)/shard_map/ppermute | solution.py:401
  58.9 1.3 %collective-permute-start.14 = (f32[256,128]{1,0:T(8,128)S(1)}, f32[256,128]{1,0:T(8,128)S(1)}, u32[]{:S(2)}, u32[]{:S(2)}) collective-permute-start(f32[256,128]{1,0:T(8,128)S(1)} %get-tuple-element.45), channel_id=1, source_target_pairs={{8,0},{16,8},{24,16},{9,1},{17,9},{25,17},{10,2},{18,10},{26,18},{... | collective-permute-start | bytes 393224 | tf_op jit(solution)/shard_map/ppermute | solution.py:375
  60.2 2.6 %collective-permute-start.15 = (f32[256,128]{1,0:T(8,128)S(1)}, f32[256,128]{1,0:T(8,128)S(1)}, u32[]{:S(2)}, u32[]{:S(2)}) collective-permute-start(f32[256,128]{1,0:T(8,128)S(1)} %get-tuple-element.46), channel_id=1, source_target_pairs={{0,7},{1,0},{2,1},{3,2},{4,3},{5,4},{6,5},{7,6},{8,15},{9,8},{10,9... | collective-permute-start | bytes 393224 | tf_op jit(solution)/shard_map/ppermute | solution.py:375
  62.8 0.0 collective-permute-done.19.refs_3_
  62.8 0.0 collective-permute-done.18.refs_2_
  62.8 0.0 collective-permute-done.17.refs_1_
  62.8 0.1 shard_map.64.rest_0_
  62.9 0.1 collective-permute-start.22
  63.0 0.8 %collective-permute-start.21 = (f32[24,128]{1,0:T(8,128)S(1)}, f32[24,128]{1,0:T(8,128)S(1)}, u32[]{:S(2)}, u32[]{:S(2)}) collective-permute-start(f32[24,128]{1,0:T(8,128)S(1)} %shard_map.64.rest_0_), channel_id=1, source_target_pairs={{0,4},{1,5},{2,6},{3,7},{4,0},{5,1},{6,2},{7,3},{8,12},{9,13},{10,... | collective-permute-start | bytes 36872 | tf_op jit(solution)/shard_map/ppermute | solution.py:401
  63.8 3.5 %collective-permute-start.20 = (f32[24,128]{1,0:T(8,128)S(1)}, f32[24,128]{1,0:T(8,128)S(1)}, u32[]{:S(2)}, u32[]{:S(2)}) collective-permute-start(f32[24,128]{1,0:T(8,128)S(1)} %shard_map.64.rest_0_), channel_id=1, source_target_pairs={{0,2},{1,3},{2,0},{3,1},{4,6},{5,7},{6,4},{7,5},{8,10},{9,11},{10,... | collective-permute-start | bytes 36872 | tf_op jit(solution)/shard_map/ppermute | solution.py:401
  67.3 1.2 %collective-permute-done.22.rest_3_ = f32[24,128]{1,0:T(8,128)S(1)} collective-permute-done((f32[24,128]{1,0:T(8,128)S(1)}, f32[24,128]{1,0:T(8,128)S(1)}, u32[]{:S(2)}, u32[]{:S(2)}) %collective-permute-start.22) | collective-permute-done | bytes 12320 | tf_op jit(solution)/shard_map/ppermute | solution.py:401
  68.6 0.0 collective-permute-done.21.rest_2_
  68.6 0.4 collective-permute-done.20.rest_1_
  69.0 0.0 collective-permute-done.14.got_up
  69.0 0.0 collective-permute-done.15.got_right
  69.0 1.6 %shard_map.65 = (f32[512,128]{1,0:T(8,128)}, f32[512,128]{1,0:T(8,128)}) custom-call(s32[9]{0:T(128)S(1)} %stack.36.info, f32[1024,128]{1,0:T(8,128)S(1)} %get-tuple-element.27.u0, f32[1024,128]{1,0:T(8,128)S(1)} %get-tuple-element.32.u1, f32[1024,128]{1,0:T(8,128)S(1)} %get-tuple-element.37.u2, f32[1024,128]{1,0:T(8,128)S(1)} %get-tuple-element.43.u3, ...), custom_call_target="tpu_custom_call" | custom-call | tf_op jit(solution)/shard_map/pallas_call | solution.py:429
  (8 shorter events, 0.1 us)
Async XLA Ops:
  1.6 14.0 %collective-permute-start.1 = (f32[256,128]{1,0:T(8,128)S(1)}, f32[256,128]{1,0:T(8,128)S(1)}, u32[]{:S(2)}, u32[]{:S(2)}) collective-permute-start(f32[256,128]{1,0:T(8,128)S(1)} %get-tuple-element.50.right), channel_id=1, source_target_pairs={{0,1},{1,2},{2,3},{3,4},{4,5},{5,6},{6,7},{7,0},{8,9},{9,10},{10,1... | collective-permute-start | bytes 393224 | tf_op jit(solution)/shard_map/ppermute | solution.py:375
  4.6 10.9 %collective-permute-start = (f32[256,128]{1,0:T(8,128)S(1)}, f32[256,128]{1,0:T(8,128)S(1)}, u32[]{:S(2)}, u32[]{:S(2)}) collective-permute-start(f32[256,128]{1,0:T(8,128)S(1)} %get-tuple-element.51.up), channel_id=1, source_target_pairs={{0,8},{8,16},{16,24},{1,9},{9,17},{17,25},{2,10},{10,18},{18,26},{... | collective-permute-start | bytes 393224 | tf_op jit(solution)/shard_map/ppermute | solution.py:375
  17.4 12.2 %collective-permute-start.4 = (f32[280,128]{1,0:T(8,128)S(1)}, f32[280,128]{1,0:T(8,128)S(1)}, u32[]{:S(2)}, u32[]{:S(2)}) collective-permute-start(f32[280,128]{1,0:T(8,128)S(1)} %get-tuple-element.30.yc.rest_2_), channel_id=1, source_target_pairs={{0,1},{1,0},{2,3},{3,2},{4,5},{5,4},{6,7},{7,6},{8,9},{9,8},{10,11... | collective-permute-start | bytes 430088 | tf_op jit(solution)/shard_map/ppermute | solution.py:385
  19.0 10.6 %collective-permute-start.5 = (f32[272,128]{1,0:T(8,128)S(1)}, f32[272,128]{1,0:T(8,128)S(1)}, u32[]{:S(2)}, u32[]{:S(2)}) collective-permute-start(f32[272,128]{1,0:T(8,128)S(1)} %get-tuple-element.31.yd.rest_3_), channel_id=1, source_target_pairs={{1,2},{2,1},{3,4},{4,3},{5,6},{6,5},{7,0},{0,7},{9,10},{10,9},{11,... | collective-permute-start | bytes 417800 | tf_op jit(solution)/shard_map/ppermute | solution.py:385
  22.5 7.1 %collective-permute-start.2 = (f32[264,128]{1,0:T(8,128)S(1)}, f32[264,128]{1,0:T(8,128)S(1)}, u32[]{:S(2)}, u32[]{:S(2)}) collective-permute-start(f32[264,128]{1,0:T(8,128)S(1)} %get-tuple-element.28.ya.rest_0_), channel_id=1, source_target_pairs={{0,8},{8,0},{16,24},{24,16},{1,9},{9,1},{17,25},{25,17},{2,10},{10... | collective-permute-start | bytes 405512 | tf_op jit(solution)/shard_map/ppermute | solution.py:385
  24.0 5.6 %collective-permute-start.3 = (f32[256,128]{1,0:T(8,128)S(1)}, f32[256,128]{1,0:T(8,128)S(1)}, u32[]{:S(2)}, u32[]{:S(2)}) collective-permute-start(f32[256,128]{1,0:T(8,128)S(1)} %get-tuple-element.29.yb.rest_1_), channel_id=1, source_target_pairs={{8,16},{16,8},{24,0},{0,24},{9,17},{17,9},{25,1},{1,25},{10,18},{1... | collective-permute-start | bytes 393224 | tf_op jit(solution)/shard_map/ppermute | solution.py:385
  31.5 8.8 %collective-permute-start.8 = (f32[280,128]{1,0:T(8,128)S(1)}, f32[280,128]{1,0:T(8,128)S(1)}, u32[]{:S(2)}, u32[]{:S(2)}) collective-permute-start(f32[280,128]{1,0:T(8,128)S(1)} %get-tuple-element.35.yc.rest_6_), channel_id=1, source_target_pairs={{0,1},{1,0},{2,3},{3,2},{4,5},{5,4},{6,7},{7,6},{8,9},{9,8},{10,11... | collective-permute-start | bytes 430088 | tf_op jit(solution)/shard_map/ppermute | solution.py:385
  31.5 8.6 %collective-permute-start.9 = (f32[272,128]{1,0:T(8,128)S(1)}, f32[272,128]{1,0:T(8,128)S(1)}, u32[]{:S(2)}, u32[]{:S(2)}) collective-permute-start(f32[272,128]{1,0:T(8,128)S(1)} %get-tuple-element.36.yd.rest_7_), channel_id=1, source_target_pairs={{1,2},{2,1},{3,4},{4,3},{5,6},{6,5},{7,0},{0,7},{9,10},{10,9},{11,... | collective-permute-start | bytes 417800 | tf_op jit(solution)/shard_map/ppermute | solution.py:385
  33.4 5.2 %collective-permute-start.6 = (f32[264,128]{1,0:T(8,128)S(1)}, f32[264,128]{1,0:T(8,128)S(1)}, u32[]{:S(2)}, u32[]{:S(2)}) collective-permute-start(f32[264,128]{1,0:T(8,128)S(1)} %get-tuple-element.33.ya.rest_4_), channel_id=1, source_target_pairs={{0,8},{8,0},{16,24},{24,16},{1,9},{9,1},{17,25},{25,17},{2,10},{10... | collective-permute-start | bytes 405512 | tf_op jit(solution)/shard_map/ppermute | solution.py:385
  33.4 5.2 %collective-permute-start.7 = (f32[256,128]{1,0:T(8,128)S(1)}, f32[256,128]{1,0:T(8,128)S(1)}, u32[]{:S(2)}, u32[]{:S(2)}) collective-permute-start(f32[256,128]{1,0:T(8,128)S(1)} %get-tuple-element.34.yb.rest_5_), channel_id=1, source_target_pairs={{8,16},{16,8},{24,0},{0,24},{9,17},{17,9},{25,1},{1,25},{10,18},{1... | collective-permute-start | bytes 393224 | tf_op jit(solution)/shard_map/ppermute | solution.py:385
  42.7 8.2 %collective-permute-start.12 = (f32[280,128]{1,0:T(8,128)S(1)}, f32[280,128]{1,0:T(8,128)S(1)}, u32[]{:S(2)}, u32[]{:S(2)}) collective-permute-start(f32[280,128]{1,0:T(8,128)S(1)} %get-tuple-element.40.yc), channel_id=1, source_target_pairs={{0,1},{1,0},{2,3},{3,2},{4,5},{5,4},{6,7},{7,6},{8,9},{9,8},{10,11... | collective-permute-start | bytes 430088 | tf_op jit(solution)/shard_map/ppermute | solution.py:385
  43.0 7.8 %collective-permute-start.13 = (f32[272,128]{1,0:T(8,128)S(1)}, f32[272,128]{1,0:T(8,128)S(1)}, u32[]{:S(2)}, u32[]{:S(2)}) collective-permute-start(f32[272,128]{1,0:T(8,128)S(1)} %get-tuple-element.41.yd), channel_id=1, source_target_pairs={{1,2},{2,1},{3,4},{4,3},{5,6},{6,5},{7,0},{0,7},{9,10},{10,9},{11,... | collective-permute-start | bytes 417800 | tf_op jit(solution)/shard_map/ppermute | solution.py:385
  45.0 5.2 %collective-permute-start.10 = (f32[264,128]{1,0:T(8,128)S(1)}, f32[264,128]{1,0:T(8,128)S(1)}, u32[]{:S(2)}, u32[]{:S(2)}) collective-permute-start(f32[264,128]{1,0:T(8,128)S(1)} %get-tuple-element.38.ya), channel_id=1, source_target_pairs={{0,8},{8,0},{16,24},{24,16},{1,9},{9,1},{17,25},{25,17},{2,10},{10... | collective-permute-start | bytes 405512 | tf_op jit(solution)/shard_map/ppermute | solution.py:385
  45.0 5.2 %collective-permute-start.11 = (f32[256,128]{1,0:T(8,128)S(1)}, f32[256,128]{1,0:T(8,128)S(1)}, u32[]{:S(2)}, u32[]{:S(2)}) collective-permute-start(f32[256,128]{1,0:T(8,128)S(1)} %get-tuple-element.39.yb), channel_id=1, source_target_pairs={{8,16},{16,8},{24,0},{0,24},{9,17},{17,9},{25,1},{1,25},{10,18},{1... | collective-permute-start | bytes 393224 | tf_op jit(solution)/shard_map/ppermute | solution.py:385
  54.0 1.2 %collective-permute-start.16 = (f32[24,128]{1,0:T(8,128)S(1)}, f32[24,128]{1,0:T(8,128)S(1)}, u32[]{:S(2)}, u32[]{:S(2)}) collective-permute-start(f32[24,128]{1,0:T(8,128)S(1)} %get-tuple-element.47.refs_0_), channel_id=1, source_target_pairs={{0,8},{1,9},{2,10},{3,11},{4,12},{5,13},{6,14},{7,15},{8,0},{9,1},... | collective-permute-start | bytes 36872 | tf_op jit(solution)/shard_map/ppermute | solution.py:401
  55.3 7.4 %collective-permute-start.19 = (f32[24,128]{1,0:T(8,128)S(1)}, f32[24,128]{1,0:T(8,128)S(1)}, u32[]{:S(2)}, u32[]{:S(2)}) collective-permute-start(f32[24,128]{1,0:T(8,128)S(1)} %shard_map.63.refs_0_), channel_id=1, source_target_pairs={{0,17},{1,16},{2,19},{3,18},{4,21},{5,20},{6,23},{7,22},{8,25},{9,... | collective-permute-start | bytes 36872 | tf_op jit(solution)/shard_map/ppermute | solution.py:401
  55.9 6.8 %collective-permute-start.18 = (f32[24,128]{1,0:T(8,128)S(1)}, f32[24,128]{1,0:T(8,128)S(1)}, u32[]{:S(2)}, u32[]{:S(2)}) collective-permute-start(f32[24,128]{1,0:T(8,128)S(1)} %shard_map.63.refs_0_), channel_id=1, source_target_pairs={{0,1},{1,0},{2,3},{3,2},{4,5},{5,4},{6,7},{7,6},{8,9},{9,8},{10,11... | collective-permute-start | bytes 36872 | tf_op jit(solution)/shard_map/ppermute | solution.py:401
  57.3 5.5 %collective-permute-start.17 = (f32[24,128]{1,0:T(8,128)S(1)}, f32[24,128]{1,0:T(8,128)S(1)}, u32[]{:S(2)}, u32[]{:S(2)}) collective-permute-start(f32[24,128]{1,0:T(8,128)S(1)} %shard_map.63.refs_0_), channel_id=1, source_target_pairs={{0,16},{1,17},{2,18},{3,19},{4,20},{5,21},{6,22},{7,23},{8,24},{9,... | collective-permute-start | bytes 36872 | tf_op jit(solution)/shard_map/ppermute | solution.py:401
  58.9 10.1 %collective-permute-start.14 = (f32[256,128]{1,0:T(8,128)S(1)}, f32[256,128]{1,0:T(8,128)S(1)}, u32[]{:S(2)}, u32[]{:S(2)}) collective-permute-start(f32[256,128]{1,0:T(8,128)S(1)} %get-tuple-element.45), channel_id=1, source_target_pairs={{8,0},{16,8},{24,16},{9,1},{17,9},{25,17},{10,2},{18,10},{26,18},{... | collective-permute-start | bytes 393224 | tf_op jit(solution)/shard_map/ppermute | solution.py:375
  60.2 8.8 %collective-permute-start.15 = (f32[256,128]{1,0:T(8,128)S(1)}, f32[256,128]{1,0:T(8,128)S(1)}, u32[]{:S(2)}, u32[]{:S(2)}) collective-permute-start(f32[256,128]{1,0:T(8,128)S(1)} %get-tuple-element.46), channel_id=1, source_target_pairs={{0,7},{1,0},{2,1},{3,2},{4,3},{5,4},{6,5},{7,6},{8,15},{9,8},{10,9... | collective-permute-start | bytes 393224 | tf_op jit(solution)/shard_map/ppermute | solution.py:375
  62.9 5.7 %collective-permute-start.22 = (f32[24,128]{1,0:T(8,128)S(1)}, f32[24,128]{1,0:T(8,128)S(1)}, u32[]{:S(2)}, u32[]{:S(2)}) collective-permute-start(f32[24,128]{1,0:T(8,128)S(1)} %shard_map.64.rest_0_), channel_id=1, source_target_pairs={{0,6},{1,7},{2,4},{3,5},{4,2},{5,3},{6,0},{7,1},{8,14},{9,15},{10,... | collective-permute-start | bytes 36872 | tf_op jit(solution)/shard_map/ppermute | solution.py:401
  63.0 5.5 %collective-permute-start.21 = (f32[24,128]{1,0:T(8,128)S(1)}, f32[24,128]{1,0:T(8,128)S(1)}, u32[]{:S(2)}, u32[]{:S(2)}) collective-permute-start(f32[24,128]{1,0:T(8,128)S(1)} %shard_map.64.rest_0_), channel_id=1, source_target_pairs={{0,4},{1,5},{2,6},{3,7},{4,0},{5,1},{6,2},{7,3},{8,12},{9,13},{10,... | collective-permute-start | bytes 36872 | tf_op jit(solution)/shard_map/ppermute | solution.py:401
  63.8 5.2 %collective-permute-start.20 = (f32[24,128]{1,0:T(8,128)S(1)}, f32[24,128]{1,0:T(8,128)S(1)}, u32[]{:S(2)}, u32[]{:S(2)}) collective-permute-start(f32[24,128]{1,0:T(8,128)S(1)} %shard_map.64.rest_0_), channel_id=1, source_target_pairs={{0,2},{1,3},{2,0},{3,1},{4,6},{5,7},{6,4},{7,5},{8,10},{9,11},{10,... | collective-permute-start | bytes 36872 | tf_op jit(solution)/shard_map/ppermute | solution.py:401

commit v2 on v1

--- a/solution.py
+++ b/solution.py
@@ -8,7 +8,7 @@
 from jax.sharding import PartitionSpec as P
 
 ITERS = 4
-SLOT, KEEP, ODD = 0, 4, 7
+SLOT, KEEP, ODD = 0, 4, 8
 PADS = (8, 0, 24, 16)
 PAIRS = [(i, j) for i in range(4) for j in range(i, 4)]
 CENTER, NODE = 20, 24
@@ -44,6 +44,7 @@
     def prepare(k):
         for copy in fetch(k):
             copy.wait()
+        begin(k + 2)
         high, low = halves(w_buf[k * face : (k + 1) * face, :])
         here, there = left.at[k % 2], right.at[k % 2]
         there[0:face, :] = high
@@ -72,15 +73,19 @@
             else:
                 total[rows, cols] += part
 
-    for k in range(4):
-        for copy in fetch(k):
-            copy.start()
+    def begin(k):
+        if k < 4:
+            for copy in fetch(k):
+                copy.start()
+
+    begin(0)
+    begin(1)
     pattern_copy.wait()
     prepare(0)
     for k in range(4):
+        multiply(k)
         if k < 3:
             prepare(k + 1)
-        multiply(k)
 
     def put(i, j, block):
         def at(k):
@@ -176,15 +181,17 @@
             out[face:, :] = jnp.zeros((out.shape[0] - face, out.shape[1]), F32)
 
 
-def first_kernel(info, below, beside, up, right, g_ref, u_ref, a, b, c, d):
-    face = up.shape[0]
-    own_up = jnp.where(info[KEEP + 2] != 0, up[...], 0.0)
-    own_right = right[...]
+def first_kernel(info, below, beside, rhs, g_ref, u_ref, a, b, c, d):
+    face = rhs.shape[0] // 2
+    own_up = jnp.where(info[KEEP + 2] != 0, rhs[0:face, :], 0.0)
+    own_right = rhs[face:, :]
+    minus_below = jnp.where(info[KEEP + 3] != 0, -below[0:face, :], 0.0)
+    minus_beside = -beside[face:, :]
     odd_floor, odd_facade = info[ODD] != 0, info[ODD + 1] != 0
-    u_ref[0:face, :] = jnp.where(odd_floor, -below[...], own_up)
-    u_ref[face : 2 * face, :] = jnp.where(odd_floor, own_up, -below[...])
-    u_ref[2 * face : 3 * face, :] = jnp.where(odd_facade, -beside[...], own_right)
-    u_ref[3 * face :, :] = jnp.where(odd_facade, own_right, -beside[...])
+    u_ref[0:face, :] = jnp.where(odd_floor, minus_below, own_up)
+    u_ref[face : 2 * face, :] = jnp.where(odd_floor, own_up, minus_below)
+    u_ref[2 * face : 3 * face, :] = jnp.where(odd_facade, minus_beside, own_right)
+    u_ref[3 * face :, :] = jnp.where(odd_facade, own_right, minus_beside)
     hand_out(product(g_ref, u_ref[...]), (a, b, c, d))
 
 
@@ -448,11 +455,11 @@
     has_above = (floor_pos < floors - 1).astype(jnp.int32)
     keep_a = jnp.where(odd_floor == 0, has_above, has_below)
     keep_b = jnp.where(odd_floor == 0, has_below, has_above)
-    flags = [1 - odd_floor, odd_floor, 3 - odd_facade, 2 + odd_facade, keep_a, keep_b, has_above, odd_floor, odd_facade]
+    flags = [1 - odd_floor, odd_floor, 3 - odd_facade, 2 + odd_facade, keep_a, keep_b, has_above, has_below, odd_floor, odd_facade]
     info = jnp.stack(flags).astype(jnp.int32)
-    up, right = interface_rhs[0, 0, 0], interface_rhs[0, 0, 1]
-    beside = upward(right, "facade", 1, True)
-    below = upward(up, "floor", 1, False)
+    rhs = interface_rhs.reshape(2 * face, cases)
+    beside = upward(rhs, "facade", 1, True)
+    below = upward(rhs, "floor", 1, True)
     operator, center = build_operator(info, inverse_factor[0, 0], near_coupling[0, 0], near_pattern[0, 0], cases)
 
     def shaped(*dims):
@@ -461,7 +468,7 @@
     whole, part, node, owned = shaped(size, cases), shaped(face, cases), shaped(NODE, cases), shaped(2 * face, cases)
     sent = [shaped(face + rows, cases) for rows in PADS]
 
-    u0, *y0 = call(first_kernel, [whole, *sent], [], 1, info, below, beside, up, right, operator)
+    u0, *y0 = call(first_kernel, [whole, *sent], [], 1, info, below, beside, rhs, operator)
     u1, *y1 = call(functools.partial(next_kernel, False), [whole, *sent], [], 1, info, *y0, *exchanged(*y0), operator)
     u2, *y2 = call(functools.partial(next_kernel, True), [whole, *sent], [], 1, info, *y1, *exchanged(*y1), operator)
     u3, y_down, y_left, y_own, total = call(
@@ -472,7 +479,7 @@
         info, *y2, *exchanged(*y2), u0, u1, u2, *y0, *y1, center, operator,
     )
     got_right = upward(y_left, "facade", -1, True)
-    got_up = upward(y_down, "floor", -1, False)
+    got_up = upward(y_down, "floor", -1, True)
     *stages, before, last = sum_stages()
     for stage in stages + [before]:
         (total,) = call(merge_kernel, [node], [], 0, *stage_parts(total, stage), flops=MERGE_FLOPS if stage is before else 0)

time: 70.9 us -> 66.8 us (0.942)
  waiting for transfers between devices: 19.4 us -> 17.9 us
  starting transfers between devices: 29.1 us -> 28.1 us
  local copies, waits for them, and re-layouts: 1.07 us -> 0.09 us
    ppermute x4, starting transfers between devices: 8.33 us -> 5.34 us  [upward(): return lax.ppermute(value, axis, pairs)]
    ppermute x12, waiting for transfers between devices: 16.6 us -> 13.9 us  [swapped(): return lax.ppermute(value, axis, pairs)]
    ppermute x12, starting transfers between devices: 12.6 us -> 14.5 us  [swapped(): return lax.ppermute(value, axis, pairs)]
    squeeze x1 -> x0, local copies, waits for them, and re-layouts: 0.99 us -> none  [local(): up, right = (interface_rhs[0, 0, 0], interface_rhs[0, 0, 1])]
  transfers between devices with their start and end apart: 23 -> 23, of which waited for: 9 -> 12; matrix products, arithmetic and copies ran while one was open for 0% -> 0% of each run, Pallas kernels for 13% -> 14%
where the time goes in v2:
time: 66.8 us; the launch traced here: 66.6 us
  starting transfers between devices  28.1 us (42%)
  Pallas kernels  19.9 us (30%)
  waiting for transfers between devices  17.9 us (27%)
  between operations  0.71 us (1%)
    ppermute x12, starting transfers between devices, swapped(): return lax.ppermute(value, axis, pairs)  14.5 us
    ppermute x12, waiting for transfers between devices, swapped(): return lax.ppermute(value, axis, pairs)  13.9 us
    pallas_call x7, Pallas kernels, call(): pl.pallas_call(kernel, in_specs=[pl.BlockSpec(memory_space=pltpu.SMEM)] *...  11 us
    pallas_call x1, Pallas kernels, build_operator(): pl.pallas_call(operator_kernel, in_specs=[pl.BlockSpec(memory_space=pltpu...  8.91 us
    ppermute x7, starting transfers between devices, flipped(): return lax.ppermute(value, AXES, pairs)  8.22 us
    ppermute x4, starting transfers between devices, upward(): return lax.ppermute(value, axis, pairs)  5.34 us
    ppermute x7, waiting for transfers between devices, flipped(): return lax.ppermute(value, AXES, pairs)  3.39 us
  transfers between devices with their start and end apart: 23, of which 12 were waited for; matrix products, arithmetic and copies ran while one was open for 0% of the time, Pallas kernels for 14%

profile of v2, /device:TPU:0, one launch (start us, length us, event | category | flops | bytes accessed | tf_op | source)
XLA Modules:
  0.0 66.6 jit_solution(1117671902242996914)
XLA Ops:
  0.6 3.0 %collective-permute-start.1 = (f32[512,128]{1,0:T(8,128)}, f32[512,128]{1,0:T(8,128)S(1)}, u32[]{:S(2)}, u32[]{:S(2)}) collective-permute-start(f32[512,128]{1,0:T(8,128)} %bitcast.15), channel_id=1, source_target_pairs={{0,1},{1,2},{2,3},{3,4},{4,5},{5,6},{6,7},{7,0},{8,9},{9,10},{10,1... | collective-permute-start | bytes 786440 | tf_op jit(solution)/shard_map/ppermute | solution.py:382
  3.7 0.0 collective-permute-start
  3.7 0.1 stack.40.info
  3.7 8.9 %operator.1 = (bf16[1024,2048]{1,0:T(8,128)(2,1)S(1)}, f32[8,128]{1,0:T(8,128)S(1)}) custom-call(s32[10]{0:T(128)S(1)} %stack.40.info, s32[8,8]{1,0:T(8,128)} %bitcast.20, f32[1024,1024]{1,0:T(8,128)} %bitcast.18, bf16[1024,1024]{1,0:T(8,128)(2,1)} %bitcast.19), custom_call_target="tpu_custom_call" | custom-call | tf_op jit(solution)/shard_map/operator/pallas_call | solution.py:116
  12.7 0.6 collective-permute-done.1.beside
  13.2 1.8 %shard_map.59 = (f32[1024,128]{1,0:T(8,128)S(1)}, f32[264,128]{1,0:T(8,128)S(1)}, f32[256,128]{1,0:T(8,128)S(1)}, f32[280,128]{1,0:T(8,128)S(1)}, f32[272,128]{1,0:T(8,128)S(1)}) custom-call(s32[10]{0:T(128)S(1)} %stack.40.info, f32[512,128]{1,0:T(8,128)S(1)} %collective-permute-done.below, f32[512,128]{1,0:T(8,128)S(1)} %collective-permute-done.1.beside, ...), custom_call_target="tpu_custom_call" | custom-call | tf_op jit(solution)/shard_map/pallas_call | solution.py:436
  15.0 1.1 %collective-permute-start.4 = (f32[280,128]{1,0:T(8,128)S(1)}, f32[280,128]{1,0:T(8,128)S(1)}, u32[]{:S(2)}, u32[]{:S(2)}) collective-permute-start(f32[280,128]{1,0:T(8,128)S(1)} %get-tuple-element.30.yc.rest_2_), channel_id=1, source_target_pairs={{0,1},{1,0},{2,3},{3,2},{4,5},{5,4},{6,7},{7,6},{8,9},{9,8},{10,11... | collective-permute-start | bytes 430088 | tf_op jit(solution)/shard_map/ppermute | solution.py:392
  16.1 3.5 %collective-permute-start.5 = (f32[272,128]{1,0:T(8,128)S(1)}, f32[272,128]{1,0:T(8,128)S(1)}, u32[]{:S(2)}, u32[]{:S(2)}) collective-permute-start(f32[272,128]{1,0:T(8,128)S(1)} %get-tuple-element.31.yd.rest_3_), channel_id=1, source_target_pairs={{1,2},{2,1},{3,4},{4,3},{5,6},{6,5},{7,0},{0,7},{9,10},{10,9},{11,... | collective-permute-start | bytes 417800 | tf_op jit(solution)/shard_map/ppermute | solution.py:392
  19.6 1.0 %collective-permute-start.2 = (f32[264,128]{1,0:T(8,128)S(1)}, f32[264,128]{1,0:T(8,128)S(1)}, u32[]{:S(2)}, u32[]{:S(2)}) collective-permute-start(f32[264,128]{1,0:T(8,128)S(1)} %get-tuple-element.28.ya.rest_0_), channel_id=1, source_target_pairs={{0,8},{8,0},{16,24},{24,16},{1,9},{9,1},{17,25},{25,17},{2,10},{10... | collective-permute-start | bytes 405512 | tf_op jit(solution)/shard_map/ppermute | solution.py:392
  20.7 0.6 collective-permute-start.3
  21.3 5.0 %collective-permute-done.3.rb = f32[256,128]{1,0:T(8,128)S(1)} collective-permute-done((f32[256,128]{1,0:T(8,128)S(1)}, f32[256,128]{1,0:T(8,128)S(1)}, u32[]{:S(2)}, u32[]{:S(2)}) %collective-permute-start.3) | collective-permute-done | bytes 131104 | tf_op jit(solution)/shard_map/ppermute | solution.py:392
  26.3 0.0 collective-permute-done.2.ra
  26.3 0.0 collective-permute-done.5.rd
  26.3 1.8 %shard_map.60 = (f32[1024,128]{1,0:T(8,128)S(1)}, f32[264,128]{1,0:T(8,128)S(1)}, f32[256,128]{1,0:T(8,128)S(1)}, f32[280,128]{1,0:T(8,128)S(1)}, f32[272,128]{1,0:T(8,128)S(1)}) custom-call(s32[10]{0:T(128)S(1)} %stack.40.info, f32[264,128]{1,0:T(8,128)S(1)} %get-tuple-element.28.ya.rest_0_, f32[256,128]{1,0:T(8,128)S(1)} %get-tuple-element.29.yb.rest_1_, ...), custom_call_target="tpu_custom_call" | custom-call | tf_op jit(solution)/shard_map/pallas_call | solution.py:436
  28.1 0.1 collective-permute-start.8
  28.2 2.4 %collective-permute-start.9 = (f32[272,128]{1,0:T(8,128)S(1)}, f32[272,128]{1,0:T(8,128)S(1)}, u32[]{:S(2)}, u32[]{:S(2)}) collective-permute-start(f32[272,128]{1,0:T(8,128)S(1)} %get-tuple-element.36.yd.rest_7_), channel_id=1, source_target_pairs={{1,2},{2,1},{3,4},{4,3},{5,6},{6,5},{7,0},{0,7},{9,10},{10,9},{11,... | collective-permute-start | bytes 417800 | tf_op jit(solution)/shard_map/ppermute | solution.py:392
  30.6 1.8 %collective-permute-start.7 = (f32[256,128]{1,0:T(8,128)S(1)}, f32[256,128]{1,0:T(8,128)S(1)}, u32[]{:S(2)}, u32[]{:S(2)}) collective-permute-start(f32[256,128]{1,0:T(8,128)S(1)} %get-tuple-element.34.yb.rest_5_), channel_id=1, source_target_pairs={{8,16},{16,8},{24,0},{0,24},{9,17},{17,9},{25,1},{1,25},{10,18},{1... | collective-permute-start | bytes 393224 | tf_op jit(solution)/shard_map/ppermute | solution.py:392
  32.4 3.5 %collective-permute-done.7.rb = f32[256,128]{1,0:T(8,128)S(1)} collective-permute-done((f32[256,128]{1,0:T(8,128)S(1)}, f32[256,128]{1,0:T(8,128)S(1)}, u32[]{:S(2)}, u32[]{:S(2)}) %collective-permute-start.7) | collective-permute-done | bytes 131104 | tf_op jit(solution)/shard_map/ppermute | solution.py:392
  35.9 0.0 collective-permute-done.6.ra
  35.9 0.9 %collective-permute-done.9.rd = f32[272,128]{1,0:T(8,128)S(1)} collective-permute-done((f32[272,128]{1,0:T(8,128)S(1)}, f32[272,128]{1,0:T(8,128)S(1)}, u32[]{:S(2)}, u32[]{:S(2)}) %collective-permute-start.9) | collective-permute-done | bytes 139296 | tf_op jit(solution)/shard_map/ppermute | solution.py:392
  36.7 0.2 collective-permute-done.8.rc
  36.9 2.4 %shard_map.61 = (f32[1024,128]{1,0:T(8,128)S(1)}, f32[264,128]{1,0:T(8,128)S(1)}, f32[256,128]{1,0:T(8,128)S(1)}, f32[280,128]{1,0:T(8,128)S(1)}, f32[272,128]{1,0:T(8,128)S(1)}) custom-call(s32[10]{0:T(128)S(1)} %stack.40.info, f32[264,128]{1,0:T(8,128)S(1)} %get-tuple-element.33.ya.rest_4_, f32[256,128]{1,0:T(8,128)S(1)} %get-tuple-element.34.yb.rest_5_, ...), custom_call_target="tpu_custom_call" | custom-call | tf_op jit(solution)/shard_map/pallas_call | solution.py:436
  39.3 0.3 collective-permute-start.12
  39.7 2.4 %collective-permute-start.13 = (f32[272,128]{1,0:T(8,128)S(1)}, f32[272,128]{1,0:T(8,128)S(1)}, u32[]{:S(2)}, u32[]{:S(2)}) collective-permute-start(f32[272,128]{1,0:T(8,128)S(1)} %get-tuple-element.41.yd), channel_id=1, source_target_pairs={{1,2},{2,1},{3,4},{4,3},{5,6},{6,5},{7,0},{0,7},{9,10},{10,9},{11,... | collective-permute-start | bytes 417800 | tf_op jit(solution)/shard_map/ppermute | solution.py:392
  42.1 0.0 collective-permute-start.10
  42.1 1.3 %collective-permute-start.11 = (f32[256,128]{1,0:T(8,128)S(1)}, f32[256,128]{1,0:T(8,128)S(1)}, u32[]{:S(2)}, u32[]{:S(2)}) collective-permute-start(f32[256,128]{1,0:T(8,128)S(1)} %get-tuple-element.39.yb), channel_id=1, source_target_pairs={{8,16},{16,8},{24,0},{0,24},{9,17},{17,9},{25,1},{1,25},{10,18},{1... | collective-permute-start | bytes 393224 | tf_op jit(solution)/shard_map/ppermute | solution.py:392
  43.4 3.9 %collective-permute-done.11.rb = f32[256,128]{1,0:T(8,128)S(1)} collective-permute-done((f32[256,128]{1,0:T(8,128)S(1)}, f32[256,128]{1,0:T(8,128)S(1)}, u32[]{:S(2)}, u32[]{:S(2)}) %collective-permute-start.11) | collective-permute-done | bytes 131104 | tf_op jit(solution)/shard_map/ppermute | solution.py:392
  47.2 0.0 collective-permute-done.10.ra
  47.2 0.3 collective-permute-done.13.rd
  47.5 0.2 collective-permute-done.12.rc
  47.7 3.2 %shard_map.62 = (f32[1024,128]{1,0:T(8,128)S(1)}, f32[256,128]{1,0:T(8,128)S(1)}, f32[256,128]{1,0:T(8,128)S(1)}, f32[512,128]{1,0:T(8,128)S(1)}, f32[24,128]{1,0:T(8,128)S(1)}) custom-call(s32[10]{0:T(128)S(1)} %stack.40.info, f32[264,128]{1,0:T(8,128)S(1)} %get-tuple-element.38.ya, f32[256,128]{1,0:T(8,128)S(1)} %get-tuple-element.39.yb, ...), custom_call_target="tpu_custom_call" | custom-call | tf_op jit(solution)/shard_map/pallas_call | solution.py:436
  50.9 0.2 collective-permute-start.16
  51.1 1.0 %collective-permute-done.16.refs_1_ = f32[24,128]{1,0:T(8,128)S(1)} collective-permute-done((f32[24,128]{1,0:T(8,128)S(1)}, f32[24,128]{1,0:T(8,128)S(1)}, u32[]{:S(2)}, u32[]{:S(2)}) %collective-permute-start.16) | collective-permute-done | bytes 12320 | tf_op jit(solution)/shard_map/ppermute | solution.py:408
  52.2 1.1 %collective-permute-start.19 = (f32[24,128]{1,0:T(8,128)S(1)}, f32[24,128]{1,0:T(8,128)S(1)}, u32[]{:S(2)}, u32[]{:S(2)}) collective-permute-start(f32[24,128]{1,0:T(8,128)S(1)} %shard_map.63.refs_0_), channel_id=1, source_target_pairs={{0,17},{1,16},{2,19},{3,18},{4,21},{5,20},{6,23},{7,22},{8,25},{9,... | collective-permute-start | bytes 36872 | tf_op jit(solution)/shard_map/ppermute | solution.py:408
  53.3 1.7 %collective-permute-start.18 = (f32[24,128]{1,0:T(8,128)S(1)}, f32[24,128]{1,0:T(8,128)S(1)}, u32[]{:S(2)}, u32[]{:S(2)}) collective-permute-start(f32[24,128]{1,0:T(8,128)S(1)} %shard_map.63.refs_0_), channel_id=1, source_target_pairs={{0,1},{1,0},{2,3},{3,2},{4,5},{5,4},{6,7},{7,6},{8,9},{9,8},{10,11... | collective-permute-start | bytes 36872 | tf_op jit(solution)/shard_map/ppermute | solution.py:408
  55.1 0.7 %collective-permute-start.17 = (f32[24,128]{1,0:T(8,128)S(1)}, f32[24,128]{1,0:T(8,128)S(1)}, u32[]{:S(2)}, u32[]{:S(2)}) collective-permute-start(f32[24,128]{1,0:T(8,128)S(1)} %shard_map.63.refs_0_), channel_id=1, source_target_pairs={{0,16},{1,17},{2,18},{3,19},{4,20},{5,21},{6,22},{7,23},{8,24},{9,... | collective-permute-start | bytes 36872 | tf_op jit(solution)/shard_map/ppermute | solution.py:408
  55.7 0.3 collective-permute-start.14
  56.0 2.1 %collective-permute-start.15 = (f32[256,128]{1,0:T(8,128)S(1)}, f32[256,128]{1,0:T(8,128)S(1)}, u32[]{:S(2)}, u32[]{:S(2)}) collective-permute-start(f32[256,128]{1,0:T(8,128)S(1)} %get-tuple-element.46), channel_id=1, source_target_pairs={{0,7},{1,0},{2,1},{3,2},{4,3},{5,4},{6,5},{7,6},{8,15},{9,8},{10,9... | collective-permute-start | bytes 393224 | tf_op jit(solution)/shard_map/ppermute | solution.py:382
  58.1 0.0 collective-permute-done.19.refs_3_
  58.1 0.0 collective-permute-done.18.refs_2_
  58.1 0.7 %collective-permute-done.17.refs_1_ = f32[24,128]{1,0:T(8,128)S(1)} collective-permute-done((f32[24,128]{1,0:T(8,128)S(1)}, f32[24,128]{1,0:T(8,128)S(1)}, u32[]{:S(2)}, u32[]{:S(2)}) %collective-permute-start.17) | collective-permute-done | bytes 12320 | tf_op jit(solution)/shard_map/ppermute | solution.py:408
  58.8 0.1 shard_map.64.rest_0_
  58.8 0.9 %collective-permute-start.22 = (f32[24,128]{1,0:T(8,128)S(1)}, f32[24,128]{1,0:T(8,128)S(1)}, u32[]{:S(2)}, u32[]{:S(2)}) collective-permute-start(f32[24,128]{1,0:T(8,128)S(1)} %shard_map.64.rest_0_), channel_id=1, source_target_pairs={{0,6},{1,7},{2,4},{3,5},{4,2},{5,3},{6,0},{7,1},{8,14},{9,15},{10,... | collective-permute-start | bytes 36872 | tf_op jit(solution)/shard_map/ppermute | solution.py:408
  59.8 0.4 collective-permute-start.21
  60.2 3.1 %collective-permute-start.20 = (f32[24,128]{1,0:T(8,128)S(1)}, f32[24,128]{1,0:T(8,128)S(1)}, u32[]{:S(2)}, u32[]{:S(2)}) collective-permute-start(f32[24,128]{1,0:T(8,128)S(1)} %shard_map.64.rest_0_), channel_id=1, source_target_pairs={{0,2},{1,3},{2,0},{3,1},{4,6},{5,7},{6,4},{7,5},{8,10},{9,11},{10,... | collective-permute-start | bytes 36872 | tf_op jit(solution)/shard_map/ppermute | solution.py:408
  63.3 1.2 %collective-permute-done.22.rest_3_ = f32[24,128]{1,0:T(8,128)S(1)} collective-permute-done((f32[24,128]{1,0:T(8,128)S(1)}, f32[24,128]{1,0:T(8,128)S(1)}, u32[]{:S(2)}, u32[]{:S(2)}) %collective-permute-start.22) | collective-permute-done | bytes 12320 | tf_op jit(solution)/shard_map/ppermute | solution.py:408
  64.5 0.5 collective-permute-done.20.rest_1_
  65.0 1.6 %shard_map.65 = (f32[512,128]{1,0:T(8,128)}, f32[512,128]{1,0:T(8,128)}) custom-call(s32[10]{0:T(128)S(1)} %stack.40.info, f32[1024,128]{1,0:T(8,128)S(1)} %get-tuple-element.27.u0, f32[1024,128]{1,0:T(8,128)S(1)} %get-tuple-element.32.u1, f32[1024,128]{1,0:T(8,128)S(1)} %get-tuple-element.37.u2, f32[1024,128]{1,0:T(8,128)S(1)} %get-tuple-element.43.u3, ...), custom_call_target="tpu_custom_call" | custom-call | tf_op jit(solution)/shard_map/pallas_call | solution.py:436
  (9 shorter events, 0.1 us)
Async XLA Ops:
  0.6 12.6 %copy-start = (f32[1,1,2,256,128]{4,3,2,1,0:T(8,128)S(1)}, f32[1,1,2,256,128]{4,3,2,1,0:T(8,128)}, u32[]{:S(2)}) copy-start(f32[1,1,2,256,128]{4,3,2,1,0:T(8,128)} %param.4) | copy-start | bytes 786436
  0.6 12.6 %collective-permute-start.1 = (f32[512,128]{1,0:T(8,128)}, f32[512,128]{1,0:T(8,128)S(1)}, u32[]{:S(2)}, u32[]{:S(2)}) collective-permute-start(f32[512,128]{1,0:T(8,128)} %bitcast.15), channel_id=1, source_target_pairs={{0,1},{1,2},{2,3},{3,4},{4,5},{5,6},{6,7},{7,0},{8,9},{9,10},{10,1... | collective-permute-start | bytes 786440 | tf_op jit(solution)/shard_map/ppermute | solution.py:382
  3.7 9.6 %collective-permute-start = (f32[512,128]{1,0:T(8,128)}, f32[512,128]{1,0:T(8,128)S(1)}, u32[]{:S(2)}, u32[]{:S(2)}) collective-permute-start(f32[512,128]{1,0:T(8,128)} %bitcast.16), channel_id=1, source_target_pairs={{0,8},{8,16},{16,24},{24,0},{1,9},{9,17},{17,25},{25,1},{2,10},{10... | collective-permute-start | bytes 786440 | tf_op jit(solution)/shard_map/ppermute | solution.py:382
  15.0 11.3 %collective-permute-start.4 = (f32[280,128]{1,0:T(8,128)S(1)}, f32[280,128]{1,0:T(8,128)S(1)}, u32[]{:S(2)}, u32[]{:S(2)}) collective-permute-start(f32[280,128]{1,0:T(8,128)S(1)} %get-tuple-element.30.yc.rest_2_), channel_id=1, source_target_pairs={{0,1},{1,0},{2,3},{3,2},{4,5},{5,4},{6,7},{7,6},{8,9},{9,8},{10,11... | collective-permute-start | bytes 430088 | tf_op jit(solution)/shard_map/ppermute | solution.py:392
  16.1 10.2 %collective-permute-start.5 = (f32[272,128]{1,0:T(8,128)S(1)}, f32[272,128]{1,0:T(8,128)S(1)}, u32[]{:S(2)}, u32[]{:S(2)}) collective-permute-start(f32[272,128]{1,0:T(8,128)S(1)} %get-tuple-element.31.yd.rest_3_), channel_id=1, source_target_pairs={{1,2},{2,1},{3,4},{4,3},{5,6},{6,5},{7,0},{0,7},{9,10},{10,9},{11,... | collective-permute-start | bytes 417800 | tf_op jit(solution)/shard_map/ppermute | solution.py:392
  19.6 6.6 %collective-permute-start.2 = (f32[264,128]{1,0:T(8,128)S(1)}, f32[264,128]{1,0:T(8,128)S(1)}, u32[]{:S(2)}, u32[]{:S(2)}) collective-permute-start(f32[264,128]{1,0:T(8,128)S(1)} %get-tuple-element.28.ya.rest_0_), channel_id=1, source_target_pairs={{0,8},{8,0},{16,24},{24,16},{1,9},{9,1},{17,25},{25,17},{2,10},{10... | collective-permute-start | bytes 405512 | tf_op jit(solution)/shard_map/ppermute | solution.py:392
  20.7 5.6 %collective-permute-start.3 = (f32[256,128]{1,0:T(8,128)S(1)}, f32[256,128]{1,0:T(8,128)S(1)}, u32[]{:S(2)}, u32[]{:S(2)}) collective-permute-start(f32[256,128]{1,0:T(8,128)S(1)} %get-tuple-element.29.yb.rest_1_), channel_id=1, source_target_pairs={{8,16},{16,8},{24,0},{0,24},{9,17},{17,9},{25,1},{1,25},{10,18},{1... | collective-permute-start | bytes 393224 | tf_op jit(solution)/shard_map/ppermute | solution.py:392
  28.1 8.8 %collective-permute-start.8 = (f32[280,128]{1,0:T(8,128)S(1)}, f32[280,128]{1,0:T(8,128)S(1)}, u32[]{:S(2)}, u32[]{:S(2)}) collective-permute-start(f32[280,128]{1,0:T(8,128)S(1)} %get-tuple-element.35.yc.rest_6_), channel_id=1, source_target_pairs={{0,1},{1,0},{2,3},{3,2},{4,5},{5,4},{6,7},{7,6},{8,9},{9,8},{10,11... | collective-permute-start | bytes 430088 | tf_op jit(solution)/shard_map/ppermute | solution.py:392
  28.2 8.6 %collective-permute-start.9 = (f32[272,128]{1,0:T(8,128)S(1)}, f32[272,128]{1,0:T(8,128)S(1)}, u32[]{:S(2)}, u32[]{:S(2)}) collective-permute-start(f32[272,128]{1,0:T(8,128)S(1)} %get-tuple-element.36.yd.rest_7_), channel_id=1, source_target_pairs={{1,2},{2,1},{3,4},{4,3},{5,6},{6,5},{7,0},{0,7},{9,10},{10,9},{11,... | collective-permute-start | bytes 417800 | tf_op jit(solution)/shard_map/ppermute | solution.py:392
  30.6 5.3 %collective-permute-start.6 = (f32[264,128]{1,0:T(8,128)S(1)}, f32[264,128]{1,0:T(8,128)S(1)}, u32[]{:S(2)}, u32[]{:S(2)}) collective-permute-start(f32[264,128]{1,0:T(8,128)S(1)} %get-tuple-element.33.ya.rest_4_), channel_id=1, source_target_pairs={{0,8},{8,0},{16,24},{24,16},{1,9},{9,1},{17,25},{25,17},{2,10},{10... | collective-permute-start | bytes 405512 | tf_op jit(solution)/shard_map/ppermute | solution.py:392
  30.6 5.3 %collective-permute-start.7 = (f32[256,128]{1,0:T(8,128)S(1)}, f32[256,128]{1,0:T(8,128)S(1)}, u32[]{:S(2)}, u32[]{:S(2)}) collective-permute-start(f32[256,128]{1,0:T(8,128)S(1)} %get-tuple-element.34.yb.rest_5_), channel_id=1, source_target_pairs={{8,16},{16,8},{24,0},{0,24},{9,17},{17,9},{25,1},{1,25},{10,18},{1... | collective-permute-start | bytes 393224 | tf_op jit(solution)/shard_map/ppermute | solution.py:392
  39.3 8.4 %collective-permute-start.12 = (f32[280,128]{1,0:T(8,128)S(1)}, f32[280,128]{1,0:T(8,128)S(1)}, u32[]{:S(2)}, u32[]{:S(2)}) collective-permute-start(f32[280,128]{1,0:T(8,128)S(1)} %get-tuple-element.40.yc), channel_id=1, source_target_pairs={{0,1},{1,0},{2,3},{3,2},{4,5},{5,4},{6,7},{7,6},{8,9},{9,8},{10,11... | collective-permute-start | bytes 430088 | tf_op jit(solution)/shard_map/ppermute | solution.py:392
  39.7 7.8 %collective-permute-start.13 = (f32[272,128]{1,0:T(8,128)S(1)}, f32[272,128]{1,0:T(8,128)S(1)}, u32[]{:S(2)}, u32[]{:S(2)}) collective-permute-start(f32[272,128]{1,0:T(8,128)S(1)} %get-tuple-element.41.yd), channel_id=1, source_target_pairs={{1,2},{2,1},{3,4},{4,3},{5,6},{6,5},{7,0},{0,7},{9,10},{10,9},{11,... | collective-permute-start | bytes 417800 | tf_op jit(solution)/shard_map/ppermute | solution.py:392
  42.1 5.2 %collective-permute-start.10 = (f32[264,128]{1,0:T(8,128)S(1)}, f32[264,128]{1,0:T(8,128)S(1)}, u32[]{:S(2)}, u32[]{:S(2)}) collective-permute-start(f32[264,128]{1,0:T(8,128)S(1)} %get-tuple-element.38.ya), channel_id=1, source_target_pairs={{0,8},{8,0},{16,24},{24,16},{1,9},{9,1},{17,25},{25,17},{2,10},{10... | collective-permute-start | bytes 405512 | tf_op jit(solution)/shard_map/ppermute | solution.py:392
  42.1 5.2 %collective-permute-start.11 = (f32[256,128]{1,0:T(8,128)S(1)}, f32[256,128]{1,0:T(8,128)S(1)}, u32[]{:S(2)}, u32[]{:S(2)}) collective-permute-start(f32[256,128]{1,0:T(8,128)S(1)} %get-tuple-element.39.yb), channel_id=1, source_target_pairs={{8,16},{16,8},{24,0},{0,24},{9,17},{17,9},{25,1},{1,25},{10,18},{1... | collective-permute-start | bytes 393224 | tf_op jit(solution)/shard_map/ppermute | solution.py:392
  50.9 1.2 %collective-permute-start.16 = (f32[24,128]{1,0:T(8,128)S(1)}, f32[24,128]{1,0:T(8,128)S(1)}, u32[]{:S(2)}, u32[]{:S(2)}) collective-permute-start(f32[24,128]{1,0:T(8,128)S(1)} %get-tuple-element.47.refs_0_), channel_id=1, source_target_pairs={{0,8},{1,9},{2,10},{3,11},{4,12},{5,13},{6,14},{7,15},{8,0},{9,1},... | collective-permute-start | bytes 36872 | tf_op jit(solution)/shard_map/ppermute | solution.py:408
  52.2 5.9 %collective-permute-start.19 = (f32[24,128]{1,0:T(8,128)S(1)}, f32[24,128]{1,0:T(8,128)S(1)}, u32[]{:S(2)}, u32[]{:S(2)}) collective-permute-start(f32[24,128]{1,0:T(8,128)S(1)} %shard_map.63.refs_0_), channel_id=1, source_target_pairs={{0,17},{1,16},{2,19},{3,18},{4,21},{5,20},{6,23},{7,22},{8,25},{9,... | collective-permute-start | bytes 36872 | tf_op jit(solution)/shard_map/ppermute | solution.py:408
  53.3 4.8 %collective-permute-start.18 = (f32[24,128]{1,0:T(8,128)S(1)}, f32[24,128]{1,0:T(8,128)S(1)}, u32[]{:S(2)}, u32[]{:S(2)}) collective-permute-start(f32[24,128]{1,0:T(8,128)S(1)} %shard_map.63.refs_0_), channel_id=1, source_target_pairs={{0,1},{1,0},{2,3},{3,2},{4,5},{5,4},{6,7},{7,6},{8,9},{9,8},{10,11... | collective-permute-start | bytes 36872 | tf_op jit(solution)/shard_map/ppermute | solution.py:408
  55.1 3.7 %collective-permute-start.17 = (f32[24,128]{1,0:T(8,128)S(1)}, f32[24,128]{1,0:T(8,128)S(1)}, u32[]{:S(2)}, u32[]{:S(2)}) collective-permute-start(f32[24,128]{1,0:T(8,128)S(1)} %shard_map.63.refs_0_), channel_id=1, source_target_pairs={{0,16},{1,17},{2,18},{3,19},{4,20},{5,21},{6,22},{7,23},{8,24},{9,... | collective-permute-start | bytes 36872 | tf_op jit(solution)/shard_map/ppermute | solution.py:408
  55.7 9.2 %collective-permute-start.14 = (f32[256,128]{1,0:T(8,128)S(1)}, f32[256,128]{1,0:T(8,128)S(1)}, u32[]{:S(2)}, u32[]{:S(2)}) collective-permute-start(f32[256,128]{1,0:T(8,128)S(1)} %get-tuple-element.45), channel_id=1, source_target_pairs={{0,24},{8,0},{16,8},{24,16},{1,25},{9,1},{17,9},{25,17},{2,26},{10... | collective-permute-start | bytes 393224 | tf_op jit(solution)/shard_map/ppermute | solution.py:382
  56.0 9.0 %collective-permute-start.15 = (f32[256,128]{1,0:T(8,128)S(1)}, f32[256,128]{1,0:T(8,128)S(1)}, u32[]{:S(2)}, u32[]{:S(2)}) collective-permute-start(f32[256,128]{1,0:T(8,128)S(1)} %get-tuple-element.46), channel_id=1, source_target_pairs={{0,7},{1,0},{2,1},{3,2},{4,3},{5,4},{6,5},{7,6},{8,15},{9,8},{10,9... | collective-permute-start | bytes 393224 | tf_op jit(solution)/shard_map/ppermute | solution.py:382
  58.8 5.6 %collective-permute-start.22 = (f32[24,128]{1,0:T(8,128)S(1)}, f32[24,128]{1,0:T(8,128)S(1)}, u32[]{:S(2)}, u32[]{:S(2)}) collective-permute-start(f32[24,128]{1,0:T(8,128)S(1)} %shard_map.64.rest_0_), channel_id=1, source_target_pairs={{0,6},{1,7},{2,4},{3,5},{4,2},{5,3},{6,0},{7,1},{8,14},{9,15},{10,... | collective-permute-start | bytes 36872 | tf_op jit(solution)/shard_map/ppermute | solution.py:408
  59.8 4.7 %collective-permute-start.21 = (f32[24,128]{1,0:T(8,128)S(1)}, f32[24,128]{1,0:T(8,128)S(1)}, u32[]{:S(2)}, u32[]{:S(2)}) collective-permute-start(f32[24,128]{1,0:T(8,128)S(1)} %shard_map.64.rest_0_), channel_id=1, source_target_pairs={{0,4},{1,5},{2,6},{3,7},{4,0},{5,1},{6,2},{7,3},{8,12},{9,13},{10,... | collective-permute-start | bytes 36872 | tf_op jit(solution)/shard_map/ppermute | solution.py:408
  60.2 4.8 %collective-permute-start.20 = (f32[24,128]{1,0:T(8,128)S(1)}, f32[24,128]{1,0:T(8,128)S(1)}, u32[]{:S(2)}, u32[]{:S(2)}) collective-permute-start(f32[24,128]{1,0:T(8,128)S(1)} %shard_map.64.rest_0_), channel_id=1, source_target_pairs={{0,2},{1,3},{2,0},{3,1},{4,6},{5,7},{6,4},{7,5},{8,10},{9,11},{10,... | collective-permute-start | bytes 36872 | tf_op jit(solution)/shard_map/ppermute | solution.py:408

commit v3 on v2

--- a/solution.py
+++ b/solution.py
@@ -321,6 +321,7 @@
     one = jnp.ones_like(rows[0][0:1, :])
     x, r, p = [], [one], [one]
     norm = inner[0, 0]
+    norms = [norm]
     for sweep in range(ITERS):
         step = norm / square(p, energy)
         x = plus(x, step, p)
@@ -330,7 +331,21 @@
             fresh = square(r, inner)
             p = plus(r, fresh / norm, p + [jnp.zeros_like(one)])
             norm = fresh
-    return x, r
+            norms.append(norm)
+    return x, r, norms
+
+
+def soundness(rows, norms, r):
+    inner = {}
+    for q, (i, j) in enumerate(PAIRS):
+        inner[i, j] = inner[j, i] = rows[q][0:1, :]
+    lengths = [
+        tree_any([float(BINOMIAL[k][i] * BINOMIAL[k][j]) * inner[i, j] for i in range(k + 1) for j in range(k + 1)])
+        for k in range(4)
+    ]
+    lengths.append(lengths[3] * (lengths[3] / lengths[2]))
+    terms = tree_any([r[k] * r[k] * lengths[k] for k in range(5)])
+    return jnp.where((terms <= GROWTH * norms[-1]) & (norms[-1] > 0.0), 1.0, 0.0)
 
 
 def powers(coefficients, scale):
@@ -358,10 +373,11 @@
 
 
 def final_kernel(info, u0, u1, u2, u3, yo_ref, got_up, got_right, *rest):
-    parts, (mult, resid) = rest[:-2], rest[-2:]
+    parts, (mult, resid, sound) = rest[:-3], rest[-3:]
     rows, middle = merged(parts)
     scale = 1.0 / middle
-    x, r = conjugate_coefficients(rows)
+    x, r, norms = conjugate_coefficients(rows)
+    sound[0, 0] = jnp.min(soundness(rows, norms, powers(r, jnp.ones_like(scale)))).astype(jnp.int32)
     x = [value * scale for value in powers(x, scale)]
     r = powers(r, scale)
     face = got_up.shape[0]
@@ -376,6 +392,11 @@
         resid[here, :] = r[0] * w[0] + r[1] * w[1] + r[2] * w[2] + r[3] * w[3] + r[4] * image
 
 
+def hand_on_kernel(mult_in, resid_in, mult, resid):
+    mult[...] = mult_in[...]
+    resid[...] = resid_in[...]
+
+
 def upward(value, axis, steps, wrap):
     count = lax.axis_size(axis)
     pairs = [(i, (i + steps) % count) for i in range(count) if wrap or 0 <= i + steps < count]
@@ -426,10 +447,49 @@
     if len(stage) == 1:
         return [value, flipped(value, *stage[0])]
     (f1, c1), (f2, c2) = stage
-    return [value, flipped(value, f1, c1), flipped(value, f2, c2), flipped(value, f1 ^ f2, c1 ^ c2)]
+    return [value, flipped(value, f1 ^ f2, c1 ^ c2), flipped(value, f2, c2), flipped(value, f1, c1)]
+
+
+def plain_iterations(rhs, factor, coupling, pattern, has_above):
+    face, cases = rhs.shape[0] // 2, rhs.shape[1]
+    size = 4 * face
+    block = size // pattern.shape[0]
+    expanded = jnp.repeat(jnp.repeat(pattern, block, axis=0), block, axis=1)
+    masked = jnp.where(expanded != 0, coupling, jnp.zeros_like(coupling))
+    top_keep = has_above.astype(F32)
+
+    def dot(x, y, contract):
+        return lax.dot_general(x, y, ((contract, (0,)), ((), ())), precision=lax.Precision.HIGHEST, preferred_element_type=F32)
+
+    def image_of(v):
+        up, right = v[:face], v[face:]
+        below, beside = upward(up, "floor", 1, False), upward(right, "facade", 1, True)
+        u = jnp.concatenate([-below, up, -beside, right], axis=0)
+        y = dot(factor, dot(factor, u, (1,)), (0,))
+        forward = dot(masked, u.astype(BF16), (1,)).astype(BF16)
+        y = (y + dot(masked, forward, (0,))).reshape(4, face, cases)
+        above, beyond = upward(y[0], "floor", -1, False), upward(y[2], "facade", -1, True)
+        return jnp.concatenate([(y[1] - above) * top_keep, y[3] - beyond], axis=0)
+
+    def inner(a, b):
+        return lax.psum(jnp.sum(a * b, axis=0), AXES)
+
+    def step(_, state):
+        mult, resid, direction, norm = state
+        image = image_of(direction)
+        length = norm / inner(direction, image)
+        mult = mult + length * direction
+        resid = resid - length * image
+        fresh = inner(resid, resid)
+        return mult, resid, resid + fresh / norm * direction, fresh
+
+    start = jnp.concatenate([rhs[:face] * top_keep, rhs[face:]], axis=0)
+    state = (jnp.zeros_like(start), start, start, inner(start, start))
+    return lax.fori_loop(0, ITERS, step, state)[:2]
 
 
 MERGE_FLOPS = 3000000000
+GROWTH = 1.0e6
 
 
 def call(kernel, outs, scratch, smem, *args, flops=0):
@@ -443,6 +503,16 @@
         compiler_params=params(16),
         cost_estimate=pl.CostEstimate(flops=flops, bytes_accessed=0, transcendentals=0) if flops else None,
     )(*args)
+
+
+def finish(outs, info, *args):
+    return pl.pallas_call(
+        final_kernel,
+        in_specs=[pl.BlockSpec(memory_space=pltpu.SMEM)] + [pl.BlockSpec(memory_space=pltpu.VMEM)] * len(args),
+        out_specs=[pl.BlockSpec(memory_space=pltpu.VMEM)] * 2 + [pl.BlockSpec(memory_space=pltpu.SMEM)],
+        out_shape=outs + [jax.ShapeDtypeStruct((1, 1), jnp.int32)],
+        compiler_params=params(16),
+    )(info, *args)
 
 
 def local(interface_rhs, inverse_factor, near_coupling, near_pattern):
@@ -483,7 +553,12 @@
     *stages, before, last = sum_stages()
     for stage in stages + [before]:
         (total,) = call(merge_kernel, [node], [], 0, *stage_parts(total, stage), flops=MERGE_FLOPS if stage is before else 0)
-    mult, resid = call(final_kernel, [owned, owned], [], 1, info, u0, u1, u2, u3, y_own, got_up, got_right, *stage_parts(total, last))
+    mult, resid, sound = finish([owned, owned], info, u0, u1, u2, u3, y_own, got_up, got_right, *stage_parts(total, last))
+    def one_by_one(state):
+        result = plain_iterations(rhs, inverse_factor[0, 0], near_coupling[0, 0], near_pattern[0, 0], has_above)
+        return (*call(hand_on_kernel, [owned, owned], [], 0, *result), jnp.int32(1))
+
+    mult, resid, _ = lax.while_loop(lambda state: state[2] == 0, one_by_one, (mult, resid, sound[0, 0]))
     shape = (1, 1, 2, face, cases)
     return mult.reshape(shape), resid.reshape(shape)
 

time: 66.8 us -> 67.6 us (1.012)
  local copies, waits for them, and re-layouts: 0.09 us -> 0.92 us
  waiting for transfers between devices: 17.9 us -> 17.2 us
  loops' own time: 0 us -> 0.68 us
    pallas_call x0 -> x1, Pallas kernels: none -> 1.73 us  [finish(): pl.pallas_call(final_kernel, in_specs=[pl.BlockSpec(memory_space=pltpu.SM...]
    pallas_call x7 -> x6, Pallas kernels: 11 us -> 9.49 us  [call(): pl.pallas_call(kernel, in_specs=[pl.BlockSpec(memory_space=pltpu.SMEM)] *...]
    ppermute x7, waiting for transfers between devices: 3.39 us -> 2.18 us  [flipped(): return lax.ppermute(value, AXES, pairs)]
    while x0 -> x1, local copies, waits for them, and re-layouts: none -> 0.83 us  [local(): lax.while_loop(lambda state: state[2] == 0, one_by_one, (mult, resid, sou...]
    another operation x0 -> x1, loops' own time: none -> 0.68 us  [local(): lax.while_loop(lambda state: state[2] == 0, one_by_one, (mult, resid, sou...]
  transfers between devices with their start and end apart: 23 -> 23, of which waited for: 12 -> 12; matrix products, arithmetic and copies ran while one was open for 0% -> 1% of each run, Pallas kernels for 14% -> 13%
where the time goes in v3:
time: 67.6 us; the launch traced here: 67.5 us
  starting transfers between devices  27.7 us (41%)
  Pallas kernels  20.1 us (30%)
  waiting for transfers between devices  17.2 us (25%)
  local copies, waits for them, and re-layouts  0.92 us (1%)
  between operations  0.9 us (1%)
  loops' own time  0.68 us (1%)
    ppermute x12, waiting for transfers between devices, swapped(): return lax.ppermute(value, axis, pairs)  14.4 us
    ppermute x12, starting transfers between devices, swapped(): return lax.ppermute(value, axis, pairs)  14.2 us
    pallas_call x6, Pallas kernels, call(): pl.pallas_call(kernel, in_specs=[pl.BlockSpec(memory_space=pltpu.SMEM)] *...  9.49 us
    pallas_call x1, Pallas kernels, build_operator(): pl.pallas_call(operator_kernel, in_specs=[pl.BlockSpec(memory_space=pltpu...  8.91 us
    ppermute x7, starting transfers between devices, flipped(): return lax.ppermute(value, AXES, pairs)  8.22 us
    ppermute x4, starting transfers between devices, upward(): return lax.ppermute(value, axis, pairs)  5.29 us
    ppermute x7, waiting for transfers between devices, flipped(): return lax.ppermute(value, AXES, pairs)  2.18 us
    pallas_call x1, Pallas kernels, finish(): pl.pallas_call(final_kernel, in_specs=[pl.BlockSpec(memory_space=pltpu.SM...  1.73 us
  transfers between devices with their start and end apart: 23, of which 12 were waited for; matrix products, arithmetic and copies ran while one was open for 1% of the time, Pallas kernels for 13%

profile of v3, /device:TPU:0, one launch (start us, length us, event | category | flops | bytes accessed | tf_op | source)
XLA Modules:
  0.0 67.5 jit_solution(11666685820069080865)
XLA Ops:
  0.6 0.5 collective-permute-start.4
  1.1 2.6 %collective-permute-start.5 = (f32[512,128]{1,0:T(8,128)}, f32[512,128]{1,0:T(8,128)S(1)}, u32[]{:S(2)}, u32[]{:S(2)}) collective-permute-start(f32[512,128]{1,0:T(8,128)} %bitcast.48), channel_id=1, source_target_pairs={{0,1},{1,2},{2,3},{3,4},{4,5},{5,6},{6,7},{7,0},{8,9},{9,10},{10,1... | collective-permute-start | bytes 786440 | tf_op jit(solution)/shard_map/ppermute | solution.py:403
  3.7 0.1 stack.40.info
  3.8 8.9 %operator.1 = (bf16[1024,2048]{1,0:T(8,128)(2,1)S(1)}, f32[8,128]{1,0:T(8,128)S(1)}) custom-call(s32[10]{0:T(128)S(1)} %stack.40.info, s32[8,8]{1,0:T(8,128)} %bitcast.57, f32[1024,1024]{1,0:T(8,128)} %bitcast.51, bf16[1024,1024]{1,0:T(8,128)(2,1)} %bitcast.55), custom_call_target="tpu_custom_call" | custom-call | tf_op jit(solution)/shard_map/operator/pallas_call | solution.py:116
  12.7 0.0 collective-permute-done.4.below
  12.7 0.5 collective-permute-done.5.beside
  13.3 1.8 %shard_map.59 = (f32[1024,128]{1,0:T(8,128)S(1)}, f32[264,128]{1,0:T(8,128)S(1)}, f32[256,128]{1,0:T(8,128)S(1)}, f32[280,128]{1,0:T(8,128)S(1)}, f32[272,128]{1,0:T(8,128)S(1)}) custom-call(s32[10]{0:T(128)S(1)} %stack.40.info, f32[512,128]{1,0:T(8,128)S(1)} %collective-permute-done.4.below, f32[512,128]{1,0:T(8,128)S(1)} %collective-permute-done.5.beside, ...), custom_call_target="tpu_custom_call" | custom-call | tf_op jit(solution)/shard_map/pallas_call | solution.py:496
  15.1 1.1 %collective-permute-start.8 = (f32[280,128]{1,0:T(8,128)S(1)}, f32[280,128]{1,0:T(8,128)S(1)}, u32[]{:S(2)}, u32[]{:S(2)}) collective-permute-start(f32[280,128]{1,0:T(8,128)S(1)} %get-tuple-element.137.yc.rest_2_), channel_id=1, source_target_pairs={{0,1},{1,0},{2,3},{3,2},{4,5},{5,4},{6,7},{7,6},{8,9},{9,8},{10,11... | collective-permute-start | bytes 430088 | tf_op jit(solution)/shard_map/ppermute | solution.py:413
  16.1 3.6 %collective-permute-start.9 = (f32[272,128]{1,0:T(8,128)S(1)}, f32[272,128]{1,0:T(8,128)S(1)}, u32[]{:S(2)}, u32[]{:S(2)}) collective-permute-start(f32[272,128]{1,0:T(8,128)S(1)} %get-tuple-element.138.yd.rest_3_), channel_id=1, source_target_pairs={{1,2},{2,1},{3,4},{4,3},{5,6},{6,5},{7,0},{0,7},{9,10},{10,9},{11,... | collective-permute-start | bytes 417800 | tf_op jit(solution)/shard_map/ppermute | solution.py:413
  19.7 0.7 %collective-permute-start.6 = (f32[264,128]{1,0:T(8,128)S(1)}, f32[264,128]{1,0:T(8,128)S(1)}, u32[]{:S(2)}, u32[]{:S(2)}) collective-permute-start(f32[264,128]{1,0:T(8,128)S(1)} %get-tuple-element.135.ya.rest_0_), channel_id=1, source_target_pairs={{0,8},{8,0},{16,24},{24,16},{1,9},{9,1},{17,25},{25,17},{2,10},{10... | collective-permute-start | bytes 405512 | tf_op jit(solution)/shard_map/ppermute | solution.py:413
  20.4 0.9 %collective-permute-start.7 = (f32[256,128]{1,0:T(8,128)S(1)}, f32[256,128]{1,0:T(8,128)S(1)}, u32[]{:S(2)}, u32[]{:S(2)}) collective-permute-start(f32[256,128]{1,0:T(8,128)S(1)} %get-tuple-element.136.yb.rest_1_), channel_id=1, source_target_pairs={{8,16},{16,8},{24,0},{0,24},{9,17},{17,9},{25,1},{1,25},{10,18},{1... | collective-permute-start | bytes 393224 | tf_op jit(solution)/shard_map/ppermute | solution.py:413
  21.3 4.7 %collective-permute-done.7.rb = f32[256,128]{1,0:T(8,128)S(1)} collective-permute-done((f32[256,128]{1,0:T(8,128)S(1)}, f32[256,128]{1,0:T(8,128)S(1)}, u32[]{:S(2)}, u32[]{:S(2)}) %collective-permute-start.7) | collective-permute-done | bytes 131104 | tf_op jit(solution)/shard_map/ppermute | solution.py:413
  26.0 0.0 collective-permute-done.8.rc
  26.0 1.8 %shard_map.60 = (f32[1024,128]{1,0:T(8,128)S(1)}, f32[264,128]{1,0:T(8,128)S(1)}, f32[256,128]{1,0:T(8,128)S(1)}, f32[280,128]{1,0:T(8,128)S(1)}, f32[272,128]{1,0:T(8,128)S(1)}) custom-call(s32[10]{0:T(128)S(1)} %stack.40.info, f32[264,128]{1,0:T(8,128)S(1)} %get-tuple-element.135.ya.rest_0_, f32[256,128]{1,0:T(8,128)S(1)} %get-tuple-element.136.yb.rest_1_, ...), custom_call_target="tpu_custom_call" | custom-call | tf_op jit(solution)/shard_map/pallas_call | solution.py:496
  27.8 0.1 collective-permute-start.12
  27.9 3.0 %collective-permute-start.13 = (f32[272,128]{1,0:T(8,128)S(1)}, f32[272,128]{1,0:T(8,128)S(1)}, u32[]{:S(2)}, u32[]{:S(2)}) collective-permute-start(f32[272,128]{1,0:T(8,128)S(1)} %get-tuple-element.143.yd.rest_7_), channel_id=1, source_target_pairs={{1,2},{2,1},{3,4},{4,3},{5,6},{6,5},{7,0},{0,7},{9,10},{10,9},{11,... | collective-permute-start | bytes 417800 | tf_op jit(solution)/shard_map/ppermute | solution.py:413
  30.9 0.0 collective-permute-start.10
  30.9 1.2 %collective-permute-start.11 = (f32[256,128]{1,0:T(8,128)S(1)}, f32[256,128]{1,0:T(8,128)S(1)}, u32[]{:S(2)}, u32[]{:S(2)}) collective-permute-start(f32[256,128]{1,0:T(8,128)S(1)} %get-tuple-element.141.yb.rest_5_), channel_id=1, source_target_pairs={{8,16},{16,8},{24,0},{0,24},{9,17},{17,9},{25,1},{1,25},{10,18},{1... | collective-permute-start | bytes 393224 | tf_op jit(solution)/shard_map/ppermute | solution.py:413
  32.1 3.9 %collective-permute-done.11.rb = f32[256,128]{1,0:T(8,128)S(1)} collective-permute-done((f32[256,128]{1,0:T(8,128)S(1)}, f32[256,128]{1,0:T(8,128)S(1)}, u32[]{:S(2)}, u32[]{:S(2)}) %collective-permute-start.11) | collective-permute-done | bytes 131104 | tf_op jit(solution)/shard_map/ppermute | solution.py:413
  36.0 0.0 collective-permute-done.10.ra
  36.0 0.4 collective-permute-done.13.rd
  36.5 0.2 collective-permute-done.12.rc
  36.7 2.4 %shard_map.61 = (f32[1024,128]{1,0:T(8,128)S(1)}, f32[264,128]{1,0:T(8,128)S(1)}, f32[256,128]{1,0:T(8,128)S(1)}, f32[280,128]{1,0:T(8,128)S(1)}, f32[272,128]{1,0:T(8,128)S(1)}) custom-call(s32[10]{0:T(128)S(1)} %stack.40.info, f32[264,128]{1,0:T(8,128)S(1)} %get-tuple-element.140.ya.rest_4_, f32[256,128]{1,0:T(8,128)S(1)} %get-tuple-element.141.yb.rest_5_, ...), custom_call_target="tpu_custom_call" | custom-call | tf_op jit(solution)/shard_map/pallas_call | solution.py:496
  39.0 0.3 collective-permute-start.16
  39.4 2.9 %collective-permute-start.17 = (f32[272,128]{1,0:T(8,128)S(1)}, f32[272,128]{1,0:T(8,128)S(1)}, u32[]{:S(2)}, u32[]{:S(2)}) collective-permute-start(f32[272,128]{1,0:T(8,128)S(1)} %get-tuple-element.148.yd), channel_id=1, source_target_pairs={{1,2},{2,1},{3,4},{4,3},{5,6},{6,5},{7,0},{0,7},{9,10},{10,9},{11,... | collective-permute-start | bytes 417800 | tf_op jit(solution)/shard_map/ppermute | solution.py:413
  42.3 0.0 collective-permute-start.14
  42.3 0.4 collective-permute-start.15
  42.7 4.7 %collective-permute-done.15.rb = f32[256,128]{1,0:T(8,128)S(1)} collective-permute-done((f32[256,128]{1,0:T(8,128)S(1)}, f32[256,128]{1,0:T(8,128)S(1)}, u32[]{:S(2)}, u32[]{:S(2)}) %collective-permute-start.15) | collective-permute-done | bytes 131104 | tf_op jit(solution)/shard_map/ppermute | solution.py:413
  47.4 0.3 collective-permute-done.17.rd
  47.7 0.2 collective-permute-done.16.rc
  47.9 3.4 %shard_map.62 = (f32[1024,128]{1,0:T(8,128)S(1)}, f32[256,128]{1,0:T(8,128)S(1)}, f32[256,128]{1,0:T(8,128)S(1)}, f32[512,128]{1,0:T(8,128)S(1)}, f32[24,128]{1,0:T(8,128)S(1)}) custom-call(s32[10]{0:T(128)S(1)} %stack.40.info, f32[264,128]{1,0:T(8,128)S(1)} %get-tuple-element.145.ya, f32[256,128]{1,0:T(8,128)S(1)} %get-tuple-element.146.yb, ...), custom_call_target="tpu_custom_call" | custom-call | tf_op jit(solution)/shard_map/pallas_call | solution.py:496
  51.3 0.2 collective-permute-start.20
  51.5 1.0 %collective-permute-done.20.refs_1_ = f32[24,128]{1,0:T(8,128)S(1)} collective-permute-done((f32[24,128]{1,0:T(8,128)S(1)}, f32[24,128]{1,0:T(8,128)S(1)}, u32[]{:S(2)}, u32[]{:S(2)}) %collective-permute-start.20) | collective-permute-done | bytes 12320 | tf_op jit(solution)/shard_map/ppermute | solution.py:429
  52.6 0.6 collective-permute-start.21
  53.2 1.7 %collective-permute-start.22 = (f32[24,128]{1,0:T(8,128)S(1)}, f32[24,128]{1,0:T(8,128)S(1)}, u32[]{:S(2)}, u32[]{:S(2)}) collective-permute-start(f32[24,128]{1,0:T(8,128)S(1)} %shard_map.63.refs_0_), channel_id=1, source_target_pairs={{0,1},{1,0},{2,3},{3,2},{4,5},{5,4},{6,7},{7,6},{8,9},{9,8},{10,11... | collective-permute-start | bytes 36872 | tf_op jit(solution)/shard_map/ppermute | solution.py:429
  54.9 1.2 %collective-permute-start.23 = (f32[24,128]{1,0:T(8,128)S(1)}, f32[24,128]{1,0:T(8,128)S(1)}, u32[]{:S(2)}, u32[]{:S(2)}) collective-permute-start(f32[24,128]{1,0:T(8,128)S(1)} %shard_map.63.refs_0_), channel_id=1, source_target_pairs={{0,16},{1,17},{2,18},{3,19},{4,20},{5,21},{6,22},{7,23},{8,24},{9,... | collective-permute-start | bytes 36872 | tf_op jit(solution)/shard_map/ppermute | solution.py:429
  56.1 2.2 %collective-permute-start.19 = (f32[256,128]{1,0:T(8,128)S(1)}, f32[256,128]{1,0:T(8,128)S(1)}, u32[]{:S(2)}, u32[]{:S(2)}) collective-permute-start(f32[256,128]{1,0:T(8,128)S(1)} %get-tuple-element.153), channel_id=1, source_target_pairs={{0,7},{1,0},{2,1},{3,2},{4,3},{5,4},{6,5},{7,6},{8,15},{9,8},{10,9... | collective-permute-start | bytes 393224 | tf_op jit(solution)/shard_map/ppermute | solution.py:403
  58.3 0.3 collective-permute-done.23.refs_3_
  58.6 0.1 shard_map.64.rest_0_
  58.7 0.0 copy-start.2
  58.7 0.8 %collective-permute-start.24 = (f32[24,128]{1,0:T(8,128)S(1)}, f32[24,128]{1,0:T(8,128)S(1)}, u32[]{:S(2)}, u32[]{:S(2)}) collective-permute-start(f32[24,128]{1,0:T(8,128)S(1)} %shard_map.64.rest_0_), channel_id=1, source_target_pairs={{0,6},{1,7},{2,4},{3,5},{4,2},{5,3},{6,0},{7,1},{8,14},{9,15},{10,... | collective-permute-start | bytes 36872 | tf_op jit(solution)/shard_map/ppermute | solution.py:429
  59.5 0.6 collective-permute-start.25
  60.1 3.1 %collective-permute-start.26 = (f32[24,128]{1,0:T(8,128)S(1)}, f32[24,128]{1,0:T(8,128)S(1)}, u32[]{:S(2)}, u32[]{:S(2)}) collective-permute-start(f32[24,128]{1,0:T(8,128)S(1)} %shard_map.64.rest_0_), channel_id=1, source_target_pairs={{0,2},{1,3},{2,0},{3,1},{4,6},{5,7},{6,4},{7,5},{8,10},{9,11},{10,... | collective-permute-start | bytes 36872 | tf_op jit(solution)/shard_map/ppermute | solution.py:429
  63.2 0.8 %copy.8 = f32[512,128]{0,1:T(8,128)} copy(f32[512,128]{1,0:T(8,128)S(1)} %bitcast.50) | data formatting | bytes 524288 | tf_op jit(solution)/shard_map/while | solution.py:561
  64.0 0.3 collective-permute-done.24.rest_1_
  64.3 0.5 collective-permute-done.26.rest_3_
  64.9 1.7 %shard_map.65 = (f32[512,128]{1,0:T(8,128)}, f32[512,128]{1,0:T(8,128)}, s32[1,1]{1,0:T(1,128)}) custom-call(s32[10]{0:T(128)S(1)} %stack.40.info, f32[1024,128]{1,0:T(8,128)S(1)} %get-tuple-element.134.u0, f32[1024,128]{1,0:T(8,128)S(1)} %get-tuple-element.139.u1, f32[1024,128]{1,0:T(8,128)S(1)} %get-tuple-element.144.u2, ...), custom_call_target="tpu_custom_call" | custom-call | tf_op jit(solution)/shard_map/pallas_call | solution.py:509
  66.6 0.7 %while.28 = (f32[512,128]{1,0:T(8,128)}, f32[512,128]{1,0:T(8,128)}, s32[]{:T(128)}, f32[512,128]{0,1:T(8,128)}, s32[]{:T(128)}, /*index=5*/f32[1,1,1024,1024]{3...) while((f32[512,128]{1,0:T(8,128)}, f32[512,128]{1,0:T(8,128)}, s32[]{:T(128)}, ...), condition=%region_9.10_spmd, body=%region_0.9_spmd | while | flops 3762094080 | bytes 49572704 | solution.py:561
  (13 shorter events, 0.1 us)
Async XLA Ops:
  0.6 12.1 %collective-permute-start.4 = (f32[512,128]{1,0:T(8,128)}, f32[512,128]{1,0:T(8,128)S(1)}, u32[]{:S(2)}, u32[]{:S(2)}) collective-permute-start(f32[512,128]{1,0:T(8,128)} %bitcast.47), channel_id=1, source_target_pairs={{0,8},{8,16},{16,24},{24,0},{1,9},{9,17},{17,25},{25,1},{2,10},{10... | collective-permute-start | bytes 786440 | tf_op jit(solution)/shard_map/ppermute | solution.py:403
  1.1 12.1 %collective-permute-start.5 = (f32[512,128]{1,0:T(8,128)}, f32[512,128]{1,0:T(8,128)S(1)}, u32[]{:S(2)}, u32[]{:S(2)}) collective-permute-start(f32[512,128]{1,0:T(8,128)} %bitcast.48), channel_id=1, source_target_pairs={{0,1},{1,2},{2,3},{3,4},{4,5},{5,6},{6,7},{7,0},{8,9},{9,10},{10,1... | collective-permute-start | bytes 786440 | tf_op jit(solution)/shard_map/ppermute | solution.py:403
  3.8 9.5 %copy-start = (f32[1,1,2,256,128]{4,3,2,1,0:T(8,128)S(1)}, f32[1,1,2,256,128]{4,3,2,1,0:T(8,128)}, u32[]{:S(2)}) copy-start(f32[1,1,2,256,128]{4,3,2,1,0:T(8,128)} %param.8) | copy-start | bytes 786436
  15.1 10.9 %collective-permute-start.8 = (f32[280,128]{1,0:T(8,128)S(1)}, f32[280,128]{1,0:T(8,128)S(1)}, u32[]{:S(2)}, u32[]{:S(2)}) collective-permute-start(f32[280,128]{1,0:T(8,128)S(1)} %get-tuple-element.137.yc.rest_2_), channel_id=1, source_target_pairs={{0,1},{1,0},{2,3},{3,2},{4,5},{5,4},{6,7},{7,6},{8,9},{9,8},{10,11... | collective-permute-start | bytes 430088 | tf_op jit(solution)/shard_map/ppermute | solution.py:413
  16.1 9.9 %collective-permute-start.9 = (f32[272,128]{1,0:T(8,128)S(1)}, f32[272,128]{1,0:T(8,128)S(1)}, u32[]{:S(2)}, u32[]{:S(2)}) collective-permute-start(f32[272,128]{1,0:T(8,128)S(1)} %get-tuple-element.138.yd.rest_3_), channel_id=1, source_target_pairs={{1,2},{2,1},{3,4},{4,3},{5,6},{6,5},{7,0},{0,7},{9,10},{10,9},{11,... | collective-permute-start | bytes 417800 | tf_op jit(solution)/shard_map/ppermute | solution.py:413
  19.7 6.3 %collective-permute-start.6 = (f32[264,128]{1,0:T(8,128)S(1)}, f32[264,128]{1,0:T(8,128)S(1)}, u32[]{:S(2)}, u32[]{:S(2)}) collective-permute-start(f32[264,128]{1,0:T(8,128)S(1)} %get-tuple-element.135.ya.rest_0_), channel_id=1, source_target_pairs={{0,8},{8,0},{16,24},{24,16},{1,9},{9,1},{17,25},{25,17},{2,10},{10... | collective-permute-start | bytes 405512 | tf_op jit(solution)/shard_map/ppermute | solution.py:413
  20.4 5.6 %collective-permute-start.7 = (f32[256,128]{1,0:T(8,128)S(1)}, f32[256,128]{1,0:T(8,128)S(1)}, u32[]{:S(2)}, u32[]{:S(2)}) collective-permute-start(f32[256,128]{1,0:T(8,128)S(1)} %get-tuple-element.136.yb.rest_1_), channel_id=1, source_target_pairs={{8,16},{16,8},{24,0},{0,24},{9,17},{17,9},{25,1},{1,25},{10,18},{1... | collective-permute-start | bytes 393224 | tf_op jit(solution)/shard_map/ppermute | solution.py:413
  27.8 8.8 %collective-permute-start.12 = (f32[280,128]{1,0:T(8,128)S(1)}, f32[280,128]{1,0:T(8,128)S(1)}, u32[]{:S(2)}, u32[]{:S(2)}) collective-permute-start(f32[280,128]{1,0:T(8,128)S(1)} %get-tuple-element.142.yc.rest_6_), channel_id=1, source_target_pairs={{0,1},{1,0},{2,3},{3,2},{4,5},{5,4},{6,7},{7,6},{8,9},{9,8},{10,11... | collective-permute-start | bytes 430088 | tf_op jit(solution)/shard_map/ppermute | solution.py:413
  27.9 8.6 %collective-permute-start.13 = (f32[272,128]{1,0:T(8,128)S(1)}, f32[272,128]{1,0:T(8,128)S(1)}, u32[]{:S(2)}, u32[]{:S(2)}) collective-permute-start(f32[272,128]{1,0:T(8,128)S(1)} %get-tuple-element.143.yd.rest_7_), channel_id=1, source_target_pairs={{1,2},{2,1},{3,4},{4,3},{5,6},{6,5},{7,0},{0,7},{9,10},{10,9},{11,... | collective-permute-start | bytes 417800 | tf_op jit(solution)/shard_map/ppermute | solution.py:413
  30.9 5.2 %collective-permute-start.10 = (f32[264,128]{1,0:T(8,128)S(1)}, f32[264,128]{1,0:T(8,128)S(1)}, u32[]{:S(2)}, u32[]{:S(2)}) collective-permute-start(f32[264,128]{1,0:T(8,128)S(1)} %get-tuple-element.140.ya.rest_4_), channel_id=1, source_target_pairs={{0,8},{8,0},{16,24},{24,16},{1,9},{9,1},{17,25},{25,17},{2,10},{10... | collective-permute-start | bytes 405512 | tf_op jit(solution)/shard_map/ppermute | solution.py:413
  30.9 5.2 %collective-permute-start.11 = (f32[256,128]{1,0:T(8,128)S(1)}, f32[256,128]{1,0:T(8,128)S(1)}, u32[]{:S(2)}, u32[]{:S(2)}) collective-permute-start(f32[256,128]{1,0:T(8,128)S(1)} %get-tuple-element.141.yb.rest_5_), channel_id=1, source_target_pairs={{8,16},{16,8},{24,0},{0,24},{9,17},{17,9},{25,1},{1,25},{10,18},{1... | collective-permute-start | bytes 393224 | tf_op jit(solution)/shard_map/ppermute | solution.py:413
  39.0 8.8 %collective-permute-start.16 = (f32[280,128]{1,0:T(8,128)S(1)}, f32[280,128]{1,0:T(8,128)S(1)}, u32[]{:S(2)}, u32[]{:S(2)}) collective-permute-start(f32[280,128]{1,0:T(8,128)S(1)} %get-tuple-element.147.yc), channel_id=1, source_target_pairs={{0,1},{1,0},{2,3},{3,2},{4,5},{5,4},{6,7},{7,6},{8,9},{9,8},{10,11... | collective-permute-start | bytes 430088 | tf_op jit(solution)/shard_map/ppermute | solution.py:413
  39.4 8.3 %collective-permute-start.17 = (f32[272,128]{1,0:T(8,128)S(1)}, f32[272,128]{1,0:T(8,128)S(1)}, u32[]{:S(2)}, u32[]{:S(2)}) collective-permute-start(f32[272,128]{1,0:T(8,128)S(1)} %get-tuple-element.148.yd), channel_id=1, source_target_pairs={{1,2},{2,1},{3,4},{4,3},{5,6},{6,5},{7,0},{0,7},{9,10},{10,9},{11,... | collective-permute-start | bytes 417800 | tf_op jit(solution)/shard_map/ppermute | solution.py:413
  42.3 5.2 %collective-permute-start.14 = (f32[264,128]{1,0:T(8,128)S(1)}, f32[264,128]{1,0:T(8,128)S(1)}, u32[]{:S(2)}, u32[]{:S(2)}) collective-permute-start(f32[264,128]{1,0:T(8,128)S(1)} %get-tuple-element.145.ya), channel_id=1, source_target_pairs={{0,8},{8,0},{16,24},{24,16},{1,9},{9,1},{17,25},{25,17},{2,10},{10... | collective-permute-start | bytes 405512 | tf_op jit(solution)/shard_map/ppermute | solution.py:413
  42.3 5.2 %collective-permute-start.15 = (f32[256,128]{1,0:T(8,128)S(1)}, f32[256,128]{1,0:T(8,128)S(1)}, u32[]{:S(2)}, u32[]{:S(2)}) collective-permute-start(f32[256,128]{1,0:T(8,128)S(1)} %get-tuple-element.146.yb), channel_id=1, source_target_pairs={{8,16},{16,8},{24,0},{0,24},{9,17},{17,9},{25,1},{1,25},{10,18},{1... | collective-permute-start | bytes 393224 | tf_op jit(solution)/shard_map/ppermute | solution.py:413
  51.3 1.2 %collective-permute-start.20 = (f32[24,128]{1,0:T(8,128)S(1)}, f32[24,128]{1,0:T(8,128)S(1)}, u32[]{:S(2)}, u32[]{:S(2)}) collective-permute-start(f32[24,128]{1,0:T(8,128)S(1)} %get-tuple-element.154.refs_0_), channel_id=1, source_target_pairs={{0,8},{1,9},{2,10},{3,11},{4,12},{5,13},{6,14},{7,15},{8,0},{9,1},... | collective-permute-start | bytes 36872 | tf_op jit(solution)/shard_map/ppermute | solution.py:429
  52.6 5.8 %collective-permute-start.21 = (f32[24,128]{1,0:T(8,128)S(1)}, f32[24,128]{1,0:T(8,128)S(1)}, u32[]{:S(2)}, u32[]{:S(2)}) collective-permute-start(f32[24,128]{1,0:T(8,128)S(1)} %shard_map.63.refs_0_), channel_id=1, source_target_pairs={{0,17},{1,16},{2,19},{3,18},{4,21},{5,20},{6,23},{7,22},{8,25},{9,... | collective-permute-start | bytes 36872 | tf_op jit(solution)/shard_map/ppermute | solution.py:429
  53.2 5.1 %collective-permute-start.22 = (f32[24,128]{1,0:T(8,128)S(1)}, f32[24,128]{1,0:T(8,128)S(1)}, u32[]{:S(2)}, u32[]{:S(2)}) collective-permute-start(f32[24,128]{1,0:T(8,128)S(1)} %shard_map.63.refs_0_), channel_id=1, source_target_pairs={{0,1},{1,0},{2,3},{3,2},{4,5},{5,4},{6,7},{7,6},{8,9},{9,8},{10,11... | collective-permute-start | bytes 36872 | tf_op jit(solution)/shard_map/ppermute | solution.py:429
  54.9 3.7 %collective-permute-start.23 = (f32[24,128]{1,0:T(8,128)S(1)}, f32[24,128]{1,0:T(8,128)S(1)}, u32[]{:S(2)}, u32[]{:S(2)}) collective-permute-start(f32[24,128]{1,0:T(8,128)S(1)} %shard_map.63.refs_0_), channel_id=1, source_target_pairs={{0,16},{1,17},{2,18},{3,19},{4,20},{5,21},{6,22},{7,23},{8,24},{9,... | collective-permute-start | bytes 36872 | tf_op jit(solution)/shard_map/ppermute | solution.py:429
  56.1 8.8 %collective-permute-start.18 = (f32[256,128]{1,0:T(8,128)S(1)}, f32[256,128]{1,0:T(8,128)S(1)}, u32[]{:S(2)}, u32[]{:S(2)}) collective-permute-start(f32[256,128]{1,0:T(8,128)S(1)} %get-tuple-element.152), channel_id=1, source_target_pairs={{0,24},{8,0},{16,8},{24,16},{1,25},{9,1},{17,9},{25,17},{2,26},{10... | collective-permute-start | bytes 393224 | tf_op jit(solution)/shard_map/ppermute | solution.py:403
  56.1 8.8 %collective-permute-start.19 = (f32[256,128]{1,0:T(8,128)S(1)}, f32[256,128]{1,0:T(8,128)S(1)}, u32[]{:S(2)}, u32[]{:S(2)}) collective-permute-start(f32[256,128]{1,0:T(8,128)S(1)} %get-tuple-element.153), channel_id=1, source_target_pairs={{0,7},{1,0},{2,1},{3,2},{4,3},{5,4},{6,5},{7,6},{8,15},{9,8},{10,9... | collective-permute-start | bytes 393224 | tf_op jit(solution)/shard_map/ppermute | solution.py:403
  58.7 7.9 %copy-start.2 = (s32[1,1,8,8]{3,2,1,0:T(8,128)S(1)}, s32[1,1,8,8]{3,2,1,0:T(8,128)}, u32[]{:S(2)}) copy-start(s32[1,1,8,8]{3,2,1,0:T(8,128)} %param.11) | copy-start | bytes 772
  58.7 5.6 %collective-permute-start.24 = (f32[24,128]{1,0:T(8,128)S(1)}, f32[24,128]{1,0:T(8,128)S(1)}, u32[]{:S(2)}, u32[]{:S(2)}) collective-permute-start(f32[24,128]{1,0:T(8,128)S(1)} %shard_map.64.rest_0_), channel_id=1, source_target_pairs={{0,6},{1,7},{2,4},{3,5},{4,2},{5,3},{6,0},{7,1},{8,14},{9,15},{10,... | collective-permute-start | bytes 36872 | tf_op jit(solution)/shard_map/ppermute | solution.py:429
  59.5 4.8 %collective-permute-start.25 = (f32[24,128]{1,0:T(8,128)S(1)}, f32[24,128]{1,0:T(8,128)S(1)}, u32[]{:S(2)}, u32[]{:S(2)}) collective-permute-start(f32[24,128]{1,0:T(8,128)S(1)} %shard_map.64.rest_0_), channel_id=1, source_target_pairs={{0,4},{1,5},{2,6},{3,7},{4,0},{5,1},{6,2},{7,3},{8,12},{9,13},{10,... | collective-permute-start | bytes 36872 | tf_op jit(solution)/shard_map/ppermute | solution.py:429
  60.1 4.8 %collective-permute-start.26 = (f32[24,128]{1,0:T(8,128)S(1)}, f32[24,128]{1,0:T(8,128)S(1)}, u32[]{:S(2)}, u32[]{:S(2)}) collective-permute-start(f32[24,128]{1,0:T(8,128)S(1)} %shard_map.64.rest_0_), channel_id=1, source_target_pairs={{0,2},{1,3},{2,0},{3,1},{4,6},{5,7},{6,4},{7,5},{8,10},{9,11},{10,... | collective-permute-start | bytes 36872 | tf_op jit(solution)/shard_map/ppermute | solution.py:429

commit v4 on v3

--- a/solution.py
+++ b/solution.py
@@ -213,9 +213,33 @@
     return out
 
 
+def shares(us, ys, scale, pairs):
+    face = us[0].shape[0] // 4
+    sums = [jnp.zeros((8, us[0].shape[1]), F32)] * (2 * len(pairs))
+    step = 16
+    for k in range(4):
+        for at in range(0, face, step):
+            here, there = slice(at, at + step), slice(k * face + at, k * face + at + step)
+            v = differences([u[there, :] for u in us], scale)
+            f = differences([y[k][here, :] for y in ys], scale)
+            for q, (i, j) in enumerate(pairs):
+                for part, term in ((0, v[i] * v[j]), (1, v[j] * f[i])):
+                    for m in range(0, step, 8):
+                        sums[2 * q + part] = sums[2 * q + part] + term[m : m + 8]
+    return [rows_sum(value) * (scale if k % 2 else 0.5) for k, value in enumerate(sums)]
+
+
+def early_shares_kernel(u0, u1, u2, *rest):
+    ys, (center, out) = rest[:12], rest[12:]
+    pairs = [pair for pair in PAIRS if pair[1] < 3]
+    values = shares((u0, u1, u2), (ys[:4], ys[4:8], ys[8:]), 1.0 / center[0:1, :], pairs)
+    out[...] = jnp.zeros_like(out)
+    for k, value in enumerate(values):
+        out[k : k + 1, :] = value
+
+
 def last_kernel(info, ya, yb, yc, yd, ra, rb, rc, rd, u0, u1, u2, *rest):
-    ys, (center, g_ref, u_ref, down, left, yo_ref, node, y_ref) = rest[:8], rest[8:]
-    ys = [ys[:4], ys[4:], (ya, yb, yc, yd)]
+    ys, (early, center, g_ref, u_ref, down, left, yo_ref, node, y_ref) = rest[:8], rest[8:]
     take_in(info, u_ref, (ya, yb, yc, yd), (ra, rb, rc, rd))
     face = down.shape[0]
     y_ref[...] = fine_product(g_ref, u_ref[...])
@@ -229,21 +253,18 @@
     yo_ref[face:, :] = y_ref[rows(3), :]
 
     middle = center[0:1, :]
-    scale = 1.0 / middle
-    sums = [jnp.zeros((8, down.shape[1]), F32)] * (2 * len(PAIRS))
-    step = 16
-    for k in range(4):
-        for at in range(0, face, step):
-            here, there = slice(at, at + step), slice(k * face + at, k * face + at + step)
-            v = differences([u[there, :] for u in (u0, u1, u2, u_ref)], scale)
-            f = differences([y[k][here, :] for y in ys] + [y_ref[there, :]], scale)
-            for q, (i, j) in enumerate(PAIRS):
-                for part, term in ((0, v[i] * v[j]), (1, v[j] * f[i])):
-                    for m in range(0, step, 8):
-                        sums[2 * q + part] = sums[2 * q + part] + term[m : m + 8]
-    for q in range(len(PAIRS)):
-        node[2 * q : 2 * q + 1, :] = 0.5 * rows_sum(sums[2 * q])
-        node[2 * q + 1 : 2 * q + 2, :] = scale * rows_sum(sums[2 * q + 1])
+    y3 = tuple(y_ref.at[k * face : (k + 1) * face, :] for k in range(4))
+    pairs = [pair for pair in PAIRS if pair[1] == 3]
+    values = shares((u0, u1, u2, u_ref), (ys[:4], ys[4:], (ya, yb, yc, yd), y3), 1.0 / middle, pairs)
+    at_early = at_late = 0
+    for q, pair in enumerate(PAIRS):
+        here = slice(2 * q, 2 * q + 2)
+        if pair[1] < 3:
+            node[here, :] = early[2 * at_early : 2 * at_early + 2, :]
+            at_early += 1
+        else:
+            node[here, :] = jnp.concatenate(values[2 * at_late : 2 * at_late + 2], axis=0)
+            at_late += 1
     node[CENTER:NODE, :] = jnp.broadcast_to(middle, (NODE - CENTER, middle.shape[1]))
 
 
@@ -541,12 +562,13 @@
     u0, *y0 = call(first_kernel, [whole, *sent], [], 1, info, below, beside, rhs, operator)
     u1, *y1 = call(functools.partial(next_kernel, False), [whole, *sent], [], 1, info, *y0, *exchanged(*y0), operator)
     u2, *y2 = call(functools.partial(next_kernel, True), [whole, *sent], [], 1, info, *y1, *exchanged(*y1), operator)
+    (early,) = call(early_shares_kernel, [shaped(16, cases)], [], 0, u0, u1, u2, *y0, *y1, *y2, center)
     u3, y_down, y_left, y_own, total = call(
         last_kernel,
         [whole, part, part, owned, node],
         [pltpu.VMEM((size, cases), F32)],
         1,
-        info, *y2, *exchanged(*y2), u0, u1, u2, *y0, *y1, center, operator,
+        info, *y2, *exchanged(*y2), u0, u1, u2, *y0, *y1, early, center, operator,
     )
     got_right = upward(y_left, "facade", -1, True)
     got_up = upward(y_down, "floor", -1, True)

time: 67.6 us -> 67.2 us (level)
  waiting for transfers between devices: 17.2 us -> 16.2 us
    ppermute x12, waiting for transfers between devices: 14.4 us -> 13.4 us  [swapped(): return lax.ppermute(value, axis, pairs)]
    pallas_call x6 -> x7, Pallas kernels: 9.49 us -> 10.1 us  [call(): pl.pallas_call(kernel, in_specs=[pl.BlockSpec(memory_space=pltpu.SMEM)] *...]
  transfers between devices with their start and end apart: 23 -> 23, of which waited for: 12 -> 12; matrix products, arithmetic and copies ran while one was open for 1% -> 1% of each run, Pallas kernels for 13% -> 15%
where the time goes in v4:
time: 67.2 us; the launch traced here: 67.1 us
  starting transfers between devices  27.7 us (41%)
  Pallas kernels  20.7 us (31%)
  waiting for transfers between devices  16.2 us (24%)
  local copies, waits for them, and re-layouts  0.92 us (1%)
  between operations  0.9 us (1%)
  loops' own time  0.68 us (1%)
    ppermute x12, starting transfers between devices, swapped(): return lax.ppermute(value, axis, pairs)  14.2 us
    ppermute x12, waiting for transfers between devices, swapped(): return lax.ppermute(value, axis, pairs)  13.4 us
    pallas_call x7, Pallas kernels, call(): pl.pallas_call(kernel, in_specs=[pl.BlockSpec(memory_space=pltpu.SMEM)] *...  10.1 us
    pallas_call x1, Pallas kernels, build_operator(): pl.pallas_call(operator_kernel, in_specs=[pl.BlockSpec(memory_space=pltpu...  8.91 us
    ppermute x7, starting transfers between devices, flipped(): return lax.ppermute(value, AXES, pairs)  8.22 us
    ppermute x4, starting transfers between devices, upward(): return lax.ppermute(value, axis, pairs)  5.29 us
    ppermute x7, waiting for transfers between devices, flipped(): return lax.ppermute(value, AXES, pairs)  2.19 us
    pallas_call x1, Pallas kernels, finish(): pl.pallas_call(final_kernel, in_specs=[pl.BlockSpec(memory_space=pltpu.SM...  1.73 us
  transfers between devices with their start and end apart: 23, of which 12 were waited for; matrix products, arithmetic and copies ran while one was open for 1% of the time, Pallas kernels for 15%

profile of v4, /device:TPU:0, one launch (start us, length us, event | category | flops | bytes accessed | tf_op | source)
XLA Modules:
  0.0 67.1 jit_solution(12831079284097494933)
XLA Ops:
  0.6 0.5 collective-permute-start.4
  1.1 2.6 %collective-permute-start.5 = (f32[512,128]{1,0:T(8,128)}, f32[512,128]{1,0:T(8,128)S(1)}, u32[]{:S(2)}, u32[]{:S(2)}) collective-permute-start(f32[512,128]{1,0:T(8,128)} %bitcast.48), channel_id=1, source_target_pairs={{0,1},{1,2},{2,3},{3,4},{4,5},{5,6},{6,7},{7,0},{8,9},{9,10},{10,1... | collective-permute-start | bytes 786440 | tf_op jit(solution)/shard_map/ppermute | solution.py:424
  3.7 0.1 stack.40.info
  3.8 8.9 %operator.1 = (bf16[1024,2048]{1,0:T(8,128)(2,1)S(1)}, f32[8,128]{1,0:T(8,128)S(1)}) custom-call(s32[10]{0:T(128)S(1)} %stack.40.info, s32[8,8]{1,0:T(8,128)} %bitcast.57, f32[1024,1024]{1,0:T(8,128)} %bitcast.51, bf16[1024,1024]{1,0:T(8,128)(2,1)} %bitcast.55), custom_call_target="tpu_custom_call" | custom-call | tf_op jit(solution)/shard_map/operator/pallas_call | solution.py:116
  12.7 0.0 collective-permute-done.4.below
  12.7 0.5 collective-permute-done.5.beside
  13.3 1.8 %shard_map.59 = (f32[1024,128]{1,0:T(8,128)S(1)}, f32[264,128]{1,0:T(8,128)S(1)}, f32[256,128]{1,0:T(8,128)S(1)}, f32[280,128]{1,0:T(8,128)S(1)}, f32[272,128]{1,0:T(8,128)S(1)}) custom-call(s32[10]{0:T(128)S(1)} %stack.40.info, f32[512,128]{1,0:T(8,128)S(1)} %collective-permute-done.4.below, f32[512,128]{1,0:T(8,128)S(1)} %collective-permute-done.5.beside, ...), custom_call_target="tpu_custom_call" | custom-call | tf_op jit(solution)/shard_map/pallas_call | solution.py:517
  15.1 1.1 %collective-permute-start.8 = (f32[280,128]{1,0:T(8,128)S(1)}, f32[280,128]{1,0:T(8,128)S(1)}, u32[]{:S(2)}, u32[]{:S(2)}) collective-permute-start(f32[280,128]{1,0:T(8,128)S(1)} %get-tuple-element.137.yc.rest_2_), channel_id=1, source_target_pairs={{0,1},{1,0},{2,3},{3,2},{4,5},{5,4},{6,7},{7,6},{8,9},{9,8},{10,11... | collective-permute-start | bytes 430088 | tf_op jit(solution)/shard_map/ppermute | solution.py:434
  16.1 3.6 %collective-permute-start.9 = (f32[272,128]{1,0:T(8,128)S(1)}, f32[272,128]{1,0:T(8,128)S(1)}, u32[]{:S(2)}, u32[]{:S(2)}) collective-permute-start(f32[272,128]{1,0:T(8,128)S(1)} %get-tuple-element.138.yd.rest_3_), channel_id=1, source_target_pairs={{1,2},{2,1},{3,4},{4,3},{5,6},{6,5},{7,0},{0,7},{9,10},{10,9},{11,... | collective-permute-start | bytes 417800 | tf_op jit(solution)/shard_map/ppermute | solution.py:434
  19.7 0.7 %collective-permute-start.6 = (f32[264,128]{1,0:T(8,128)S(1)}, f32[264,128]{1,0:T(8,128)S(1)}, u32[]{:S(2)}, u32[]{:S(2)}) collective-permute-start(f32[264,128]{1,0:T(8,128)S(1)} %get-tuple-element.135.ya.rest_0_), channel_id=1, source_target_pairs={{0,8},{8,0},{16,24},{24,16},{1,9},{9,1},{17,25},{25,17},{2,10},{10... | collective-permute-start | bytes 405512 | tf_op jit(solution)/shard_map/ppermute | solution.py:434
  20.4 0.9 %collective-permute-start.7 = (f32[256,128]{1,0:T(8,128)S(1)}, f32[256,128]{1,0:T(8,128)S(1)}, u32[]{:S(2)}, u32[]{:S(2)}) collective-permute-start(f32[256,128]{1,0:T(8,128)S(1)} %get-tuple-element.136.yb.rest_1_), channel_id=1, source_target_pairs={{8,16},{16,8},{24,0},{0,24},{9,17},{17,9},{25,1},{1,25},{10,18},{1... | collective-permute-start | bytes 393224 | tf_op jit(solution)/shard_map/ppermute | solution.py:434
  21.3 4.7 %collective-permute-done.7.rb = f32[256,128]{1,0:T(8,128)S(1)} collective-permute-done((f32[256,128]{1,0:T(8,128)S(1)}, f32[256,128]{1,0:T(8,128)S(1)}, u32[]{:S(2)}, u32[]{:S(2)}) %collective-permute-start.7) | collective-permute-done | bytes 131104 | tf_op jit(solution)/shard_map/ppermute | solution.py:434
  26.0 0.0 collective-permute-done.6.ra
  26.0 0.0 collective-permute-done.9.rd
  26.0 0.0 collective-permute-done.8.rc
  26.0 1.8 %shard_map.60 = (f32[1024,128]{1,0:T(8,128)S(1)}, f32[264,128]{1,0:T(8,128)S(1)}, f32[256,128]{1,0:T(8,128)S(1)}, f32[280,128]{1,0:T(8,128)S(1)}, f32[272,128]{1,0:T(8,128)S(1)}) custom-call(s32[10]{0:T(128)S(1)} %stack.40.info, f32[264,128]{1,0:T(8,128)S(1)} %get-tuple-element.135.ya.rest_0_, f32[256,128]{1,0:T(8,128)S(1)} %get-tuple-element.136.yb.rest_1_, ...), custom_call_target="tpu_custom_call" | custom-call | tf_op jit(solution)/shard_map/pallas_call | solution.py:517
  27.8 0.1 collective-permute-start.12
  27.9 3.0 %collective-permute-start.13 = (f32[272,128]{1,0:T(8,128)S(1)}, f32[272,128]{1,0:T(8,128)S(1)}, u32[]{:S(2)}, u32[]{:S(2)}) collective-permute-start(f32[272,128]{1,0:T(8,128)S(1)} %get-tuple-element.143.yd.rest_7_), channel_id=1, source_target_pairs={{1,2},{2,1},{3,4},{4,3},{5,6},{6,5},{7,0},{0,7},{9,10},{10,9},{11,... | collective-permute-start | bytes 417800 | tf_op jit(solution)/shard_map/ppermute | solution.py:434
  30.9 1.2 %collective-permute-start.11 = (f32[256,128]{1,0:T(8,128)S(1)}, f32[256,128]{1,0:T(8,128)S(1)}, u32[]{:S(2)}, u32[]{:S(2)}) collective-permute-start(f32[256,128]{1,0:T(8,128)S(1)} %get-tuple-element.141.yb.rest_5_), channel_id=1, source_target_pairs={{8,16},{16,8},{24,0},{0,24},{9,17},{17,9},{25,1},{1,25},{10,18},{1... | collective-permute-start | bytes 393224 | tf_op jit(solution)/shard_map/ppermute | solution.py:434
  32.1 3.9 %collective-permute-done.11.rb = f32[256,128]{1,0:T(8,128)S(1)} collective-permute-done((f32[256,128]{1,0:T(8,128)S(1)}, f32[256,128]{1,0:T(8,128)S(1)}, u32[]{:S(2)}, u32[]{:S(2)}) %collective-permute-start.11) | collective-permute-done | bytes 131104 | tf_op jit(solution)/shard_map/ppermute | solution.py:434
  36.0 0.4 collective-permute-done.13.rd
  36.5 0.2 collective-permute-done.12.rc
  36.7 2.4 %shard_map.61 = (f32[1024,128]{1,0:T(8,128)S(1)}, f32[264,128]{1,0:T(8,128)S(1)}, f32[256,128]{1,0:T(8,128)S(1)}, f32[280,128]{1,0:T(8,128)S(1)}, f32[272,128]{1,0:T(8,128)S(1)}) custom-call(s32[10]{0:T(128)S(1)} %stack.40.info, f32[264,128]{1,0:T(8,128)S(1)} %get-tuple-element.140.ya.rest_4_, f32[256,128]{1,0:T(8,128)S(1)} %get-tuple-element.141.yb.rest_5_, ...), custom_call_target="tpu_custom_call" | custom-call | tf_op jit(solution)/shard_map/pallas_call | solution.py:517
  39.0 0.3 collective-permute-start.16
  39.4 2.9 %collective-permute-start.17 = (f32[272,128]{1,0:T(8,128)S(1)}, f32[272,128]{1,0:T(8,128)S(1)}, u32[]{:S(2)}, u32[]{:S(2)}) collective-permute-start(f32[272,128]{1,0:T(8,128)S(1)} %get-tuple-element.148.rest_11_.yd), channel_id=1, source_target_pairs={{1,2},{2,1},{3,4},{4,3},{5,6},{6,5},{7,0},{0,7},{9,10},{10,9},{11,... | collective-permute-start | bytes 417800 | tf_op jit(solution)/shard_map/ppermute | solution.py:434
  42.3 0.4 collective-permute-start.15
  42.7 1.0 %shard_map.62.rest_8_ = f32[16,128]{1,0:T(8,128)S(1)} custom-call(f32[1024,128]{1,0:T(8,128)S(1)} %get-tuple-element.134.u0, f32[1024,128]{1,0:T(8,128)S(1)} %get-tuple-element.139.u1, f32[1024,128]{1,0:T(8,128)S(1)} %get-tuple-element.144.u2, f32[264,128]{1,0:T(8,128)S(1)} %get-tuple-element.135.ya.rest_0_, f32[256,128]{1,0:T(8,128)S(1)} %get-tuple-element.136.yb.rest_1_, ...), custom_call_target="tpu_custom_call" | custom-call | tf_op jit(solution)/shard_map/pallas_call | solution.py:517
  43.7 3.7 %collective-permute-done.15.rb = f32[256,128]{1,0:T(8,128)S(1)} collective-permute-done((f32[256,128]{1,0:T(8,128)S(1)}, f32[256,128]{1,0:T(8,128)S(1)}, u32[]{:S(2)}, u32[]{:S(2)}) %collective-permute-start.15) | collective-permute-done | bytes 131104 | tf_op jit(solution)/shard_map/ppermute | solution.py:434
  47.4 0.3 collective-permute-done.17.rd
  47.7 0.2 collective-permute-done.16.rc
  47.9 3.0 %shard_map.63 = (f32[1024,128]{1,0:T(8,128)S(1)}, f32[256,128]{1,0:T(8,128)S(1)}, f32[256,128]{1,0:T(8,128)S(1)}, f32[512,128]{1,0:T(8,128)S(1)}, f32[24,128]{1,0:T(8,128)S(1)}) custom-call(s32[10]{0:T(128)S(1)} %stack.40.info, f32[264,128]{1,0:T(8,128)S(1)} %get-tuple-element.145.rest_8_.ya, f32[256,128]{1,0:T(8,128)S(1)} %get-tuple-element.146.rest_9_.yb, ...), custom_call_target="tpu_custom_call" | custom-call | tf_op jit(solution)/shard_map/pallas_call | solution.py:517
  50.9 0.2 collective-permute-start.20
  51.1 1.0 %collective-permute-done.20.refs_1_ = f32[24,128]{1,0:T(8,128)S(1)} collective-permute-done((f32[24,128]{1,0:T(8,128)S(1)}, f32[24,128]{1,0:T(8,128)S(1)}, u32[]{:S(2)}, u32[]{:S(2)}) %collective-permute-start.20) | collective-permute-done | bytes 12320 | tf_op jit(solution)/shard_map/ppermute | solution.py:450
  52.2 0.6 collective-permute-start.21
  52.8 1.7 %collective-permute-start.22 = (f32[24,128]{1,0:T(8,128)S(1)}, f32[24,128]{1,0:T(8,128)S(1)}, u32[]{:S(2)}, u32[]{:S(2)}) collective-permute-start(f32[24,128]{1,0:T(8,128)S(1)} %shard_map.64.refs_0_), channel_id=1, source_target_pairs={{0,1},{1,0},{2,3},{3,2},{4,5},{5,4},{6,7},{7,6},{8,9},{9,8},{10,11... | collective-permute-start | bytes 36872 | tf_op jit(solution)/shard_map/ppermute | solution.py:450
  54.6 1.2 %collective-permute-start.23 = (f32[24,128]{1,0:T(8,128)S(1)}, f32[24,128]{1,0:T(8,128)S(1)}, u32[]{:S(2)}, u32[]{:S(2)}) collective-permute-start(f32[24,128]{1,0:T(8,128)S(1)} %shard_map.64.refs_0_), channel_id=1, source_target_pairs={{0,16},{1,17},{2,18},{3,19},{4,20},{5,21},{6,22},{7,23},{8,24},{9,... | collective-permute-start | bytes 36872 | tf_op jit(solution)/shard_map/ppermute | solution.py:450
  55.7 2.2 %collective-permute-start.19 = (f32[256,128]{1,0:T(8,128)S(1)}, f32[256,128]{1,0:T(8,128)S(1)}, u32[]{:S(2)}, u32[]{:S(2)}) collective-permute-start(f32[256,128]{1,0:T(8,128)S(1)} %get-tuple-element.153), channel_id=1, source_target_pairs={{0,7},{1,0},{2,1},{3,2},{4,3},{5,4},{6,5},{7,6},{8,15},{9,8},{10,9... | collective-permute-start | bytes 393224 | tf_op jit(solution)/shard_map/ppermute | solution.py:424
  57.9 0.3 collective-permute-done.23.refs_3_
  58.3 0.1 shard_map.65.rest_0_
  58.3 0.0 copy-start.2
  58.4 0.8 %collective-permute-start.24 = (f32[24,128]{1,0:T(8,128)S(1)}, f32[24,128]{1,0:T(8,128)S(1)}, u32[]{:S(2)}, u32[]{:S(2)}) collective-permute-start(f32[24,128]{1,0:T(8,128)S(1)} %shard_map.65.rest_0_), channel_id=1, source_target_pairs={{0,6},{1,7},{2,4},{3,5},{4,2},{5,3},{6,0},{7,1},{8,14},{9,15},{10,... | collective-permute-start | bytes 36872 | tf_op jit(solution)/shard_map/ppermute | solution.py:450
  59.2 0.6 collective-permute-start.25
  59.7 3.1 %collective-permute-start.26 = (f32[24,128]{1,0:T(8,128)S(1)}, f32[24,128]{1,0:T(8,128)S(1)}, u32[]{:S(2)}, u32[]{:S(2)}) collective-permute-start(f32[24,128]{1,0:T(8,128)S(1)} %shard_map.65.rest_0_), channel_id=1, source_target_pairs={{0,2},{1,3},{2,0},{3,1},{4,6},{5,7},{6,4},{7,5},{8,10},{9,11},{10,... | collective-permute-start | bytes 36872 | tf_op jit(solution)/shard_map/ppermute | solution.py:450
  62.8 0.8 %copy.8 = f32[512,128]{0,1:T(8,128)} copy(f32[512,128]{1,0:T(8,128)S(1)} %bitcast.50) | data formatting | bytes 524288 | tf_op jit(solution)/shard_map/while | solution.py:583
  63.6 0.3 collective-permute-done.24.rest_1_
  63.9 0.6 collective-permute-done.26.rest_3_
  64.5 1.7 %shard_map.66 = (f32[512,128]{1,0:T(8,128)}, f32[512,128]{1,0:T(8,128)}, s32[1,1]{1,0:T(1,128)}) custom-call(s32[10]{0:T(128)S(1)} %stack.40.info, f32[1024,128]{1,0:T(8,128)S(1)} %get-tuple-element.134.u0, f32[1024,128]{1,0:T(8,128)S(1)} %get-tuple-element.139.u1, f32[1024,128]{1,0:T(8,128)S(1)} %get-tuple-element.144.u2, ...), custom_call_target="tpu_custom_call" | custom-call | tf_op jit(solution)/shard_map/pallas_call | solution.py:530
  66.2 0.7 %while.28 = (f32[512,128]{1,0:T(8,128)}, f32[512,128]{1,0:T(8,128)}, s32[]{:T(128)}, f32[512,128]{0,1:T(8,128)}, s32[]{:T(128)}, /*index=5*/f32[1,1,1024,1024]{3...) while((f32[512,128]{1,0:T(8,128)}, f32[512,128]{1,0:T(8,128)}, s32[]{:T(128)}, ...), condition=%region_9.10_spmd, body=%region_0.9_spmd | while | flops 3762094080 | bytes 49572704 | solution.py:583
  (14 shorter events, 0.1 us)
Async XLA Ops:
  0.6 12.1 %collective-permute-start.4 = (f32[512,128]{1,0:T(8,128)}, f32[512,128]{1,0:T(8,128)S(1)}, u32[]{:S(2)}, u32[]{:S(2)}) collective-permute-start(f32[512,128]{1,0:T(8,128)} %bitcast.47), channel_id=1, source_target_pairs={{0,8},{8,16},{16,24},{24,0},{1,9},{9,17},{17,25},{25,1},{2,10},{10... | collective-permute-start | bytes 786440 | tf_op jit(solution)/shard_map/ppermute | solution.py:424
  1.1 12.1 %collective-permute-start.5 = (f32[512,128]{1,0:T(8,128)}, f32[512,128]{1,0:T(8,128)S(1)}, u32[]{:S(2)}, u32[]{:S(2)}) collective-permute-start(f32[512,128]{1,0:T(8,128)} %bitcast.48), channel_id=1, source_target_pairs={{0,1},{1,2},{2,3},{3,4},{4,5},{5,6},{6,7},{7,0},{8,9},{9,10},{10,1... | collective-permute-start | bytes 786440 | tf_op jit(solution)/shard_map/ppermute | solution.py:424
  3.8 9.5 %copy-start = (f32[1,1,2,256,128]{4,3,2,1,0:T(8,128)S(1)}, f32[1,1,2,256,128]{4,3,2,1,0:T(8,128)}, u32[]{:S(2)}) copy-start(f32[1,1,2,256,128]{4,3,2,1,0:T(8,128)} %param.8) | copy-start | bytes 786436
  15.1 10.9 %collective-permute-start.8 = (f32[280,128]{1,0:T(8,128)S(1)}, f32[280,128]{1,0:T(8,128)S(1)}, u32[]{:S(2)}, u32[]{:S(2)}) collective-permute-start(f32[280,128]{1,0:T(8,128)S(1)} %get-tuple-element.137.yc.rest_2_), channel_id=1, source_target_pairs={{0,1},{1,0},{2,3},{3,2},{4,5},{5,4},{6,7},{7,6},{8,9},{9,8},{10,11... | collective-permute-start | bytes 430088 | tf_op jit(solution)/shard_map/ppermute | solution.py:434
  16.1 9.9 %collective-permute-start.9 = (f32[272,128]{1,0:T(8,128)S(1)}, f32[272,128]{1,0:T(8,128)S(1)}, u32[]{:S(2)}, u32[]{:S(2)}) collective-permute-start(f32[272,128]{1,0:T(8,128)S(1)} %get-tuple-element.138.yd.rest_3_), channel_id=1, source_target_pairs={{1,2},{2,1},{3,4},{4,3},{5,6},{6,5},{7,0},{0,7},{9,10},{10,9},{11,... | collective-permute-start | bytes 417800 | tf_op jit(solution)/shard_map/ppermute | solution.py:434
  19.7 6.3 %collective-permute-start.6 = (f32[264,128]{1,0:T(8,128)S(1)}, f32[264,128]{1,0:T(8,128)S(1)}, u32[]{:S(2)}, u32[]{:S(2)}) collective-permute-start(f32[264,128]{1,0:T(8,128)S(1)} %get-tuple-element.135.ya.rest_0_), channel_id=1, source_target_pairs={{0,8},{8,0},{16,24},{24,16},{1,9},{9,1},{17,25},{25,17},{2,10},{10... | collective-permute-start | bytes 405512 | tf_op jit(solution)/shard_map/ppermute | solution.py:434
  20.4 5.6 %collective-permute-start.7 = (f32[256,128]{1,0:T(8,128)S(1)}, f32[256,128]{1,0:T(8,128)S(1)}, u32[]{:S(2)}, u32[]{:S(2)}) collective-permute-start(f32[256,128]{1,0:T(8,128)S(1)} %get-tuple-element.136.yb.rest_1_), channel_id=1, source_target_pairs={{8,16},{16,8},{24,0},{0,24},{9,17},{17,9},{25,1},{1,25},{10,18},{1... | collective-permute-start | bytes 393224 | tf_op jit(solution)/shard_map/ppermute | solution.py:434
  27.8 8.8 %collective-permute-start.12 = (f32[280,128]{1,0:T(8,128)S(1)}, f32[280,128]{1,0:T(8,128)S(1)}, u32[]{:S(2)}, u32[]{:S(2)}) collective-permute-start(f32[280,128]{1,0:T(8,128)S(1)} %get-tuple-element.142.yc.rest_6_), channel_id=1, source_target_pairs={{0,1},{1,0},{2,3},{3,2},{4,5},{5,4},{6,7},{7,6},{8,9},{9,8},{10,11... | collective-permute-start | bytes 430088 | tf_op jit(solution)/shard_map/ppermute | solution.py:434
  27.9 8.6 %collective-permute-start.13 = (f32[272,128]{1,0:T(8,128)S(1)}, f32[272,128]{1,0:T(8,128)S(1)}, u32[]{:S(2)}, u32[]{:S(2)}) collective-permute-start(f32[272,128]{1,0:T(8,128)S(1)} %get-tuple-element.143.yd.rest_7_), channel_id=1, source_target_pairs={{1,2},{2,1},{3,4},{4,3},{5,6},{6,5},{7,0},{0,7},{9,10},{10,9},{11,... | collective-permute-start | bytes 417800 | tf_op jit(solution)/shard_map/ppermute | solution.py:434
  30.9 5.2 %collective-permute-start.10 = (f32[264,128]{1,0:T(8,128)S(1)}, f32[264,128]{1,0:T(8,128)S(1)}, u32[]{:S(2)}, u32[]{:S(2)}) collective-permute-start(f32[264,128]{1,0:T(8,128)S(1)} %get-tuple-element.140.ya.rest_4_), channel_id=1, source_target_pairs={{0,8},{8,0},{16,24},{24,16},{1,9},{9,1},{17,25},{25,17},{2,10},{10... | collective-permute-start | bytes 405512 | tf_op jit(solution)/shard_map/ppermute | solution.py:434
  30.9 5.2 %collective-permute-start.11 = (f32[256,128]{1,0:T(8,128)S(1)}, f32[256,128]{1,0:T(8,128)S(1)}, u32[]{:S(2)}, u32[]{:S(2)}) collective-permute-start(f32[256,128]{1,0:T(8,128)S(1)} %get-tuple-element.141.yb.rest_5_), channel_id=1, source_target_pairs={{8,16},{16,8},{24,0},{0,24},{9,17},{17,9},{25,1},{1,25},{10,18},{1... | collective-permute-start | bytes 393224 | tf_op jit(solution)/shard_map/ppermute | solution.py:434
  39.0 8.8 %collective-permute-start.16 = (f32[280,128]{1,0:T(8,128)S(1)}, f32[280,128]{1,0:T(8,128)S(1)}, u32[]{:S(2)}, u32[]{:S(2)}) collective-permute-start(f32[280,128]{1,0:T(8,128)S(1)} %get-tuple-element.147.rest_10_.yc), channel_id=1, source_target_pairs={{0,1},{1,0},{2,3},{3,2},{4,5},{5,4},{6,7},{7,6},{8,9},{9,8},{10,11... | collective-permute-start | bytes 430088 | tf_op jit(solution)/shard_map/ppermute | solution.py:434
  39.4 8.3 %collective-permute-start.17 = (f32[272,128]{1,0:T(8,128)S(1)}, f32[272,128]{1,0:T(8,128)S(1)}, u32[]{:S(2)}, u32[]{:S(2)}) collective-permute-start(f32[272,128]{1,0:T(8,128)S(1)} %get-tuple-element.148.rest_11_.yd), channel_id=1, source_target_pairs={{1,2},{2,1},{3,4},{4,3},{5,6},{6,5},{7,0},{0,7},{9,10},{10,9},{11,... | collective-permute-start | bytes 417800 | tf_op jit(solution)/shard_map/ppermute | solution.py:434
  42.3 5.2 %collective-permute-start.14 = (f32[264,128]{1,0:T(8,128)S(1)}, f32[264,128]{1,0:T(8,128)S(1)}, u32[]{:S(2)}, u32[]{:S(2)}) collective-permute-start(f32[264,128]{1,0:T(8,128)S(1)} %get-tuple-element.145.rest_8_.ya), channel_id=1, source_target_pairs={{0,8},{8,0},{16,24},{24,16},{1,9},{9,1},{17,25},{25,17},{2,10},{10... | collective-permute-start | bytes 405512 | tf_op jit(solution)/shard_map/ppermute | solution.py:434
  42.3 5.2 %collective-permute-start.15 = (f32[256,128]{1,0:T(8,128)S(1)}, f32[256,128]{1,0:T(8,128)S(1)}, u32[]{:S(2)}, u32[]{:S(2)}) collective-permute-start(f32[256,128]{1,0:T(8,128)S(1)} %get-tuple-element.146.rest_9_.yb), channel_id=1, source_target_pairs={{8,16},{16,8},{24,0},{0,24},{9,17},{17,9},{25,1},{1,25},{10,18},{1... | collective-permute-start | bytes 393224 | tf_op jit(solution)/shard_map/ppermute | solution.py:434
  50.9 1.2 %collective-permute-start.20 = (f32[24,128]{1,0:T(8,128)S(1)}, f32[24,128]{1,0:T(8,128)S(1)}, u32[]{:S(2)}, u32[]{:S(2)}) collective-permute-start(f32[24,128]{1,0:T(8,128)S(1)} %get-tuple-element.154.refs_0_), channel_id=1, source_target_pairs={{0,8},{1,9},{2,10},{3,11},{4,12},{5,13},{6,14},{7,15},{8,0},{9,1},... | collective-permute-start | bytes 36872 | tf_op jit(solution)/shard_map/ppermute | solution.py:450
  52.2 5.8 %collective-permute-start.21 = (f32[24,128]{1,0:T(8,128)S(1)}, f32[24,128]{1,0:T(8,128)S(1)}, u32[]{:S(2)}, u32[]{:S(2)}) collective-permute-start(f32[24,128]{1,0:T(8,128)S(1)} %shard_map.64.refs_0_), channel_id=1, source_target_pairs={{0,17},{1,16},{2,19},{3,18},{4,21},{5,20},{6,23},{7,22},{8,25},{9,... | collective-permute-start | bytes 36872 | tf_op jit(solution)/shard_map/ppermute | solution.py:450
  52.8 5.1 %collective-permute-start.22 = (f32[24,128]{1,0:T(8,128)S(1)}, f32[24,128]{1,0:T(8,128)S(1)}, u32[]{:S(2)}, u32[]{:S(2)}) collective-permute-start(f32[24,128]{1,0:T(8,128)S(1)} %shard_map.64.refs_0_), channel_id=1, source_target_pairs={{0,1},{1,0},{2,3},{3,2},{4,5},{5,4},{6,7},{7,6},{8,9},{9,8},{10,11... | collective-permute-start | bytes 36872 | tf_op jit(solution)/shard_map/ppermute | solution.py:450
  54.6 3.7 %collective-permute-start.23 = (f32[24,128]{1,0:T(8,128)S(1)}, f32[24,128]{1,0:T(8,128)S(1)}, u32[]{:S(2)}, u32[]{:S(2)}) collective-permute-start(f32[24,128]{1,0:T(8,128)S(1)} %shard_map.64.refs_0_), channel_id=1, source_target_pairs={{0,16},{1,17},{2,18},{3,19},{4,20},{5,21},{6,22},{7,23},{8,24},{9,... | collective-permute-start | bytes 36872 | tf_op jit(solution)/shard_map/ppermute | solution.py:450
  55.7 8.8 %collective-permute-start.18 = (f32[256,128]{1,0:T(8,128)S(1)}, f32[256,128]{1,0:T(8,128)S(1)}, u32[]{:S(2)}, u32[]{:S(2)}) collective-permute-start(f32[256,128]{1,0:T(8,128)S(1)} %get-tuple-element.152), channel_id=1, source_target_pairs={{0,24},{8,0},{16,8},{24,16},{1,25},{9,1},{17,9},{25,17},{2,26},{10... | collective-permute-start | bytes 393224 | tf_op jit(solution)/shard_map/ppermute | solution.py:424
  55.7 8.8 %collective-permute-start.19 = (f32[256,128]{1,0:T(8,128)S(1)}, f32[256,128]{1,0:T(8,128)S(1)}, u32[]{:S(2)}, u32[]{:S(2)}) collective-permute-start(f32[256,128]{1,0:T(8,128)S(1)} %get-tuple-element.153), channel_id=1, source_target_pairs={{0,7},{1,0},{2,1},{3,2},{4,3},{5,4},{6,5},{7,6},{8,15},{9,8},{10,9... | collective-permute-start | bytes 393224 | tf_op jit(solution)/shard_map/ppermute | solution.py:424
  58.3 7.9 %copy-start.2 = (s32[1,1,8,8]{3,2,1,0:T(8,128)S(1)}, s32[1,1,8,8]{3,2,1,0:T(8,128)}, u32[]{:S(2)}) copy-start(s32[1,1,8,8]{3,2,1,0:T(8,128)} %param.11) | copy-start | bytes 772
  58.4 5.6 %collective-permute-start.24 = (f32[24,128]{1,0:T(8,128)S(1)}, f32[24,128]{1,0:T(8,128)S(1)}, u32[]{:S(2)}, u32[]{:S(2)}) collective-permute-start(f32[24,128]{1,0:T(8,128)S(1)} %shard_map.65.rest_0_), channel_id=1, source_target_pairs={{0,6},{1,7},{2,4},{3,5},{4,2},{5,3},{6,0},{7,1},{8,14},{9,15},{10,... | collective-permute-start | bytes 36872 | tf_op jit(solution)/shard_map/ppermute | solution.py:450
  59.2 4.8 %collective-permute-start.25 = (f32[24,128]{1,0:T(8,128)S(1)}, f32[24,128]{1,0:T(8,128)S(1)}, u32[]{:S(2)}, u32[]{:S(2)}) collective-permute-start(f32[24,128]{1,0:T(8,128)S(1)} %shard_map.65.rest_0_), channel_id=1, source_target_pairs={{0,4},{1,5},{2,6},{3,7},{4,0},{5,1},{6,2},{7,3},{8,12},{9,13},{10,... | collective-permute-start | bytes 36872 | tf_op jit(solution)/shard_map/ppermute | solution.py:450
  59.7 4.8 %collective-permute-start.26 = (f32[24,128]{1,0:T(8,128)S(1)}, f32[24,128]{1,0:T(8,128)S(1)}, u32[]{:S(2)}, u32[]{:S(2)}) collective-permute-start(f32[24,128]{1,0:T(8,128)S(1)} %shard_map.65.rest_0_), channel_id=1, source_target_pairs={{0,2},{1,3},{2,0},{3,1},{4,6},{5,7},{6,4},{7,5},{8,10},{9,11},{10,... | collective-permute-start | bytes 36872 | tf_op jit(solution)/shard_map/ppermute | solution.py:450

commit v5 on v4

--- a/solution.py
+++ b/solution.py
@@ -9,6 +9,7 @@
 
 ITERS = 4
 SLOT, KEEP, ODD = 0, 4, 8
+KEEP_A, KEEP_B, ABOVE, BELOW, ODD_FLOOR, ODD_FACADE = range(6)
 PADS = (8, 0, 24, 16)
 PAIRS = [(i, j) for i in range(4) for j in range(i, 4)]
 CENTER, NODE = 20, 24
@@ -164,12 +165,16 @@
     return jnp.sum(x, axis=0, keepdims=True)
 
 
-def take_in(info, u_ref, own, got):
+def holds(facts, row):
+    return facts[row : row + 1, :] > 0.5
+
+
+def take_in(facts, u_ref, own, got):
     face = u_ref.shape[0] // 4
     for k in range(4):
         value = own[k][0:face, :] - got[k][0:face, :]
         if k < 2:
-            value = jnp.where(info[KEEP + k] != 0, value, 0.0)
+            value = jnp.where(holds(facts, KEEP_A + k), value, 0.0)
         u_ref[k * face : (k + 1) * face, :] = value
 
 
@@ -181,13 +186,13 @@
             out[face:, :] = jnp.zeros((out.shape[0] - face, out.shape[1]), F32)
 
 
-def first_kernel(info, below, beside, rhs, g_ref, u_ref, a, b, c, d):
+def first_kernel(facts, below, beside, rhs, g_ref, u_ref, a, b, c, d):
     face = rhs.shape[0] // 2
-    own_up = jnp.where(info[KEEP + 2] != 0, rhs[0:face, :], 0.0)
+    own_up = jnp.where(holds(facts, ABOVE), rhs[0:face, :], 0.0)
     own_right = rhs[face:, :]
-    minus_below = jnp.where(info[KEEP + 3] != 0, -below[0:face, :], 0.0)
+    minus_below = jnp.where(holds(facts, BELOW), -below[0:face, :], 0.0)
     minus_beside = -beside[face:, :]
-    odd_floor, odd_facade = info[ODD] != 0, info[ODD + 1] != 0
+    odd_floor, odd_facade = holds(facts, ODD_FLOOR), holds(facts, ODD_FACADE)
     u_ref[0:face, :] = jnp.where(odd_floor, minus_below, own_up)
     u_ref[face : 2 * face, :] = jnp.where(odd_floor, own_up, minus_below)
     u_ref[2 * face : 3 * face, :] = jnp.where(odd_facade, minus_beside, own_right)
@@ -195,8 +200,8 @@
     hand_out(product(g_ref, u_ref[...]), (a, b, c, d))
 
 
-def next_kernel(fine, info, ya, yb, yc, yd, ra, rb, rc, rd, g_ref, u_ref, a, b, c, d):
-    take_in(info, u_ref, (ya, yb, yc, yd), (ra, rb, rc, rd))
+def next_kernel(fine, facts, ya, yb, yc, yd, ra, rb, rc, rd, g_ref, u_ref, a, b, c, d):
+    take_in(facts, u_ref, (ya, yb, yc, yd), (ra, rb, rc, rd))
     hand_out((fine_product if fine else product)(g_ref, u_ref[...]), (a, b, c, d))
 
 
@@ -238,19 +243,18 @@
         out[k : k + 1, :] = value
 
 
-def last_kernel(info, ya, yb, yc, yd, ra, rb, rc, rd, u0, u1, u2, *rest):
+def last_kernel(facts, ya, yb, yc, yd, ra, rb, rc, rd, u0, u1, u2, *rest):
     ys, (early, center, g_ref, u_ref, down, left, yo_ref, node, y_ref) = rest[:8], rest[8:]
-    take_in(info, u_ref, (ya, yb, yc, yd), (ra, rb, rc, rd))
+    take_in(facts, u_ref, (ya, yb, yc, yd), (ra, rb, rc, rd))
     face = down.shape[0]
     y_ref[...] = fine_product(g_ref, u_ref[...])
 
-    def rows(j):
-        return pl.ds(pl.multiple_of(info[SLOT + j] * face, face), face)
-
-    down[...] = y_ref[rows(0), :]
-    left[...] = y_ref[rows(2), :]
-    yo_ref[0:face, :] = y_ref[rows(1), :]
-    yo_ref[face:, :] = y_ref[rows(3), :]
+    odd_floor, odd_facade = holds(facts, ODD_FLOOR), holds(facts, ODD_FACADE)
+    a, b, c, d = (y_ref[k * face : (k + 1) * face, :] for k in range(4))
+    down[...] = jnp.where(odd_floor, a, b)
+    left[...] = jnp.where(odd_facade, c, d)
+    yo_ref[0:face, :] = jnp.where(odd_floor, b, a)
+    yo_ref[face:, :] = jnp.where(odd_facade, d, c)
 
     middle = center[0:1, :]
     y3 = tuple(y_ref.at[k * face : (k + 1) * face, :] for k in range(4))
@@ -388,12 +392,12 @@
         rows = slice(f * face, (f + 1) * face)
         image = yo_ref[rows, :] - got[...]
         if f == 0:
-            image = jnp.where(info[KEEP + 2] != 0, image, 0.0)
+            image = jnp.where(holds(facts, ABOVE), image, 0.0)
         w4_ref[rows, :] = image
     write_node(node, *merged(parts))
 
 
-def final_kernel(info, u0, u1, u2, u3, yo_ref, got_up, got_right, *rest):
+def final_kernel(facts, u0, u1, u2, u3, yo_ref, got_up, got_right, *rest):
     parts, (mult, resid, sound) = rest[:-3], rest[-3:]
     rows, middle = merged(parts)
     scale = 1.0 / middle
@@ -403,12 +407,13 @@
     r = powers(r, scale)
     face = got_up.shape[0]
     for f, got in enumerate((got_up, got_right)):
-        place = pl.ds(pl.multiple_of(info[SLOT + 2 * f + 1] * face, face), face)
+        odd = holds(facts, ODD_FACADE if f else ODD_FLOOR)
+        low, high = (slice((2 * f + k) * face, (2 * f + k + 1) * face) for k in range(2))
         here = slice(f * face, (f + 1) * face)
-        w = [u[place, :] for u in (u0, u1, u2, u3)]
+        w = [jnp.where(odd, u[high, :], u[low, :]) for u in (u0, u1, u2, u3)]
         image = yo_ref[here, :] - got[...]
         if f == 0:
-            image = jnp.where(info[KEEP + 2] != 0, image, 0.0)
+            image = jnp.where(holds(facts, ABOVE), image, 0.0)
         mult[here, :] = x[0] * w[0] + x[1] * w[1] + x[2] * w[2] + x[3] * w[3]
         resid[here, :] = r[0] * w[0] + r[1] * w[1] + r[2] * w[2] + r[3] * w[3] + r[4] * image
 
@@ -526,14 +531,14 @@
     )(*args)
 
 
-def finish(outs, info, *args):
+def finish(outs, *args):
     return pl.pallas_call(
         final_kernel,
-        in_specs=[pl.BlockSpec(memory_space=pltpu.SMEM)] + [pl.BlockSpec(memory_space=pltpu.VMEM)] * len(args),
+        in_specs=[pl.BlockSpec(memory_space=pltpu.VMEM)] * len(args),
         out_specs=[pl.BlockSpec(memory_space=pltpu.VMEM)] * 2 + [pl.BlockSpec(memory_space=pltpu.SMEM)],
         out_shape=outs + [jax.ShapeDtypeStruct((1, 1), jnp.int32)],
         compiler_params=params(16),
-    )(info, *args)
+    )(*args)
 
 
 def local(interface_rhs, inverse_factor, near_coupling, near_pattern):
@@ -548,9 +553,11 @@
     keep_b = jnp.where(odd_floor == 0, has_below, has_above)
     flags = [1 - odd_floor, odd_floor, 3 - odd_facade, 2 + odd_facade, keep_a, keep_b, has_above, has_below, odd_floor, odd_facade]
     info = jnp.stack(flags).astype(jnp.int32)
+    facts = jnp.stack(flags[KEEP:] + [0] * (8 - len(flags[KEEP:]))).astype(F32)
+    facts = jnp.broadcast_to(facts[:, None], (8, cases))
     rhs = interface_rhs.reshape(2 * face, cases)
+    below = upward(rhs, "floor", 1, True)
     beside = upward(rhs, "facade", 1, True)
-    below = upward(rhs, "floor", 1, True)
     operator, center = build_operator(info, inverse_factor[0, 0], near_coupling[0, 0], near_pattern[0, 0], cases)
 
     def shaped(*dims):
@@ -559,23 +566,23 @@
     whole, part, node, owned = shaped(size, cases), shaped(face, cases), shaped(NODE, cases), shaped(2 * face, cases)
     sent = [shaped(face + rows, cases) for rows in PADS]
 
-    u0, *y0 = call(first_kernel, [whole, *sent], [], 1, info, below, beside, rhs, operator)
-    u1, *y1 = call(functools.partial(next_kernel, False), [whole, *sent], [], 1, info, *y0, *exchanged(*y0), operator)
-    u2, *y2 = call(functools.partial(next_kernel, True), [whole, *sent], [], 1, info, *y1, *exchanged(*y1), operator)
+    u0, *y0 = call(first_kernel, [whole, *sent], [], 0, facts, below, beside, rhs, operator)
+    u1, *y1 = call(functools.partial(next_kernel, False), [whole, *sent], [], 0, facts, *y0, *exchanged(*y0), operator)
+    u2, *y2 = call(functools.partial(next_kernel, True), [whole, *sent], [], 0, facts, *y1, *exchanged(*y1), operator)
     (early,) = call(early_shares_kernel, [shaped(16, cases)], [], 0, u0, u1, u2, *y0, *y1, *y2, center)
     u3, y_down, y_left, y_own, total = call(
         last_kernel,
         [whole, part, part, owned, node],
         [pltpu.VMEM((size, cases), F32)],
-        1,
-        info, *y2, *exchanged(*y2), u0, u1, u2, *y0, *y1, early, center, operator,
+        0,
+        facts, *y2, *exchanged(*y2), u0, u1, u2, *y0, *y1, early, center, operator,
     )
     got_right = upward(y_left, "facade", -1, True)
     got_up = upward(y_down, "floor", -1, True)
     *stages, before, last = sum_stages()
     for stage in stages + [before]:
         (total,) = call(merge_kernel, [node], [], 0, *stage_parts(total, stage), flops=MERGE_FLOPS if stage is before else 0)
-    mult, resid, sound = finish([owned, owned], info, u0, u1, u2, u3, y_own, got_up, got_right, *stage_parts(total, last))
+    mult, resid, sound = finish([owned, owned], facts, u0, u1, u2, u3, y_own, got_up, got_right, *stage_parts(total, last))
     def one_by_one(state):
         result = plain_iterations(rhs, inverse_factor[0, 0], near_coupling[0, 0], near_pattern[0, 0], has_above)
         return (*call(hand_on_kernel, [owned, owned], [], 0, *result), jnp.int32(1))

time: 67.2 us -> 64.8 us (0.964)
  Pallas kernels: 20.7 us -> 18.2 us
    pallas_call x7, Pallas kernels: 10.1 us -> 7.99 us  [call(): pl.pallas_call(kernel, in_specs=[pl.BlockSpec(memory_space=pltpu.SMEM)] *...]
  transfers between devices with their start and end apart: 23 -> 23, of which waited for: 12 -> 12; matrix products, arithmetic and copies ran while one was open for 1% -> 2% of each run, Pallas kernels for 15% -> 15%
where the time goes in v5:
time: 64.8 us; the launch traced here: 64.7 us
  starting transfers between devices  27.8 us (43%)
  Pallas kernels  18.2 us (28%)
  waiting for transfers between devices  16 us (25%)
  local copies, waits for them, and re-layouts  1.08 us (2%)
  between operations  0.9 us (1%)
  loops' own time  0.68 us (1%)
    ppermute x12, starting transfers between devices, swapped(): return lax.ppermute(value, axis, pairs)  14.3 us
    ppermute x12, waiting for transfers between devices, swapped(): return lax.ppermute(value, axis, pairs)  13.4 us
    pallas_call x1, Pallas kernels, build_operator(): pl.pallas_call(operator_kernel, in_specs=[pl.BlockSpec(memory_space=pltpu...  8.91 us
    ppermute x7, starting transfers between devices, flipped(): return lax.ppermute(value, AXES, pairs)  8.21 us
    pallas_call x7, Pallas kernels, call(): pl.pallas_call(kernel, in_specs=[pl.BlockSpec(memory_space=pltpu.SMEM)] *...  7.99 us
    ppermute x4, starting transfers between devices, upward(): return lax.ppermute(value, axis, pairs)  5.33 us
    ppermute x7, waiting for transfers between devices, flipped(): return lax.ppermute(value, AXES, pairs)  2.16 us
  transfers between devices with their start and end apart: 23, of which 12 were waited for; matrix products, arithmetic and copies ran while one was open for 2% of the time, Pallas kernels for 15%

profile of v5, /device:TPU:0, one launch (start us, length us, event | category | flops | bytes accessed | tf_op | source)
XLA Modules:
  0.0 64.7 jit_solution(1051261849535124135)
XLA Ops:
  0.6 0.5 collective-permute-start.4
  1.1 2.6 %collective-permute-start.5 = (f32[512,128]{1,0:T(8,128)}, f32[512,128]{1,0:T(8,128)S(1)}, u32[]{:S(2)}, u32[]{:S(2)}) collective-permute-start(f32[512,128]{1,0:T(8,128)} %bitcast.48), channel_id=1, source_target_pairs={{0,1},{1,2},{2,3},{3,4},{4,5},{5,6},{6,7},{7,0},{8,9},{9,10},{10,1... | collective-permute-start | bytes 786440 | tf_op jit(solution)/shard_map/ppermute | solution.py:429
  3.7 0.1 stack.49
  3.8 0.1 stack.53.info
  3.9 8.9 %operator.1 = (bf16[1024,2048]{1,0:T(8,128)(2,1)S(1)}, f32[8,128]{1,0:T(8,128)S(1)}) custom-call(s32[10]{0:T(128)S(1)} %stack.53.info, s32[8,8]{1,0:T(8,128)} %bitcast.57, f32[1024,1024]{1,0:T(8,128)} %bitcast.51, bf16[1024,1024]{1,0:T(8,128)(2,1)} %bitcast.55), custom_call_target="tpu_custom_call" | custom-call | tf_op jit(solution)/shard_map/operator/pallas_call | solution.py:117
  12.8 0.0 collective-permute-done.4.below
  12.8 0.4 collective-permute-done.5.beside
  13.3 0.1 broadcast_in_dim.8.facts
  13.3 1.3 %shard_map.59 = (f32[1024,128]{1,0:T(8,128)S(1)}, f32[264,128]{1,0:T(8,128)S(1)}, f32[256,128]{1,0:T(8,128)S(1)}, f32[280,128]{1,0:T(8,128)S(1)}, f32[272,128]{1,0:T(8,128)S(1)}) custom-call(f32[8,128]{1,0:T(8,128)S(1)} %broadcast_in_dim.8.facts, f32[512,128]{1,0:T(8,128)S(1)} %collective-permute-done.4.below, f32[512,128]{1,0:T(8,128)S(1)} %collective-permute-done.5.beside, ...), custom_call_target="tpu_custom_call" | custom-call | tf_op jit(solution)/shard_map/pallas_call | solution.py:522
  14.6 1.2 %collective-permute-start.8 = (f32[280,128]{1,0:T(8,128)S(1)}, f32[280,128]{1,0:T(8,128)S(1)}, u32[]{:S(2)}, u32[]{:S(2)}) collective-permute-start(f32[280,128]{1,0:T(8,128)S(1)} %get-tuple-element.137.yc.rest_2_), channel_id=1, source_target_pairs={{0,1},{1,0},{2,3},{3,2},{4,5},{5,4},{6,7},{7,6},{8,9},{9,8},{10,11... | collective-permute-start | bytes 430088 | tf_op jit(solution)/shard_map/ppermute | solution.py:439
  15.8 3.5 %collective-permute-start.9 = (f32[272,128]{1,0:T(8,128)S(1)}, f32[272,128]{1,0:T(8,128)S(1)}, u32[]{:S(2)}, u32[]{:S(2)}) collective-permute-start(f32[272,128]{1,0:T(8,128)S(1)} %get-tuple-element.138.yd.rest_3_), channel_id=1, source_target_pairs={{1,2},{2,1},{3,4},{4,3},{5,6},{6,5},{7,0},{0,7},{9,10},{10,9},{11,... | collective-permute-start | bytes 417800 | tf_op jit(solution)/shard_map/ppermute | solution.py:439
  19.3 0.7 %collective-permute-start.6 = (f32[264,128]{1,0:T(8,128)S(1)}, f32[264,128]{1,0:T(8,128)S(1)}, u32[]{:S(2)}, u32[]{:S(2)}) collective-permute-start(f32[264,128]{1,0:T(8,128)S(1)} %get-tuple-element.135.ya.rest_0_), channel_id=1, source_target_pairs={{0,8},{8,0},{16,24},{24,16},{1,9},{9,1},{17,25},{25,17},{2,10},{10... | collective-permute-start | bytes 405512 | tf_op jit(solution)/shard_map/ppermute | solution.py:439
  20.0 0.9 %collective-permute-start.7 = (f32[256,128]{1,0:T(8,128)S(1)}, f32[256,128]{1,0:T(8,128)S(1)}, u32[]{:S(2)}, u32[]{:S(2)}) collective-permute-start(f32[256,128]{1,0:T(8,128)S(1)} %get-tuple-element.136.yb.rest_1_), channel_id=1, source_target_pairs={{8,16},{16,8},{24,0},{0,24},{9,17},{17,9},{25,1},{1,25},{10,18},{1... | collective-permute-start | bytes 393224 | tf_op jit(solution)/shard_map/ppermute | solution.py:439
  20.9 4.7 %collective-permute-done.7.rb = f32[256,128]{1,0:T(8,128)S(1)} collective-permute-done((f32[256,128]{1,0:T(8,128)S(1)}, f32[256,128]{1,0:T(8,128)S(1)}, u32[]{:S(2)}, u32[]{:S(2)}) %collective-permute-start.7) | collective-permute-done | bytes 131104 | tf_op jit(solution)/shard_map/ppermute | solution.py:439
  25.6 0.0 collective-permute-done.6.ra
  25.6 1.3 %shard_map.60 = (f32[1024,128]{1,0:T(8,128)S(1)}, f32[264,128]{1,0:T(8,128)S(1)}, f32[256,128]{1,0:T(8,128)S(1)}, f32[280,128]{1,0:T(8,128)S(1)}, f32[272,128]{1,0:T(8,128)S(1)}) custom-call(f32[8,128]{1,0:T(8,128)S(1)} %broadcast_in_dim.8.facts, f32[264,128]{1,0:T(8,128)S(1)} %get-tuple-element.135.ya.rest_0_, ...), custom_call_target="tpu_custom_call" | custom-call | tf_op jit(solution)/shard_map/pallas_call | solution.py:522
  26.9 0.1 collective-permute-start.12
  27.0 3.0 %collective-permute-start.13 = (f32[272,128]{1,0:T(8,128)S(1)}, f32[272,128]{1,0:T(8,128)S(1)}, u32[]{:S(2)}, u32[]{:S(2)}) collective-permute-start(f32[272,128]{1,0:T(8,128)S(1)} %get-tuple-element.143.yd.rest_7_), channel_id=1, source_target_pairs={{1,2},{2,1},{3,4},{4,3},{5,6},{6,5},{7,0},{0,7},{9,10},{10,9},{11,... | collective-permute-start | bytes 417800 | tf_op jit(solution)/shard_map/ppermute | solution.py:439
  30.0 1.2 %collective-permute-start.11 = (f32[256,128]{1,0:T(8,128)S(1)}, f32[256,128]{1,0:T(8,128)S(1)}, u32[]{:S(2)}, u32[]{:S(2)}) collective-permute-start(f32[256,128]{1,0:T(8,128)S(1)} %get-tuple-element.141.yb.rest_5_), channel_id=1, source_target_pairs={{8,16},{16,8},{24,0},{0,24},{9,17},{17,9},{25,1},{1,25},{10,18},{1... | collective-permute-start | bytes 393224 | tf_op jit(solution)/shard_map/ppermute | solution.py:439
  31.2 3.9 %collective-permute-done.11.rb = f32[256,128]{1,0:T(8,128)S(1)} collective-permute-done((f32[256,128]{1,0:T(8,128)S(1)}, f32[256,128]{1,0:T(8,128)S(1)}, u32[]{:S(2)}, u32[]{:S(2)}) %collective-permute-start.11) | collective-permute-done | bytes 131104 | tf_op jit(solution)/shard_map/ppermute | solution.py:439
  35.1 0.4 collective-permute-done.13.rd
  35.5 0.2 collective-permute-done.12.rc
  35.7 1.8 %shard_map.61 = (f32[1024,128]{1,0:T(8,128)S(1)}, f32[264,128]{1,0:T(8,128)S(1)}, f32[256,128]{1,0:T(8,128)S(1)}, f32[280,128]{1,0:T(8,128)S(1)}, f32[272,128]{1,0:T(8,128)S(1)}) custom-call(f32[8,128]{1,0:T(8,128)S(1)} %broadcast_in_dim.8.facts, f32[264,128]{1,0:T(8,128)S(1)} %get-tuple-element.140.ya.rest_4_, ...), custom_call_target="tpu_custom_call" | custom-call | tf_op jit(solution)/shard_map/pallas_call | solution.py:522
  37.6 0.3 collective-permute-start.16
  37.9 2.9 %collective-permute-start.17 = (f32[272,128]{1,0:T(8,128)S(1)}, f32[272,128]{1,0:T(8,128)S(1)}, u32[]{:S(2)}, u32[]{:S(2)}) collective-permute-start(f32[272,128]{1,0:T(8,128)S(1)} %get-tuple-element.148.rest_11_.yd), channel_id=1, source_target_pairs={{1,2},{2,1},{3,4},{4,3},{5,6},{6,5},{7,0},{0,7},{9,10},{10,9},{11,... | collective-permute-start | bytes 417800 | tf_op jit(solution)/shard_map/ppermute | solution.py:439
  40.9 0.4 collective-permute-start.15
  41.3 1.0 %shard_map.62.rest_8_ = f32[16,128]{1,0:T(8,128)S(1)} custom-call(f32[1024,128]{1,0:T(8,128)S(1)} %get-tuple-element.134.u0, f32[1024,128]{1,0:T(8,128)S(1)} %get-tuple-element.139.u1, f32[1024,128]{1,0:T(8,128)S(1)} %get-tuple-element.144.u2, f32[264,128]{1,0:T(8,128)S(1)} %get-tuple-element.135.ya.rest_0_, f32[256,128]{1,0:T(8,128)S(1)} %get-tuple-element.136.yb.rest_1_, ...), custom_call_target="tpu_custom_call" | custom-call | tf_op jit(solution)/shard_map/pallas_call | solution.py:522
  42.3 3.7 %collective-permute-done.15.rb = f32[256,128]{1,0:T(8,128)S(1)} collective-permute-done((f32[256,128]{1,0:T(8,128)S(1)}, f32[256,128]{1,0:T(8,128)S(1)}, u32[]{:S(2)}, u32[]{:S(2)}) %collective-permute-start.15) | collective-permute-done | bytes 131104 | tf_op jit(solution)/shard_map/ppermute | solution.py:439
  46.0 0.2 collective-permute-done.17.rd
  46.2 0.2 collective-permute-done.16.rc
  46.4 2.5 %shard_map.63 = (f32[1024,128]{1,0:T(8,128)S(1)}, f32[256,128]{1,0:T(8,128)S(1)}, f32[256,128]{1,0:T(8,128)S(1)}, f32[512,128]{1,0:T(8,128)S(1)}, f32[24,128]{1,0:T(8,128)S(1)}) custom-call(f32[8,128]{1,0:T(8,128)S(1)} %broadcast_in_dim.8.facts, f32[264,128]{1,0:T(8,128)S(1)} %get-tuple-element.145.rest_8_.ya, f32[256,128]{1,0:T(8,128)S(1)} %get-tuple-element.146.rest_9_.yb, ...), custom_call_target="tpu_custom_call" | custom-call | tf_op jit(solution)/shard_map/pallas_call | solution.py:522
  48.9 0.2 collective-permute-start.20
  49.1 1.0 %collective-permute-done.20.refs_1_ = f32[24,128]{1,0:T(8,128)S(1)} collective-permute-done((f32[24,128]{1,0:T(8,128)S(1)}, f32[24,128]{1,0:T(8,128)S(1)}, u32[]{:S(2)}, u32[]{:S(2)}) %collective-permute-start.20) | collective-permute-done | bytes 12320 | tf_op jit(solution)/shard_map/ppermute | solution.py:455
  50.2 0.7 %collective-permute-start.21 = (f32[24,128]{1,0:T(8,128)S(1)}, f32[24,128]{1,0:T(8,128)S(1)}, u32[]{:S(2)}, u32[]{:S(2)}) collective-permute-start(f32[24,128]{1,0:T(8,128)S(1)} %shard_map.64.refs_0_), channel_id=1, source_target_pairs={{0,17},{1,16},{2,19},{3,18},{4,21},{5,20},{6,23},{7,22},{8,25},{9,... | collective-permute-start | bytes 36872 | tf_op jit(solution)/shard_map/ppermute | solution.py:455
  50.9 1.7 %collective-permute-start.22 = (f32[24,128]{1,0:T(8,128)S(1)}, f32[24,128]{1,0:T(8,128)S(1)}, u32[]{:S(2)}, u32[]{:S(2)}) collective-permute-start(f32[24,128]{1,0:T(8,128)S(1)} %shard_map.64.refs_0_), channel_id=1, source_target_pairs={{0,1},{1,0},{2,3},{3,2},{4,5},{5,4},{6,7},{7,6},{8,9},{9,8},{10,11... | collective-permute-start | bytes 36872 | tf_op jit(solution)/shard_map/ppermute | solution.py:455
  52.6 1.2 %collective-permute-start.23 = (f32[24,128]{1,0:T(8,128)S(1)}, f32[24,128]{1,0:T(8,128)S(1)}, u32[]{:S(2)}, u32[]{:S(2)}) collective-permute-start(f32[24,128]{1,0:T(8,128)S(1)} %shard_map.64.refs_0_), channel_id=1, source_target_pairs={{0,16},{1,17},{2,18},{3,19},{4,20},{5,21},{6,22},{7,23},{8,24},{9,... | collective-permute-start | bytes 36872 | tf_op jit(solution)/shard_map/ppermute | solution.py:455
  53.8 2.2 %collective-permute-start.19 = (f32[256,128]{1,0:T(8,128)S(1)}, f32[256,128]{1,0:T(8,128)S(1)}, u32[]{:S(2)}, u32[]{:S(2)}) collective-permute-start(f32[256,128]{1,0:T(8,128)S(1)} %get-tuple-element.153), channel_id=1, source_target_pairs={{0,7},{1,0},{2,1},{3,2},{4,3},{5,4},{6,5},{7,6},{8,15},{9,8},{10,9... | collective-permute-start | bytes 393224 | tf_op jit(solution)/shard_map/ppermute | solution.py:429
  56.0 0.3 collective-permute-done.23.refs_3_
  56.3 0.1 shard_map.65.rest_0_
  56.4 0.0 copy-start.2
  56.4 0.8 %collective-permute-start.24 = (f32[24,128]{1,0:T(8,128)S(1)}, f32[24,128]{1,0:T(8,128)S(1)}, u32[]{:S(2)}, u32[]{:S(2)}) collective-permute-start(f32[24,128]{1,0:T(8,128)S(1)} %shard_map.65.rest_0_), channel_id=1, source_target_pairs={{0,6},{1,7},{2,4},{3,5},{4,2},{5,3},{6,0},{7,1},{8,14},{9,15},{10,... | collective-permute-start | bytes 36872 | tf_op jit(solution)/shard_map/ppermute | solution.py:455
  57.2 0.5 collective-permute-start.25
  57.8 3.1 %collective-permute-start.26 = (f32[24,128]{1,0:T(8,128)S(1)}, f32[24,128]{1,0:T(8,128)S(1)}, u32[]{:S(2)}, u32[]{:S(2)}) collective-permute-start(f32[24,128]{1,0:T(8,128)S(1)} %shard_map.65.rest_0_), channel_id=1, source_target_pairs={{0,2},{1,3},{2,0},{3,1},{4,6},{5,7},{6,4},{7,5},{8,10},{9,11},{10,... | collective-permute-start | bytes 36872 | tf_op jit(solution)/shard_map/ppermute | solution.py:455
  60.9 0.8 %copy.8 = f32[512,128]{0,1:T(8,128)} copy(f32[512,128]{1,0:T(8,128)S(1)} %bitcast.50) | data formatting | bytes 524288 | tf_op jit(solution)/shard_map/while | solution.py:590
  61.7 0.3 collective-permute-done.24.rest_1_
  62.0 0.5 collective-permute-done.26.rest_3_
  62.5 1.3 %shard_map.66 = (f32[512,128]{1,0:T(8,128)}, f32[512,128]{1,0:T(8,128)}, s32[1,1]{1,0:T(1,128)}) custom-call(f32[8,128]{1,0:T(8,128)S(1)} %broadcast_in_dim.8.facts, f32[1024,128]{1,0:T(8,128)S(1)} %get-tuple-element.134.u0, f32[1024,128]{1,0:T(8,128)S(1)} %get-tuple-element.139.u1, f32[1024,128]{1,0:T(8,128)S(1)} %get-tuple-element.144.u2, ...), custom_call_target="tpu_custom_call" | custom-call | tf_op jit(solution)/shard_map/pallas_call | solution.py:535
  63.8 0.7 %while.28 = (f32[512,128]{1,0:T(8,128)}, f32[512,128]{1,0:T(8,128)}, s32[]{:T(128)}, f32[512,128]{0,1:T(8,128)}, s32[]{:T(128)}, /*index=5*/f32[1,1,1024,1024]{3...) while((f32[512,128]{1,0:T(8,128)}, f32[512,128]{1,0:T(8,128)}, s32[]{:T(128)}, ...), condition=%region_9.10_spmd, body=%region_0.9_spmd | while | flops 3762094080 | bytes 49572704 | solution.py:590
  (18 shorter events, 0.1 us)
Async XLA Ops:
  0.6 12.2 %collective-permute-start.4 = (f32[512,128]{1,0:T(8,128)}, f32[512,128]{1,0:T(8,128)S(1)}, u32[]{:S(2)}, u32[]{:S(2)}) collective-permute-start(f32[512,128]{1,0:T(8,128)} %bitcast.47), channel_id=1, source_target_pairs={{0,8},{8,16},{16,24},{24,0},{1,9},{9,17},{17,25},{25,1},{2,10},{10... | collective-permute-start | bytes 786440 | tf_op jit(solution)/shard_map/ppermute | solution.py:429
  1.1 12.1 %collective-permute-start.5 = (f32[512,128]{1,0:T(8,128)}, f32[512,128]{1,0:T(8,128)S(1)}, u32[]{:S(2)}, u32[]{:S(2)}) collective-permute-start(f32[512,128]{1,0:T(8,128)} %bitcast.48), channel_id=1, source_target_pairs={{0,1},{1,2},{2,3},{3,4},{4,5},{5,6},{6,7},{7,0},{8,9},{9,10},{10,1... | collective-permute-start | bytes 786440 | tf_op jit(solution)/shard_map/ppermute | solution.py:429
  3.9 9.4 %copy-start = (f32[1,1,2,256,128]{4,3,2,1,0:T(8,128)S(1)}, f32[1,1,2,256,128]{4,3,2,1,0:T(8,128)}, u32[]{:S(2)}) copy-start(f32[1,1,2,256,128]{4,3,2,1,0:T(8,128)} %param.8) | copy-start | bytes 786436
  14.6 11.0 %collective-permute-start.8 = (f32[280,128]{1,0:T(8,128)S(1)}, f32[280,128]{1,0:T(8,128)S(1)}, u32[]{:S(2)}, u32[]{:S(2)}) collective-permute-start(f32[280,128]{1,0:T(8,128)S(1)} %get-tuple-element.137.yc.rest_2_), channel_id=1, source_target_pairs={{0,1},{1,0},{2,3},{3,2},{4,5},{5,4},{6,7},{7,6},{8,9},{9,8},{10,11... | collective-permute-start | bytes 430088 | tf_op jit(solution)/shard_map/ppermute | solution.py:439
  15.8 9.9 %collective-permute-start.9 = (f32[272,128]{1,0:T(8,128)S(1)}, f32[272,128]{1,0:T(8,128)S(1)}, u32[]{:S(2)}, u32[]{:S(2)}) collective-permute-start(f32[272,128]{1,0:T(8,128)S(1)} %get-tuple-element.138.yd.rest_3_), channel_id=1, source_target_pairs={{1,2},{2,1},{3,4},{4,3},{5,6},{6,5},{7,0},{0,7},{9,10},{10,9},{11,... | collective-permute-start | bytes 417800 | tf_op jit(solution)/shard_map/ppermute | solution.py:439
  19.3 6.3 %collective-permute-start.6 = (f32[264,128]{1,0:T(8,128)S(1)}, f32[264,128]{1,0:T(8,128)S(1)}, u32[]{:S(2)}, u32[]{:S(2)}) collective-permute-start(f32[264,128]{1,0:T(8,128)S(1)} %get-tuple-element.135.ya.rest_0_), channel_id=1, source_target_pairs={{0,8},{8,0},{16,24},{24,16},{1,9},{9,1},{17,25},{25,17},{2,10},{10... | collective-permute-start | bytes 405512 | tf_op jit(solution)/shard_map/ppermute | solution.py:439
  20.0 5.6 %collective-permute-start.7 = (f32[256,128]{1,0:T(8,128)S(1)}, f32[256,128]{1,0:T(8,128)S(1)}, u32[]{:S(2)}, u32[]{:S(2)}) collective-permute-start(f32[256,128]{1,0:T(8,128)S(1)} %get-tuple-element.136.yb.rest_1_), channel_id=1, source_target_pairs={{8,16},{16,8},{24,0},{0,24},{9,17},{17,9},{25,1},{1,25},{10,18},{1... | collective-permute-start | bytes 393224 | tf_op jit(solution)/shard_map/ppermute | solution.py:439
  26.9 8.8 %collective-permute-start.12 = (f32[280,128]{1,0:T(8,128)S(1)}, f32[280,128]{1,0:T(8,128)S(1)}, u32[]{:S(2)}, u32[]{:S(2)}) collective-permute-start(f32[280,128]{1,0:T(8,128)S(1)} %get-tuple-element.142.yc.rest_6_), channel_id=1, source_target_pairs={{0,1},{1,0},{2,3},{3,2},{4,5},{5,4},{6,7},{7,6},{8,9},{9,8},{10,11... | collective-permute-start | bytes 430088 | tf_op jit(solution)/shard_map/ppermute | solution.py:439
  27.0 8.6 %collective-permute-start.13 = (f32[272,128]{1,0:T(8,128)S(1)}, f32[272,128]{1,0:T(8,128)S(1)}, u32[]{:S(2)}, u32[]{:S(2)}) collective-permute-start(f32[272,128]{1,0:T(8,128)S(1)} %get-tuple-element.143.yd.rest_7_), channel_id=1, source_target_pairs={{1,2},{2,1},{3,4},{4,3},{5,6},{6,5},{7,0},{0,7},{9,10},{10,9},{11,... | collective-permute-start | bytes 417800 | tf_op jit(solution)/shard_map/ppermute | solution.py:439
  30.0 5.2 %collective-permute-start.10 = (f32[264,128]{1,0:T(8,128)S(1)}, f32[264,128]{1,0:T(8,128)S(1)}, u32[]{:S(2)}, u32[]{:S(2)}) collective-permute-start(f32[264,128]{1,0:T(8,128)S(1)} %get-tuple-element.140.ya.rest_4_), channel_id=1, source_target_pairs={{0,8},{8,0},{16,24},{24,16},{1,9},{9,1},{17,25},{25,17},{2,10},{10... | collective-permute-start | bytes 405512 | tf_op jit(solution)/shard_map/ppermute | solution.py:439
  30.0 5.2 %collective-permute-start.11 = (f32[256,128]{1,0:T(8,128)S(1)}, f32[256,128]{1,0:T(8,128)S(1)}, u32[]{:S(2)}, u32[]{:S(2)}) collective-permute-start(f32[256,128]{1,0:T(8,128)S(1)} %get-tuple-element.141.yb.rest_5_), channel_id=1, source_target_pairs={{8,16},{16,8},{24,0},{0,24},{9,17},{17,9},{25,1},{1,25},{10,18},{1... | collective-permute-start | bytes 393224 | tf_op jit(solution)/shard_map/ppermute | solution.py:439
  37.6 8.8 %collective-permute-start.16 = (f32[280,128]{1,0:T(8,128)S(1)}, f32[280,128]{1,0:T(8,128)S(1)}, u32[]{:S(2)}, u32[]{:S(2)}) collective-permute-start(f32[280,128]{1,0:T(8,128)S(1)} %get-tuple-element.147.rest_10_.yc), channel_id=1, source_target_pairs={{0,1},{1,0},{2,3},{3,2},{4,5},{5,4},{6,7},{7,6},{8,9},{9,8},{10,11... | collective-permute-start | bytes 430088 | tf_op jit(solution)/shard_map/ppermute | solution.py:439
  37.9 8.3 %collective-permute-start.17 = (f32[272,128]{1,0:T(8,128)S(1)}, f32[272,128]{1,0:T(8,128)S(1)}, u32[]{:S(2)}, u32[]{:S(2)}) collective-permute-start(f32[272,128]{1,0:T(8,128)S(1)} %get-tuple-element.148.rest_11_.yd), channel_id=1, source_target_pairs={{1,2},{2,1},{3,4},{4,3},{5,6},{6,5},{7,0},{0,7},{9,10},{10,9},{11,... | collective-permute-start | bytes 417800 | tf_op jit(solution)/shard_map/ppermute | solution.py:439
  40.8 5.2 %collective-permute-start.14 = (f32[264,128]{1,0:T(8,128)S(1)}, f32[264,128]{1,0:T(8,128)S(1)}, u32[]{:S(2)}, u32[]{:S(2)}) collective-permute-start(f32[264,128]{1,0:T(8,128)S(1)} %get-tuple-element.145.rest_8_.ya), channel_id=1, source_target_pairs={{0,8},{8,0},{16,24},{24,16},{1,9},{9,1},{17,25},{25,17},{2,10},{10... | collective-permute-start | bytes 405512 | tf_op jit(solution)/shard_map/ppermute | solution.py:439
  40.9 5.2 %collective-permute-start.15 = (f32[256,128]{1,0:T(8,128)S(1)}, f32[256,128]{1,0:T(8,128)S(1)}, u32[]{:S(2)}, u32[]{:S(2)}) collective-permute-start(f32[256,128]{1,0:T(8,128)S(1)} %get-tuple-element.146.rest_9_.yb), channel_id=1, source_target_pairs={{8,16},{16,8},{24,0},{0,24},{9,17},{17,9},{25,1},{1,25},{10,18},{1... | collective-permute-start | bytes 393224 | tf_op jit(solution)/shard_map/ppermute | solution.py:439
  48.9 1.2 %collective-permute-start.20 = (f32[24,128]{1,0:T(8,128)S(1)}, f32[24,128]{1,0:T(8,128)S(1)}, u32[]{:S(2)}, u32[]{:S(2)}) collective-permute-start(f32[24,128]{1,0:T(8,128)S(1)} %get-tuple-element.154.refs_0_), channel_id=1, source_target_pairs={{0,8},{1,9},{2,10},{3,11},{4,12},{5,13},{6,14},{7,15},{8,0},{9,1},... | collective-permute-start | bytes 36872 | tf_op jit(solution)/shard_map/ppermute | solution.py:455
  50.2 5.8 %collective-permute-start.21 = (f32[24,128]{1,0:T(8,128)S(1)}, f32[24,128]{1,0:T(8,128)S(1)}, u32[]{:S(2)}, u32[]{:S(2)}) collective-permute-start(f32[24,128]{1,0:T(8,128)S(1)} %shard_map.64.refs_0_), channel_id=1, source_target_pairs={{0,17},{1,16},{2,19},{3,18},{4,21},{5,20},{6,23},{7,22},{8,25},{9,... | collective-permute-start | bytes 36872 | tf_op jit(solution)/shard_map/ppermute | solution.py:455
  50.9 5.2 %collective-permute-start.22 = (f32[24,128]{1,0:T(8,128)S(1)}, f32[24,128]{1,0:T(8,128)S(1)}, u32[]{:S(2)}, u32[]{:S(2)}) collective-permute-start(f32[24,128]{1,0:T(8,128)S(1)} %shard_map.64.refs_0_), channel_id=1, source_target_pairs={{0,1},{1,0},{2,3},{3,2},{4,5},{5,4},{6,7},{7,6},{8,9},{9,8},{10,11... | collective-permute-start | bytes 36872 | tf_op jit(solution)/shard_map/ppermute | solution.py:455
  52.6 3.7 %collective-permute-start.23 = (f32[24,128]{1,0:T(8,128)S(1)}, f32[24,128]{1,0:T(8,128)S(1)}, u32[]{:S(2)}, u32[]{:S(2)}) collective-permute-start(f32[24,128]{1,0:T(8,128)S(1)} %shard_map.64.refs_0_), channel_id=1, source_target_pairs={{0,16},{1,17},{2,18},{3,19},{4,20},{5,21},{6,22},{7,23},{8,24},{9,... | collective-permute-start | bytes 36872 | tf_op jit(solution)/shard_map/ppermute | solution.py:455
  53.8 8.8 %collective-permute-start.18 = (f32[256,128]{1,0:T(8,128)S(1)}, f32[256,128]{1,0:T(8,128)S(1)}, u32[]{:S(2)}, u32[]{:S(2)}) collective-permute-start(f32[256,128]{1,0:T(8,128)S(1)} %get-tuple-element.152), channel_id=1, source_target_pairs={{0,24},{8,0},{16,8},{24,16},{1,25},{9,1},{17,9},{25,17},{2,26},{10... | collective-permute-start | bytes 393224 | tf_op jit(solution)/shard_map/ppermute | solution.py:429
  53.8 8.8 %collective-permute-start.19 = (f32[256,128]{1,0:T(8,128)S(1)}, f32[256,128]{1,0:T(8,128)S(1)}, u32[]{:S(2)}, u32[]{:S(2)}) collective-permute-start(f32[256,128]{1,0:T(8,128)S(1)} %get-tuple-element.153), channel_id=1, source_target_pairs={{0,7},{1,0},{2,1},{3,2},{4,3},{5,4},{6,5},{7,6},{8,15},{9,8},{10,9... | collective-permute-start | bytes 393224 | tf_op jit(solution)/shard_map/ppermute | solution.py:429
  56.4 7.4 %copy-start.2 = (s32[1,1,8,8]{3,2,1,0:T(8,128)S(1)}, s32[1,1,8,8]{3,2,1,0:T(8,128)}, u32[]{:S(2)}) copy-start(s32[1,1,8,8]{3,2,1,0:T(8,128)} %param.11) | copy-start | bytes 772
  56.4 5.6 %collective-permute-start.24 = (f32[24,128]{1,0:T(8,128)S(1)}, f32[24,128]{1,0:T(8,128)S(1)}, u32[]{:S(2)}, u32[]{:S(2)}) collective-permute-start(f32[24,128]{1,0:T(8,128)S(1)} %shard_map.65.rest_0_), channel_id=1, source_target_pairs={{0,6},{1,7},{2,4},{3,5},{4,2},{5,3},{6,0},{7,1},{8,14},{9,15},{10,... | collective-permute-start | bytes 36872 | tf_op jit(solution)/shard_map/ppermute | solution.py:455
  57.2 4.8 %collective-permute-start.25 = (f32[24,128]{1,0:T(8,128)S(1)}, f32[24,128]{1,0:T(8,128)S(1)}, u32[]{:S(2)}, u32[]{:S(2)}) collective-permute-start(f32[24,128]{1,0:T(8,128)S(1)} %shard_map.65.rest_0_), channel_id=1, source_target_pairs={{0,4},{1,5},{2,6},{3,7},{4,0},{5,1},{6,2},{7,3},{8,12},{9,13},{10,... | collective-permute-start | bytes 36872 | tf_op jit(solution)/shard_map/ppermute | solution.py:455
  57.8 4.8 %collective-permute-start.26 = (f32[24,128]{1,0:T(8,128)S(1)}, f32[24,128]{1,0:T(8,128)S(1)}, u32[]{:S(2)}, u32[]{:S(2)}) collective-permute-start(f32[24,128]{1,0:T(8,128)S(1)} %shard_map.65.rest_0_), channel_id=1, source_target_pairs={{0,2},{1,3},{2,0},{3,1},{4,6},{5,7},{6,4},{7,5},{8,10},{9,11},{10,... | collective-permute-start | bytes 36872 | tf_op jit(solution)/shard_map/ppermute | solution.py:455

commit v6 on v5

--- a/solution.py
+++ b/solution.py
@@ -27,13 +27,15 @@
     return pltpu.CompilerParams(vmem_limit_bytes=mib << 20)
 
 
-def operator_kernel(info, pattern_hbm, w_hbm, n_hbm, g_ref, center_ref, pattern, w_buf, n_buf, sems, left, right, total):
+def operator_kernel(info_hbm, pattern_hbm, w_hbm, n_hbm, g_ref, center_ref, info, pattern, w_buf, n_buf, sems, left, right, total):
     size = w_buf.shape[1]
     face = size // 4
     nb = pattern.shape[0]
     blk = size // nb
     pattern_copy = pltpu.make_async_copy(pattern_hbm, pattern, sems.at[2, 0])
     pattern_copy.start()
+    info_copy = pltpu.make_async_copy(info_hbm, info, sems.at[2, 1])
+    info_copy.start()
 
     def fetch(k):
         rows = pl.ds(k * face, face)
@@ -82,6 +84,7 @@
     begin(0)
     begin(1)
     pattern_copy.wait()
+    info_copy.wait()
     prepare(0)
     for k in range(4):
         multiply(k)
@@ -90,7 +93,7 @@
 
     def put(i, j, block):
         def at(k):
-            return pl.multiple_of(info[k] * face, face)
+            return pl.multiple_of(info[0, k] * face, face)
 
         rows = pl.ds(at(i), face)
         high, low = halves(block)
@@ -116,10 +119,11 @@
     size = factor.shape[0]
     return pl.pallas_call(
         operator_kernel,
-        in_specs=[pl.BlockSpec(memory_space=pltpu.SMEM)] + [pl.BlockSpec(memory_space=pl.ANY)] * 3,
+        in_specs=[pl.BlockSpec(memory_space=pl.ANY)] * 4,
         out_specs=[pl.BlockSpec(memory_space=pltpu.VMEM)] * 2,
         out_shape=[jax.ShapeDtypeStruct((size, 2 * size), BF16), jax.ShapeDtypeStruct((8, cases), F32)],
         scratch_shapes=[
+            pltpu.SMEM(info.shape, jnp.int32),
             pltpu.SMEM(pattern.shape, jnp.int32),
             pltpu.VMEM((size, size), F32),
             pltpu.VMEM((size, size), BF16),
@@ -131,7 +135,7 @@
         compiler_params=params(32),
         name="operator",
     )(
-        info,
+        pltpu.with_memory_space_constraint(info, pltpu.HBM),
         pltpu.with_memory_space_constraint(pattern, pltpu.HBM),
         pltpu.with_memory_space_constraint(factor, pltpu.HBM),
         pltpu.with_memory_space_constraint(coupling, pltpu.HBM),
@@ -552,7 +556,7 @@
     keep_a = jnp.where(odd_floor == 0, has_above, has_below)
     keep_b = jnp.where(odd_floor == 0, has_below, has_above)
     flags = [1 - odd_floor, odd_floor, 3 - odd_facade, 2 + odd_facade, keep_a, keep_b, has_above, has_below, odd_floor, odd_facade]
-    info = jnp.stack(flags).astype(jnp.int32)
+    info = jnp.stack(flags).astype(jnp.int32).reshape(1, -1)
     facts = jnp.stack(flags[KEEP:] + [0] * (8 - len(flags[KEEP:]))).astype(F32)
     facts = jnp.broadcast_to(facts[:, None], (8, cases))
     rhs = interface_rhs.reshape(2 * face, cases)

time: 64.8 us -> 64.9 us (level)
  no operation moved by 1% of the time
where the time goes in v6:
time: 64.9 us; the launch traced here: 64.7 us
  starting transfers between devices  27.9 us (43%)
  Pallas kernels  17.7 us (27%)
  waiting for transfers between devices  16 us (25%)
  local copies, waits for them, and re-layouts  1.67 us (3%)
  between operations  0.9 us (1%)
  loops' own time  0.68 us (1%)
    ppermute x12, starting transfers between devices, swapped(): return lax.ppermute(value, axis, pairs)  14.3 us
    ppermute x12, waiting for transfers between devices, swapped(): return lax.ppermute(value, axis, pairs)  13.4 us
    pallas_call x1, Pallas kernels, build_operator(): pl.pallas_call(operator_kernel, in_specs=[pl.BlockSpec(memory_space=pl.AN...  8.41 us
    ppermute x7, starting transfers between devices, flipped(): return lax.ppermute(value, AXES, pairs)  8.21 us
    pallas_call x7, Pallas kernels, call(): pl.pallas_call(kernel, in_specs=[pl.BlockSpec(memory_space=pltpu.SMEM)] *...  7.99 us
    ppermute x4, starting transfers between devices, upward(): return lax.ppermute(value, axis, pairs)  5.31 us
    ppermute x7, waiting for transfers between devices, flipped(): return lax.ppermute(value, AXES, pairs)  2.17 us
  transfers between devices with their start and end apart: 23, of which 12 were waited for; matrix products, arithmetic and copies ran while one was open for 2% of the time, Pallas kernels for 15%

profile of v6, /device:TPU:0, one launch (start us, length us, event | category | flops | bytes accessed | tf_op | source)
XLA Modules:
  0.0 64.7 jit_solution(5146132958899635821)
XLA Ops:
  0.6 0.5 collective-permute-start.4
  1.1 2.6 %collective-permute-start.5 = (f32[512,128]{1,0:T(8,128)}, f32[512,128]{1,0:T(8,128)S(1)}, u32[]{:S(2)}, u32[]{:S(2)}) collective-permute-start(f32[512,128]{1,0:T(8,128)} %bitcast.49), channel_id=1, source_target_pairs={{0,1},{1,2},{2,3},{3,4},{4,5},{5,6},{6,7},{7,0},{8,9},{9,10},{10,1... | collective-permute-start | bytes 786440 | tf_op jit(solution)/shard_map/ppermute | solution.py:433
  3.7 0.1 stack.49
  3.8 0.7 %stack.53 = s32[10]{0:T(128)} concatenate(s32[1]{0:T(128)} %bitcast.11, s32[1]{0:T(128)} %bitcast.8, s32[1]{0:T(128)} %bitcast.12, s32[1]{0:T(128)} %bitcast.13, s32[1]{0:T(128)} %bitcast.4, s32[1]{0:T(128)} %bitcast.5, s32[1]{0:T(128)} %bitcast.6, s32[1]{0:T(128)} %bitcast.7, s32[1]{0:T(128)} %bitcast.8, s32[1]{0:T(128)} %bitcast.9), dimensions={0} | concatenate | bytes 80 | tf_op jit(solution)/shard_map/stack | solution.py:559
  4.5 8.4 %operator.1 = (bf16[1024,2048]{1,0:T(8,128)(2,1)S(1)}, f32[8,128]{1,0:T(8,128)S(1)}) custom-call(s32[1,10]{1,0:T(1,128)} %bitcast.59, s32[8,8]{1,0:T(8,128)} %bitcast.58, f32[1024,1024]{1,0:T(8,128)} %bitcast.52, bf16[1024,1024]{1,0:T(8,128)(2,1)} %bitcast.56), custom_call_target="tpu_custom_call" | custom-call | tf_op jit(solution)/shard_map/operator/pallas_call | solution.py:120
  12.9 0.0 collective-permute-done.4.below
  12.9 0.4 collective-permute-done.5.beside
  13.3 0.1 broadcast_in_dim.8.facts
  13.3 1.3 %shard_map.59 = (f32[1024,128]{1,0:T(8,128)S(1)}, f32[264,128]{1,0:T(8,128)S(1)}, f32[256,128]{1,0:T(8,128)S(1)}, f32[280,128]{1,0:T(8,128)S(1)}, f32[272,128]{1,0:T(8,128)S(1)}) custom-call(f32[8,128]{1,0:T(8,128)S(1)} %broadcast_in_dim.8.facts, f32[512,128]{1,0:T(8,128)S(1)} %collective-permute-done.4.below, f32[512,128]{1,0:T(8,128)S(1)} %collective-permute-done.5.beside, ...), custom_call_target="tpu_custom_call" | custom-call | tf_op jit(solution)/shard_map/pallas_call | solution.py:526
  14.6 1.2 %collective-permute-start.8 = (f32[280,128]{1,0:T(8,128)S(1)}, f32[280,128]{1,0:T(8,128)S(1)}, u32[]{:S(2)}, u32[]{:S(2)}) collective-permute-start(f32[280,128]{1,0:T(8,128)S(1)} %get-tuple-element.137.yc.rest_2_), channel_id=1, source_target_pairs={{0,1},{1,0},{2,3},{3,2},{4,5},{5,4},{6,7},{7,6},{8,9},{9,8},{10,11... | collective-permute-start | bytes 430088 | tf_op jit(solution)/shard_map/ppermute | solution.py:443
  15.8 3.6 %collective-permute-start.9 = (f32[272,128]{1,0:T(8,128)S(1)}, f32[272,128]{1,0:T(8,128)S(1)}, u32[]{:S(2)}, u32[]{:S(2)}) collective-permute-start(f32[272,128]{1,0:T(8,128)S(1)} %get-tuple-element.138.yd.rest_3_), channel_id=1, source_target_pairs={{1,2},{2,1},{3,4},{4,3},{5,6},{6,5},{7,0},{0,7},{9,10},{10,9},{11,... | collective-permute-start | bytes 417800 | tf_op jit(solution)/shard_map/ppermute | solution.py:443
  19.4 0.7 %collective-permute-start.6 = (f32[264,128]{1,0:T(8,128)S(1)}, f32[264,128]{1,0:T(8,128)S(1)}, u32[]{:S(2)}, u32[]{:S(2)}) collective-permute-start(f32[264,128]{1,0:T(8,128)S(1)} %get-tuple-element.135.ya.rest_0_), channel_id=1, source_target_pairs={{0,8},{8,0},{16,24},{24,16},{1,9},{9,1},{17,25},{25,17},{2,10},{10... | collective-permute-start | bytes 405512 | tf_op jit(solution)/shard_map/ppermute | solution.py:443
  20.1 0.9 %collective-permute-start.7 = (f32[256,128]{1,0:T(8,128)S(1)}, f32[256,128]{1,0:T(8,128)S(1)}, u32[]{:S(2)}, u32[]{:S(2)}) collective-permute-start(f32[256,128]{1,0:T(8,128)S(1)} %get-tuple-element.136.yb.rest_1_), channel_id=1, source_target_pairs={{8,16},{16,8},{24,0},{0,24},{9,17},{17,9},{25,1},{1,25},{10,18},{1... | collective-permute-start | bytes 393224 | tf_op jit(solution)/shard_map/ppermute | solution.py:443
  21.0 4.7 %collective-permute-done.7.rb = f32[256,128]{1,0:T(8,128)S(1)} collective-permute-done((f32[256,128]{1,0:T(8,128)S(1)}, f32[256,128]{1,0:T(8,128)S(1)}, u32[]{:S(2)}, u32[]{:S(2)}) %collective-permute-start.7) | collective-permute-done | bytes 131104 | tf_op jit(solution)/shard_map/ppermute | solution.py:443
  25.7 0.0 collective-permute-done.6.ra
  25.7 1.3 %shard_map.60 = (f32[1024,128]{1,0:T(8,128)S(1)}, f32[264,128]{1,0:T(8,128)S(1)}, f32[256,128]{1,0:T(8,128)S(1)}, f32[280,128]{1,0:T(8,128)S(1)}, f32[272,128]{1,0:T(8,128)S(1)}) custom-call(f32[8,128]{1,0:T(8,128)S(1)} %broadcast_in_dim.8.facts, f32[264,128]{1,0:T(8,128)S(1)} %get-tuple-element.135.ya.rest_0_, ...), custom_call_target="tpu_custom_call" | custom-call | tf_op jit(solution)/shard_map/pallas_call | solution.py:526
  27.0 0.1 collective-permute-start.12
  27.1 3.0 %collective-permute-start.13 = (f32[272,128]{1,0:T(8,128)S(1)}, f32[272,128]{1,0:T(8,128)S(1)}, u32[]{:S(2)}, u32[]{:S(2)}) collective-permute-start(f32[272,128]{1,0:T(8,128)S(1)} %get-tuple-element.143.yd.rest_7_), channel_id=1, source_target_pairs={{1,2},{2,1},{3,4},{4,3},{5,6},{6,5},{7,0},{0,7},{9,10},{10,9},{11,... | collective-permute-start | bytes 417800 | tf_op jit(solution)/shard_map/ppermute | solution.py:443
  30.1 1.2 %collective-permute-start.11 = (f32[256,128]{1,0:T(8,128)S(1)}, f32[256,128]{1,0:T(8,128)S(1)}, u32[]{:S(2)}, u32[]{:S(2)}) collective-permute-start(f32[256,128]{1,0:T(8,128)S(1)} %get-tuple-element.141.yb.rest_5_), channel_id=1, source_target_pairs={{8,16},{16,8},{24,0},{0,24},{9,17},{17,9},{25,1},{1,25},{10,18},{1... | collective-permute-start | bytes 393224 | tf_op jit(solution)/shard_map/ppermute | solution.py:443
  31.3 3.9 %collective-permute-done.11.rb = f32[256,128]{1,0:T(8,128)S(1)} collective-permute-done((f32[256,128]{1,0:T(8,128)S(1)}, f32[256,128]{1,0:T(8,128)S(1)}, u32[]{:S(2)}, u32[]{:S(2)}) %collective-permute-start.11) | collective-permute-done | bytes 131104 | tf_op jit(solution)/shard_map/ppermute | solution.py:443
  35.2 0.4 collective-permute-done.13.rd
  35.6 0.2 collective-permute-done.12.rc
  35.8 1.8 %shard_map.61 = (f32[1024,128]{1,0:T(8,128)S(1)}, f32[264,128]{1,0:T(8,128)S(1)}, f32[256,128]{1,0:T(8,128)S(1)}, f32[280,128]{1,0:T(8,128)S(1)}, f32[272,128]{1,0:T(8,128)S(1)}) custom-call(f32[8,128]{1,0:T(8,128)S(1)} %broadcast_in_dim.8.facts, f32[264,128]{1,0:T(8,128)S(1)} %get-tuple-element.140.ya.rest_4_, ...), custom_call_target="tpu_custom_call" | custom-call | tf_op jit(solution)/shard_map/pallas_call | solution.py:526
  37.7 0.3 collective-permute-start.16
  38.0 2.9 %collective-permute-start.17 = (f32[272,128]{1,0:T(8,128)S(1)}, f32[272,128]{1,0:T(8,128)S(1)}, u32[]{:S(2)}, u32[]{:S(2)}) collective-permute-start(f32[272,128]{1,0:T(8,128)S(1)} %get-tuple-element.148.rest_11_.yd), channel_id=1, source_target_pairs={{1,2},{2,1},{3,4},{4,3},{5,6},{6,5},{7,0},{0,7},{9,10},{10,9},{11,... | collective-permute-start | bytes 417800 | tf_op jit(solution)/shard_map/ppermute | solution.py:443
  40.9 0.4 collective-permute-start.15
  41.3 1.0 %shard_map.62.rest_8_ = f32[16,128]{1,0:T(8,128)S(1)} custom-call(f32[1024,128]{1,0:T(8,128)S(1)} %get-tuple-element.134.u0, f32[1024,128]{1,0:T(8,128)S(1)} %get-tuple-element.139.u1, f32[1024,128]{1,0:T(8,128)S(1)} %get-tuple-element.144.u2, f32[264,128]{1,0:T(8,128)S(1)} %get-tuple-element.135.ya.rest_0_, f32[256,128]{1,0:T(8,128)S(1)} %get-tuple-element.136.yb.rest_1_, ...), custom_call_target="tpu_custom_call" | custom-call | tf_op jit(solution)/shard_map/pallas_call | solution.py:526
  42.3 3.7 %collective-permute-done.15.rb = f32[256,128]{1,0:T(8,128)S(1)} collective-permute-done((f32[256,128]{1,0:T(8,128)S(1)}, f32[256,128]{1,0:T(8,128)S(1)}, u32[]{:S(2)}, u32[]{:S(2)}) %collective-permute-start.15) | collective-permute-done | bytes 131104 | tf_op jit(solution)/shard_map/ppermute | solution.py:443
  46.1 0.2 collective-permute-done.17.rd
  46.3 0.2 collective-permute-done.16.rc
  46.5 2.5 %shard_map.63 = (f32[1024,128]{1,0:T(8,128)S(1)}, f32[256,128]{1,0:T(8,128)S(1)}, f32[256,128]{1,0:T(8,128)S(1)}, f32[512,128]{1,0:T(8,128)S(1)}, f32[24,128]{1,0:T(8,128)S(1)}) custom-call(f32[8,128]{1,0:T(8,128)S(1)} %broadcast_in_dim.8.facts, f32[264,128]{1,0:T(8,128)S(1)} %get-tuple-element.145.rest_8_.ya, f32[256,128]{1,0:T(8,128)S(1)} %get-tuple-element.146.rest_9_.yb, ...), custom_call_target="tpu_custom_call" | custom-call | tf_op jit(solution)/shard_map/pallas_call | solution.py:526
  49.0 0.2 collective-permute-start.20
  49.2 1.0 %collective-permute-done.20.refs_1_ = f32[24,128]{1,0:T(8,128)S(1)} collective-permute-done((f32[24,128]{1,0:T(8,128)S(1)}, f32[24,128]{1,0:T(8,128)S(1)}, u32[]{:S(2)}, u32[]{:S(2)}) %collective-permute-start.20) | collective-permute-done | bytes 12320 | tf_op jit(solution)/shard_map/ppermute | solution.py:459
  50.3 0.6 collective-permute-start.21
  51.0 1.7 %collective-permute-start.22 = (f32[24,128]{1,0:T(8,128)S(1)}, f32[24,128]{1,0:T(8,128)S(1)}, u32[]{:S(2)}, u32[]{:S(2)}) collective-permute-start(f32[24,128]{1,0:T(8,128)S(1)} %shard_map.64.refs_0_), channel_id=1, source_target_pairs={{0,1},{1,0},{2,3},{3,2},{4,5},{5,4},{6,7},{7,6},{8,9},{9,8},{10,11... | collective-permute-start | bytes 36872 | tf_op jit(solution)/shard_map/ppermute | solution.py:459
  52.7 1.2 %collective-permute-start.23 = (f32[24,128]{1,0:T(8,128)S(1)}, f32[24,128]{1,0:T(8,128)S(1)}, u32[]{:S(2)}, u32[]{:S(2)}) collective-permute-start(f32[24,128]{1,0:T(8,128)S(1)} %shard_map.64.refs_0_), channel_id=1, source_target_pairs={{0,16},{1,17},{2,18},{3,19},{4,20},{5,21},{6,22},{7,23},{8,24},{9,... | collective-permute-start | bytes 36872 | tf_op jit(solution)/shard_map/ppermute | solution.py:459
  53.9 2.2 %collective-permute-start.19 = (f32[256,128]{1,0:T(8,128)S(1)}, f32[256,128]{1,0:T(8,128)S(1)}, u32[]{:S(2)}, u32[]{:S(2)}) collective-permute-start(f32[256,128]{1,0:T(8,128)S(1)} %get-tuple-element.153), channel_id=1, source_target_pairs={{0,7},{1,0},{2,1},{3,2},{4,3},{5,4},{6,5},{7,6},{8,15},{9,8},{10,9... | collective-permute-start | bytes 393224 | tf_op jit(solution)/shard_map/ppermute | solution.py:433
  56.1 0.3 collective-permute-done.23.refs_3_
  56.4 0.1 shard_map.65.rest_0_
  56.5 0.0 copy-start.2
  56.5 0.8 %collective-permute-start.24 = (f32[24,128]{1,0:T(8,128)S(1)}, f32[24,128]{1,0:T(8,128)S(1)}, u32[]{:S(2)}, u32[]{:S(2)}) collective-permute-start(f32[24,128]{1,0:T(8,128)S(1)} %shard_map.65.rest_0_), channel_id=1, source_target_pairs={{0,6},{1,7},{2,4},{3,5},{4,2},{5,3},{6,0},{7,1},{8,14},{9,15},{10,... | collective-permute-start | bytes 36872 | tf_op jit(solution)/shard_map/ppermute | solution.py:459
  57.3 0.5 collective-permute-start.25
  57.8 3.1 %collective-permute-start.26 = (f32[24,128]{1,0:T(8,128)S(1)}, f32[24,128]{1,0:T(8,128)S(1)}, u32[]{:S(2)}, u32[]{:S(2)}) collective-permute-start(f32[24,128]{1,0:T(8,128)S(1)} %shard_map.65.rest_0_), channel_id=1, source_target_pairs={{0,2},{1,3},{2,0},{3,1},{4,6},{5,7},{6,4},{7,5},{8,10},{9,11},{10,... | collective-permute-start | bytes 36872 | tf_op jit(solution)/shard_map/ppermute | solution.py:459
  60.9 0.8 %copy.8 = f32[512,128]{0,1:T(8,128)} copy(f32[512,128]{1,0:T(8,128)S(1)} %bitcast.51) | data formatting | bytes 524288 | tf_op jit(solution)/shard_map/while | solution.py:594
  61.8 0.3 collective-permute-done.24.rest_1_
  62.1 0.5 collective-permute-done.26.rest_3_
  62.6 1.3 %shard_map.66 = (f32[512,128]{1,0:T(8,128)}, f32[512,128]{1,0:T(8,128)}, s32[1,1]{1,0:T(1,128)}) custom-call(f32[8,128]{1,0:T(8,128)S(1)} %broadcast_in_dim.8.facts, f32[1024,128]{1,0:T(8,128)S(1)} %get-tuple-element.134.u0, f32[1024,128]{1,0:T(8,128)S(1)} %get-tuple-element.139.u1, f32[1024,128]{1,0:T(8,128)S(1)} %get-tuple-element.144.u2, ...), custom_call_target="tpu_custom_call" | custom-call | tf_op jit(solution)/shard_map/pallas_call | solution.py:539
  63.9 0.7 %while.28 = (f32[512,128]{1,0:T(8,128)}, f32[512,128]{1,0:T(8,128)}, s32[]{:T(128)}, f32[512,128]{0,1:T(8,128)}, s32[]{:T(128)}, /*index=5*/f32[1,1,1024,1024]{3...) while((f32[512,128]{1,0:T(8,128)}, f32[512,128]{1,0:T(8,128)}, s32[]{:T(128)}, ...), condition=%region_9.10_spmd, body=%region_0.9_spmd | while | flops 3762094080 | bytes 49572704 | solution.py:594
  (18 shorter events, 0.1 us)
Async XLA Ops:
  0.6 12.3 %collective-permute-start.4 = (f32[512,128]{1,0:T(8,128)}, f32[512,128]{1,0:T(8,128)S(1)}, u32[]{:S(2)}, u32[]{:S(2)}) collective-permute-start(f32[512,128]{1,0:T(8,128)} %bitcast.48), channel_id=1, source_target_pairs={{0,8},{8,16},{16,24},{24,0},{1,9},{9,17},{17,25},{25,1},{2,10},{10... | collective-permute-start | bytes 786440 | tf_op jit(solution)/shard_map/ppermute | solution.py:433
  1.1 12.1 %collective-permute-start.5 = (f32[512,128]{1,0:T(8,128)}, f32[512,128]{1,0:T(8,128)S(1)}, u32[]{:S(2)}, u32[]{:S(2)}) collective-permute-start(f32[512,128]{1,0:T(8,128)} %bitcast.49), channel_id=1, source_target_pairs={{0,1},{1,2},{2,3},{3,4},{4,5},{5,6},{6,7},{7,0},{8,9},{9,10},{10,1... | collective-permute-start | bytes 786440 | tf_op jit(solution)/shard_map/ppermute | solution.py:433
  4.5 8.9 %copy-start = (f32[1,1,2,256,128]{4,3,2,1,0:T(8,128)S(1)}, f32[1,1,2,256,128]{4,3,2,1,0:T(8,128)}, u32[]{:S(2)}) copy-start(f32[1,1,2,256,128]{4,3,2,1,0:T(8,128)} %param.8) | copy-start | bytes 786436
  14.6 11.1 %collective-permute-start.8 = (f32[280,128]{1,0:T(8,128)S(1)}, f32[280,128]{1,0:T(8,128)S(1)}, u32[]{:S(2)}, u32[]{:S(2)}) collective-permute-start(f32[280,128]{1,0:T(8,128)S(1)} %get-tuple-element.137.yc.rest_2_), channel_id=1, source_target_pairs={{0,1},{1,0},{2,3},{3,2},{4,5},{5,4},{6,7},{7,6},{8,9},{9,8},{10,11... | collective-permute-start | bytes 430088 | tf_op jit(solution)/shard_map/ppermute | solution.py:443
  15.8 9.9 %collective-permute-start.9 = (f32[272,128]{1,0:T(8,128)S(1)}, f32[272,128]{1,0:T(8,128)S(1)}, u32[]{:S(2)}, u32[]{:S(2)}) collective-permute-start(f32[272,128]{1,0:T(8,128)S(1)} %get-tuple-element.138.yd.rest_3_), channel_id=1, source_target_pairs={{1,2},{2,1},{3,4},{4,3},{5,6},{6,5},{7,0},{0,7},{9,10},{10,9},{11,... | collective-permute-start | bytes 417800 | tf_op jit(solution)/shard_map/ppermute | solution.py:443
  19.4 6.3 %collective-permute-start.6 = (f32[264,128]{1,0:T(8,128)S(1)}, f32[264,128]{1,0:T(8,128)S(1)}, u32[]{:S(2)}, u32[]{:S(2)}) collective-permute-start(f32[264,128]{1,0:T(8,128)S(1)} %get-tuple-element.135.ya.rest_0_), channel_id=1, source_target_pairs={{0,8},{8,0},{16,24},{24,16},{1,9},{9,1},{17,25},{25,17},{2,10},{10... | collective-permute-start | bytes 405512 | tf_op jit(solution)/shard_map/ppermute | solution.py:443
  20.1 5.6 %collective-permute-start.7 = (f32[256,128]{1,0:T(8,128)S(1)}, f32[256,128]{1,0:T(8,128)S(1)}, u32[]{:S(2)}, u32[]{:S(2)}) collective-permute-start(f32[256,128]{1,0:T(8,128)S(1)} %get-tuple-element.136.yb.rest_1_), channel_id=1, source_target_pairs={{8,16},{16,8},{24,0},{0,24},{9,17},{17,9},{25,1},{1,25},{10,18},{1... | collective-permute-start | bytes 393224 | tf_op jit(solution)/shard_map/ppermute | solution.py:443
  27.0 8.8 %collective-permute-start.12 = (f32[280,128]{1,0:T(8,128)S(1)}, f32[280,128]{1,0:T(8,128)S(1)}, u32[]{:S(2)}, u32[]{:S(2)}) collective-permute-start(f32[280,128]{1,0:T(8,128)S(1)} %get-tuple-element.142.yc.rest_6_), channel_id=1, source_target_pairs={{0,1},{1,0},{2,3},{3,2},{4,5},{5,4},{6,7},{7,6},{8,9},{9,8},{10,11... | collective-permute-start | bytes 430088 | tf_op jit(solution)/shard_map/ppermute | solution.py:443
  27.1 8.6 %collective-permute-start.13 = (f32[272,128]{1,0:T(8,128)S(1)}, f32[272,128]{1,0:T(8,128)S(1)}, u32[]{:S(2)}, u32[]{:S(2)}) collective-permute-start(f32[272,128]{1,0:T(8,128)S(1)} %get-tuple-element.143.yd.rest_7_), channel_id=1, source_target_pairs={{1,2},{2,1},{3,4},{4,3},{5,6},{6,5},{7,0},{0,7},{9,10},{10,9},{11,... | collective-permute-start | bytes 417800 | tf_op jit(solution)/shard_map/ppermute | solution.py:443
  30.1 5.2 %collective-permute-start.10 = (f32[264,128]{1,0:T(8,128)S(1)}, f32[264,128]{1,0:T(8,128)S(1)}, u32[]{:S(2)}, u32[]{:S(2)}) collective-permute-start(f32[264,128]{1,0:T(8,128)S(1)} %get-tuple-element.140.ya.rest_4_), channel_id=1, source_target_pairs={{0,8},{8,0},{16,24},{24,16},{1,9},{9,1},{17,25},{25,17},{2,10},{10... | collective-permute-start | bytes 405512 | tf_op jit(solution)/shard_map/ppermute | solution.py:443
  30.1 5.2 %collective-permute-start.11 = (f32[256,128]{1,0:T(8,128)S(1)}, f32[256,128]{1,0:T(8,128)S(1)}, u32[]{:S(2)}, u32[]{:S(2)}) collective-permute-start(f32[256,128]{1,0:T(8,128)S(1)} %get-tuple-element.141.yb.rest_5_), channel_id=1, source_target_pairs={{8,16},{16,8},{24,0},{0,24},{9,17},{17,9},{25,1},{1,25},{10,18},{1... | collective-permute-start | bytes 393224 | tf_op jit(solution)/shard_map/ppermute | solution.py:443
  37.7 8.8 %collective-permute-start.16 = (f32[280,128]{1,0:T(8,128)S(1)}, f32[280,128]{1,0:T(8,128)S(1)}, u32[]{:S(2)}, u32[]{:S(2)}) collective-permute-start(f32[280,128]{1,0:T(8,128)S(1)} %get-tuple-element.147.rest_10_.yc), channel_id=1, source_target_pairs={{0,1},{1,0},{2,3},{3,2},{4,5},{5,4},{6,7},{7,6},{8,9},{9,8},{10,11... | collective-permute-start | bytes 430088 | tf_op jit(solution)/shard_map/ppermute | solution.py:443
  38.0 8.3 %collective-permute-start.17 = (f32[272,128]{1,0:T(8,128)S(1)}, f32[272,128]{1,0:T(8,128)S(1)}, u32[]{:S(2)}, u32[]{:S(2)}) collective-permute-start(f32[272,128]{1,0:T(8,128)S(1)} %get-tuple-element.148.rest_11_.yd), channel_id=1, source_target_pairs={{1,2},{2,1},{3,4},{4,3},{5,6},{6,5},{7,0},{0,7},{9,10},{10,9},{11,... | collective-permute-start | bytes 417800 | tf_op jit(solution)/shard_map/ppermute | solution.py:443
  40.9 5.2 %collective-permute-start.14 = (f32[264,128]{1,0:T(8,128)S(1)}, f32[264,128]{1,0:T(8,128)S(1)}, u32[]{:S(2)}, u32[]{:S(2)}) collective-permute-start(f32[264,128]{1,0:T(8,128)S(1)} %get-tuple-element.145.rest_8_.ya), channel_id=1, source_target_pairs={{0,8},{8,0},{16,24},{24,16},{1,9},{9,1},{17,25},{25,17},{2,10},{10... | collective-permute-start | bytes 405512 | tf_op jit(solution)/shard_map/ppermute | solution.py:443
  40.9 5.2 %collective-permute-start.15 = (f32[256,128]{1,0:T(8,128)S(1)}, f32[256,128]{1,0:T(8,128)S(1)}, u32[]{:S(2)}, u32[]{:S(2)}) collective-permute-start(f32[256,128]{1,0:T(8,128)S(1)} %get-tuple-element.146.rest_9_.yb), channel_id=1, source_target_pairs={{8,16},{16,8},{24,0},{0,24},{9,17},{17,9},{25,1},{1,25},{10,18},{1... | collective-permute-start | bytes 393224 | tf_op jit(solution)/shard_map/ppermute | solution.py:443
  49.0 1.2 %collective-permute-start.20 = (f32[24,128]{1,0:T(8,128)S(1)}, f32[24,128]{1,0:T(8,128)S(1)}, u32[]{:S(2)}, u32[]{:S(2)}) collective-permute-start(f32[24,128]{1,0:T(8,128)S(1)} %get-tuple-element.154.refs_0_), channel_id=1, source_target_pairs={{0,8},{1,9},{2,10},{3,11},{4,12},{5,13},{6,14},{7,15},{8,0},{9,1},... | collective-permute-start | bytes 36872 | tf_op jit(solution)/shard_map/ppermute | solution.py:459
  50.3 5.8 %collective-permute-start.21 = (f32[24,128]{1,0:T(8,128)S(1)}, f32[24,128]{1,0:T(8,128)S(1)}, u32[]{:S(2)}, u32[]{:S(2)}) collective-permute-start(f32[24,128]{1,0:T(8,128)S(1)} %shard_map.64.refs_0_), channel_id=1, source_target_pairs={{0,17},{1,16},{2,19},{3,18},{4,21},{5,20},{6,23},{7,22},{8,25},{9,... | collective-permute-start | bytes 36872 | tf_op jit(solution)/shard_map/ppermute | solution.py:459
  51.0 5.1 %collective-permute-start.22 = (f32[24,128]{1,0:T(8,128)S(1)}, f32[24,128]{1,0:T(8,128)S(1)}, u32[]{:S(2)}, u32[]{:S(2)}) collective-permute-start(f32[24,128]{1,0:T(8,128)S(1)} %shard_map.64.refs_0_), channel_id=1, source_target_pairs={{0,1},{1,0},{2,3},{3,2},{4,5},{5,4},{6,7},{7,6},{8,9},{9,8},{10,11... | collective-permute-start | bytes 36872 | tf_op jit(solution)/shard_map/ppermute | solution.py:459
  52.7 3.7 %collective-permute-start.23 = (f32[24,128]{1,0:T(8,128)S(1)}, f32[24,128]{1,0:T(8,128)S(1)}, u32[]{:S(2)}, u32[]{:S(2)}) collective-permute-start(f32[24,128]{1,0:T(8,128)S(1)} %shard_map.64.refs_0_), channel_id=1, source_target_pairs={{0,16},{1,17},{2,18},{3,19},{4,20},{5,21},{6,22},{7,23},{8,24},{9,... | collective-permute-start | bytes 36872 | tf_op jit(solution)/shard_map/ppermute | solution.py:459
  53.9 8.8 %collective-permute-start.18 = (f32[256,128]{1,0:T(8,128)S(1)}, f32[256,128]{1,0:T(8,128)S(1)}, u32[]{:S(2)}, u32[]{:S(2)}) collective-permute-start(f32[256,128]{1,0:T(8,128)S(1)} %get-tuple-element.152), channel_id=1, source_target_pairs={{0,24},{8,0},{16,8},{24,16},{1,25},{9,1},{17,9},{25,17},{2,26},{10... | collective-permute-start | bytes 393224 | tf_op jit(solution)/shard_map/ppermute | solution.py:433
  53.9 8.8 %collective-permute-start.19 = (f32[256,128]{1,0:T(8,128)S(1)}, f32[256,128]{1,0:T(8,128)S(1)}, u32[]{:S(2)}, u32[]{:S(2)}) collective-permute-start(f32[256,128]{1,0:T(8,128)S(1)} %get-tuple-element.153), channel_id=1, source_target_pairs={{0,7},{1,0},{2,1},{3,2},{4,3},{5,4},{6,5},{7,6},{8,15},{9,8},{10,9... | collective-permute-start | bytes 393224 | tf_op jit(solution)/shard_map/ppermute | solution.py:433
  56.5 7.4 %copy-start.2 = (s32[1,1,8,8]{3,2,1,0:T(8,128)S(1)}, s32[1,1,8,8]{3,2,1,0:T(8,128)}, u32[]{:S(2)}) copy-start(s32[1,1,8,8]{3,2,1,0:T(8,128)} %param.11) | copy-start | bytes 772
  56.5 5.6 %collective-permute-start.24 = (f32[24,128]{1,0:T(8,128)S(1)}, f32[24,128]{1,0:T(8,128)S(1)}, u32[]{:S(2)}, u32[]{:S(2)}) collective-permute-start(f32[24,128]{1,0:T(8,128)S(1)} %shard_map.65.rest_0_), channel_id=1, source_target_pairs={{0,6},{1,7},{2,4},{3,5},{4,2},{5,3},{6,0},{7,1},{8,14},{9,15},{10,... | collective-permute-start | bytes 36872 | tf_op jit(solution)/shard_map/ppermute | solution.py:459
  57.3 4.8 %collective-permute-start.25 = (f32[24,128]{1,0:T(8,128)S(1)}, f32[24,128]{1,0:T(8,128)S(1)}, u32[]{:S(2)}, u32[]{:S(2)}) collective-permute-start(f32[24,128]{1,0:T(8,128)S(1)} %shard_map.65.rest_0_), channel_id=1, source_target_pairs={{0,4},{1,5},{2,6},{3,7},{4,0},{5,1},{6,2},{7,3},{8,12},{9,13},{10,... | collective-permute-start | bytes 36872 | tf_op jit(solution)/shard_map/ppermute | solution.py:459
  57.8 4.8 %collective-permute-start.26 = (f32[24,128]{1,0:T(8,128)S(1)}, f32[24,128]{1,0:T(8,128)S(1)}, u32[]{:S(2)}, u32[]{:S(2)}) collective-permute-start(f32[24,128]{1,0:T(8,128)S(1)} %shard_map.65.rest_0_), channel_id=1, source_target_pairs={{0,2},{1,3},{2,0},{3,1},{4,6},{5,7},{6,4},{7,5},{8,10},{9,11},{10,... | collective-permute-start | bytes 36872 | tf_op jit(solution)/shard_map/ppermute | solution.py:459
